TPU v7x, 256 devices: a whole 4x4x8 slice. The times are simulated.
256 devices in a mesh: tenant: 16 (over x, z_hi, core), tensor: 16 (over z_lo, y).
Axes of the slice: x: 4, y: 4, z: 8 (z_hi: 2, z_lo: 4; z = z_hi * 4 + z_lo), core: 2. Of those that a mesh axis runs over, the one named last changes fastest.
Arguments:
- projection_input: bfloat16 [8192, 8192], P('tenant', 'tensor'), may hold values from -6 to 6
- output_gradient: bfloat16 [8192, 8192], P('tenant', 'tensor'), may hold values from -6 to 6
- frozen_weight: bfloat16 [8192, 8192], P('tenant', 'tensor'), may hold values from -0.0625 to 0.0625
- down_adapters: bfloat16 [16, 64, 8192], P('tenant', None, 'tensor'), may hold values from -0.0625 to 0.0625
- up_adapters: bfloat16 [16, 64, 8192], P('tenant', None, 'tensor'), may hold values from -0.0625 to 0.0625
- lengths: int32 [16], P('tenant'), may hold values from 128 to 512, as said below
Outputs:
- grad_input: bfloat16 [8192, 8192], P('tenant', 'tensor')
- down_gradient: float32 [16, 64, 8192], P('tenant', None, 'tensor')
- up_gradient: float32 [16, 64, 8192], P('tenant', None, 'tensor')
Inputs may be any that keep to these rules, and one draw needn't show every extreme that they name: `lengths`: each entry is a multiple of 128; some tenant has exactly 512 live tokens.
All inputs are finite; a program needn't handle non-finite values.
Results may differ from a plain program's by a relative error of at most 0.001.
Values may be sent and summed in bfloat16 or wider, within the bound.
No kernel may reach another device: no remote copies, remote signals or barrier semaphores. Data moves between devices by JAX's collectives and lax.ppermute only.
A program may use at most 128 MiB of HBM per device.

v0:
```python
import jax
import jax.numpy as jnp
from jax import lax
from jax.sharding import PartitionSpec as P

adapter_scale = 2.0


def shards(projection_input, output_gradient, frozen_weight, down_adapters, up_adapters, lengths):
    tokens = output_gradient.shape[0]
    highest = lax.Precision.HIGHEST
    positions = lax.iota(jnp.int32, tokens)
    kept_rows = (positions < lengths[0]).astype(output_gradient.dtype)[:, None]
    masked_rows = output_gradient * kept_rows
    down_adapter = down_adapters[0]
    up_adapter = up_adapters[0]
    rank_width = down_adapter.shape[0]
    lowered_part = jnp.dot(projection_input, down_adapter.T, preferred_element_type=jnp.float32)
    pulled_part = jnp.dot(masked_rows, up_adapter.T, preferred_element_type=jnp.float32)
    rank_both = lax.psum(jnp.concatenate([lowered_part, pulled_part], axis=1), "tensor")
    rank_projected = rank_both[:, :rank_width]
    pulled_rows = rank_both[:, rank_width:]
    scaled_gradient = adapter_scale * pulled_rows
    partial_value = lax.dot_general(
        masked_rows,
        lax.all_gather(frozen_weight, "tenant", axis=0, tiled=True),
        (((1,), (1,)), ((), ())),
        preferred_element_type=jnp.float32,
    )
    base_part = lax.psum_scatter(partial_value, "tensor", scatter_dimension=1, tiled=True)
    adapter_part = jnp.dot(scaled_gradient, down_adapter.astype(jnp.float32), precision=highest)
    grad_input = (base_part + adapter_part).astype(jnp.bfloat16)
    inverse_order = 1.0 / lengths[0].astype(jnp.float32)
    down_gradient = (
        jnp.dot(scaled_gradient.T, projection_input.astype(jnp.float32), precision=highest)
        * inverse_order
    )[None]
    up_gradient = (
        adapter_scale
        * jnp.dot(rank_projected.T, masked_rows.astype(jnp.float32), precision=highest)
        * inverse_order
    )[None]
    return (grad_input, down_gradient, up_gradient)


def solution(mesh):
    placed = (
        P("tenant", "tensor"),
        P("tenant", "tensor"),
        P("tenant", "tensor"),
        P("tenant", None, "tensor"),
        P("tenant", None, "tensor"),
        P("tenant"),
    )
    return jax.shard_map(
        shards,
        mesh=mesh,
        in_specs=placed,
        out_specs=(P("tenant", "tensor"), P("tenant", None, "tensor"), P("tenant", None, "tensor")),
        check_vma=False,
    )
```

profile of v0, /device:TPU:1, one launch (start us, length us, event | category | flops | bytes accessed | tf_op | source)
XLA Modules:
  0.0 423.8 jit_solution(14801731016318953357)
XLA Ops:
  8.0 0.0 copy-start
  8.0 0.0 all-gather.2.cloned.1.call-start
  8.1 0.7 all-gather.2.cloned.1.call-update
  8.7 0.0 all-reduce.2.cloned.1.call-start
  9.5 0.0 copy-done
  9.5 1.1 fusion.14
  10.6 1.4 fusion.4
  12.0 0.7 pad_maximum_fusion
  12.7 0.0 all-reduce.2.cloned.1.call-update
  12.7 0.0 reduce-scatter.2.cloned.1.call-start
  12.8 109.4 %all-gather.2.cloned.1.call-done = bf16[8192,512]{1,0:T(8,128)(2,1)} async-done(((bf16[512,512]{1,0:T(8,128)(2,1)}), bf16[8192,512]{1,0:T(8,128)(2,1)}) %all-gather.2.cloned.1.call-update) | async-done | bytes 8388624 | tf_op jit(solution)/shard_map/all_gather | solution.py:26
  122.1 13.9 %fusion.6 = f32[512,8192]{1,0:T(8,128)} fusion(bf16[8192,512]{1,0:T(8,128)(2,1)} %all-gather.2.cloned.1.call-done, bf16[512,512]{1,0:T(8,128)(2,1)} %param.7, bf16[512]{0:T(512)(128)(2,1)S(1)} %fusion.18), kind=kOutput, calls=%fused_computation.9 | convolution fusion | flops 4295229440 | bytes 25691136 | tf_op jit(solution)/shard_map/dot_general | solution.py:24
  136.0 0.0 copy-start.1
  136.0 0.0 copy-start.2
  136.0 0.0 reduce-scatter.2.cloned.1.call-update
  136.1 79.6 %all-reduce.2.cloned.1.call-done = f32[512,128]{0,1:T(8,128)} async-done(((f32[512,128]{0,1:T(8,128)}), f32[512,128]{0,1:T(8,128)}) %all-reduce.2.cloned.1.call-update) | async-done | bytes 262160 | tf_op jit(solution)/shard_map/psum | solution.py:20
  215.7 1.9 fusion.2
  217.7 0.0 copy-done.1
  217.7 2.0 fusion.1
  219.7 193.9 %reduce-scatter.2.cloned.1.call-done = f32[512,512]{1,0:T(8,128)} async-done(((f32[512,8192]{1,0:T(8,128)}), f32[512,512]{1,0:T(8,128)}) %reduce-scatter.2.cloned.1.call-update) | async-done | bytes 1048592 | tf_op jit(solution)/shard_map/reduce_scatter | solution.py:30
  413.7 0.0 copy-done.2
  413.7 2.7 fusion
  (1 shorter events, 0.0 us)
Async XLA Ops:
  8.0 1.5 copy-start
  8.0 114.1 %all-gather.2.cloned.1.call-start = ((), (), s32[]{:S(2)}) async-start(), calls=%async_computation.1 | async-start | bytes 8912896 | tf_op jit(solution)/shard_map/all_gather | solution.py:26
  8.7 207.0 %all-reduce.2.cloned.1.call-start = ((), (), s32[]{:S(2)}) async-start(), calls=%async_computation.3 | async-start | bytes 524288 | tf_op jit(solution)/shard_map/psum | solution.py:20
  12.7 400.9 %reduce-scatter.2.cloned.1.call-start = ((), (), s32[]{:S(2)}) async-start(), calls=%async_computation.2 | async-start | bytes 17825792 | tf_op jit(solution)/shard_map/reduce_scatter | solution.py:30
  136.0 81.6 %copy-start.1 = (bf16[512,512]{1,0:T(8,128)(2,1)S(1)}, bf16[512,512]{1,0:T(8,128)(2,1)}, u32[]{:S(2)}) copy-start(bf16[512,512]{1,0:T(8,128)(2,1)} %param.7) | copy-start | bytes 1572868
  136.0 277.6 %copy-start.2 = (bf16[1,64,512]{2,1,0:T(8,128)(2,1)S(1)}, bf16[1,64,512]{2,1,0:T(8,128)(2,1)}, u32[]{:S(2)}) copy-start(bf16[1,64,512]{2,1,0:T(8,128)(2,1)} %param.9) | copy-start | bytes 196612
Sparse Core Ops, SparseCore 0:
  11.9 110.2 all-gather.1
Sparse Core Ops, SparseCore 1:
  12.8 202.9 all-reduce.1
  218.3 195.3 reduce-scatter.1
where the time goes:
time: 424 us
  waiting for transfers between devices  384 us (91%)
  matrix products  23.1 us (5%)
  between operations  16.2 us (4%)
    reduce_scatter x1, waiting for transfers between devices, shards(): lax.psum_scatter(partial_value, 'tensor', scatter_dimension=1, tiled=True)  194 us
    all_gather x1, waiting for transfers between devices, shards(): lax.all_gather(frozen_weight, 'tenant', axis=0, tiled=True)  109 us
    psum x1, waiting for transfers between devices, shards(): lax.psum(jnp.concatenate([lowered_part, pulled_part], axis=1), 'tensor')  79.6 us
    dot_general x1, matrix products, shards(): lax.dot_general(masked_rows, lax.all_gather(frozen_weight, 'tenant', axis...  13.9 us
  transfers between devices with their start and end apart: 3, of which 3 were waited for; matrix products, arithmetic and copies ran while one was open for 5% of the time, Pallas kernels for 0%

commit v1 on v0

v1 whole, which is shorter than its diff:
```python
import itertools

import jax
import jax.numpy as jnp
from jax import lax
from jax.experimental import pallas as pl
from jax.experimental.pallas import tpu as pltpu
from jax.sharding import Mesh, PartitionSpec as P

adapter_scale = 2.0
AXES = ("x", "zh", "c", "zl", "y")
SIZES = (4, 2, 2, 4, 4)
DIM = 512
HALF = 256


def moves(target):
    pairs = []
    for source, place in enumerate(itertools.product(*[range(n) for n in SIZES])):
        index = 0
        for n, i in zip(SIZES, target(*place)):
            index = index * n + i % n
        pairs.append((source, index))
    return pairs


def send(value, target):
    return lax.ppermute(value, AXES, moves(target))


def way(c):
    return 1 - 2 * c


def product_kernel(slot_ref, *refs):
    g_refs, w_refs = refs[:16], refs[16:32]
    add_ref, kept_ref, out_ref, gs, ws, acc, g_sems, w_sems = refs[32:]
    for i in range(16):
        pltpu.make_async_copy(g_refs[i], gs.at[i], g_sems.at[i]).start()
    for i in range(16):
        for h in range(2):
            slot = slot_ref[16 + 2 * i + h]
            rows = pl.ds(h * HALF, HALF)
            pltpu.make_async_copy(w_refs[i].at[rows], ws.at[slot, rows], w_sems.at[h, slot]).start()
    acc[...] = jnp.zeros_like(acc)

    def step(i, carry):
        slot = slot_ref[i]
        pltpu.make_async_copy(gs.at[i], gs.at[i], g_sems.at[i]).wait()
        for h in range(2):
            rows = pl.ds(h * HALF, HALF)
            pltpu.make_async_copy(ws.at[slot, rows], ws.at[slot, rows], w_sems.at[h, slot]).wait()
        acc[...] += lax.dot_general(
            gs[i], ws[slot], (((1,), (1,)), ((), ())), preferred_element_type=jnp.float32
        )
        return carry

    lax.fori_loop(0, 16, step, 0)
    out_ref[...] = (acc[...] * kept_ref[...] + add_ref[...]).astype(out_ref.dtype)


def shards(projection_input, output_gradient, frozen_weight, down_adapters, up_adapters, lengths):
    tokens = output_gradient.shape[0]
    highest = lax.Precision.HIGHEST
    x, zh, c, zl, y = (lax.axis_index(a) for a in AXES)
    turn = way(c)

    parts = {}
    for s in range(2):
        for r in (0, 2):
            h = r // 2
            parts[s, r] = send(
                frozen_weight[h * HALF : (h + 1) * HALF],
                lambda x, zh, c, zl, y: (zl + r, (y // 2) ^ s, y % 2, x, 2 * zh + c),
            )
    own = [[jnp.concatenate([parts[s, 0], parts[s, 2]], axis=0)] for s in range(2)]
    for t in range(3):
        for s in range(2):
            own[s].append(send(own[s][-1], lambda x, zh, c, zl, y: (x + way(c), zh, c, zl, y)))
    other = [[send(v, lambda x, zh, c, zl, y: (x, zh, 1 - c, zl, y)) for v in own[s]] for s in range(2)]

    blocks = []
    for j in range(4):
        here = output_gradient if j == 0 else send(
            output_gradient, lambda x, zh, c, zl, y: (x, zh, c, zl + j, y)
        )
        behind = send(here, lambda x, zh, c, zl, y: (x, zh, c, zl, y + way(c)))
        ahead = send(here, lambda x, zh, c, zl, y: (x, zh, c, zl, y - way(c)))
        across = send(behind, lambda x, zh, c, zl, y: (x, zh, c, zl, y + way(c)))
        source_zl = (zl - j) % 4
        blocks += [
            (here, source_zl, y),
            (behind, source_zl, (y - turn) % 4),
            (ahead, source_zl, (y + turn) % 4),
            (across, source_zl, (y + 2) % 4),
        ]

    slots = [4 * block_zl + block_y for _, block_zl, block_y in blocks]
    weights = []
    for held, core, direction in ((own, c, turn), (other, 1 - c, -turn)):
        for s in range(2):
            for t in range(4):
                from_x = x - t * direction
                block_y = 2 * (zh ^ s) + core
                weights.append(held[s][t])
                slots += [4 * (from_x % 4) + block_y, 4 * ((from_x - 2) % 4) + block_y]
    slots = jnp.stack([jnp.asarray(v, jnp.int32) for v in slots])

    positions = lax.iota(jnp.int32, tokens)
    kept = positions < lengths[0]
    masked_rows = output_gradient * kept.astype(output_gradient.dtype)[:, None]
    down_adapter = down_adapters[0]
    up_adapter = up_adapters[0]
    rank_width = down_adapter.shape[0]
    lowered_part = jnp.dot(projection_input, down_adapter.T, preferred_element_type=jnp.float32)
    pulled_part = jnp.dot(masked_rows, up_adapter.T, preferred_element_type=jnp.float32)
    rank_both = jnp.concatenate([lowered_part, pulled_part], axis=1)
    for target in (
        lambda x, zh, c, zl, y: (x, zh, c, zl, y ^ 1),
        lambda x, zh, c, zl, y: (x, zh, c, zl, y ^ 3),
        lambda x, zh, c, zl, y: (x, zh, c, zl ^ 1, y),
        lambda x, zh, c, zl, y: (x, zh, c, zl ^ 2, y),
    ):
        rank_both = rank_both + send(rank_both, target)
    rank_projected = rank_both[:, :rank_width]
    scaled_gradient = adapter_scale * rank_both[:, rank_width:]
    adapter_part = jnp.dot(scaled_gradient, down_adapter.astype(jnp.float32), precision=highest)
    inverse_order = 1.0 / lengths[0].astype(jnp.float32)
    down_gradient = (
        jnp.dot(scaled_gradient.T, projection_input.astype(jnp.float32), precision=highest)
        * inverse_order
    )[None]
    up_gradient = (
        adapter_scale
        * jnp.dot(rank_projected.T, masked_rows.astype(jnp.float32), precision=highest)
        * inverse_order
    )[None]

    anywhere = pl.BlockSpec(memory_space=pl.ANY)
    in_vmem = pl.BlockSpec(memory_space=pltpu.VMEM)
    grad_input = pl.pallas_call(
        product_kernel,
        out_shape=jax.ShapeDtypeStruct((tokens, DIM), jnp.bfloat16),
        in_specs=[pl.BlockSpec(memory_space=pltpu.SMEM)] + [anywhere] * 32 + [in_vmem] * 2,
        out_specs=in_vmem,
        scratch_shapes=[
            pltpu.VMEM((16, tokens, DIM), jnp.bfloat16),
            pltpu.VMEM((16, DIM, DIM), jnp.bfloat16),
            pltpu.VMEM((tokens, DIM), jnp.float32),
            pltpu.SemaphoreType.DMA((16,)),
            pltpu.SemaphoreType.DMA((2, 16)),
        ],
        compiler_params=pltpu.CompilerParams(vmem_limit_bytes=32 * 1024 * 1024),
        cost_estimate=pl.CostEstimate(
            flops=2 * tokens * DIM * DIM * 16, bytes_accessed=18 * 1024 * 1024, transcendentals=0
        ),
    )(slots, *[b[0] for b in blocks], *weights, adapter_part, kept.astype(jnp.float32)[:, None])
    return (grad_input, down_gradient, up_gradient)


def solution(mesh):
    parts = Mesh(mesh.devices.reshape(SIZES), AXES)
    tenant, tensor = ("x", "zh", "c"), ("zl", "y")
    placed = (
        P(tenant, tensor),
        P(tenant, tensor),
        P(tenant, tensor),
        P(tenant, None, tensor),
        P(tenant, None, tensor),
        P(tenant),
    )
    return jax.shard_map(
        shards,
        mesh=parts,
        in_specs=placed,
        out_specs=(P(tenant, tensor), P(tenant, None, tensor), P(tenant, None, tensor)),
        check_vma=False,
    )
```

time: 424 us -> 208 us (0.49)
  waiting for transfers between devices: 384 us -> 69.6 us
  starting transfers between devices: 0.13 us -> 104 us
  matrix products: 23.1 us -> 4.28 us
  local copies, waits for them, and re-layouts: 0.02 us -> 14.3 us
  between operations: 16.2 us -> 1.93 us
  Pallas kernels: 0 us -> 11.1 us
    reduce_scatter x1 -> x0, waiting for transfers between devices: 194 us -> none  [shards(): lax.psum_scatter(partial_value, 'tensor', scatter_dimension=1, tiled=True)]
    all_gather x1 -> x0, waiting for transfers between devices: 109 us -> none  [shards(): lax.all_gather(frozen_weight, 'tenant', axis=0, tiled=True)]
    ppermute x0 -> x37, starting transfers between devices: none -> 104 us  [send(): return lax.ppermute(value, AXES, moves(target))]
    psum x1 -> x0, waiting for transfers between devices: 79.6 us -> none  [shards(): lax.psum(jnp.concatenate([lowered_part, pulled_part], axis=1), 'tensor')]
    ppermute x0 -> x37, waiting for transfers between devices: none -> 69.6 us  [send(): return lax.ppermute(value, AXES, moves(target))]
    unnamed x6 -> x60, local copies, waits for them, and re-layouts: 0.02 us -> 14.1 us
    dot_general x1 -> x0, matrix products: 13.9 us -> none  [shards(): lax.dot_general(masked_rows, lax.all_gather(frozen_weight, 'tenant', axis...]
    pallas_call x0 -> x1, Pallas kernels: none -> 11.1 us  [shards(): pl.pallas_call(product_kernel, out_shape=jax.ShapeDtypeStruct((tokens, DI...]
  transfers between devices with their start and end apart: 3 -> 37, of which waited for: 3 -> 11; matrix products, arithmetic and copies ran while one was open for 5% -> 2% of each run, Pallas kernels for 0% -> 0%
where the time goes in v1:
time: 208 us; the launch traced here: 206 us
  starting transfers between devices  104 us (50%)
  waiting for transfers between devices  69.6 us (33%)
  local copies, waits for them, and re-layouts  14.3 us (7%)
  Pallas kernels  11.1 us (5%)
  matrix products  4.28 us (2%)
    ppermute x37, starting transfers between devices, send(): return lax.ppermute(value, AXES, moves(target))  104 us
    ppermute x37, waiting for transfers between devices, send(): return lax.ppermute(value, AXES, moves(target))  69.6 us
    unnamed x60, local copies, waits for them, and re-layouts  14.1 us
    pallas_call x1, Pallas kernels, shards(): pl.pallas_call(product_kernel, out_shape=jax.ShapeDtypeStruct((tokens, DI...  11.1 us
  transfers between devices with their start and end apart: 37, of which 11 were waited for; matrix products, arithmetic and copies ran while one was open for 2% of the time, Pallas kernels for 0%

profile of v1, /device:TPU:1, one launch (start us, length us, event | category | flops | bytes accessed | tf_op | source)
XLA Modules:
  0.0 206.4 jit_solution(12753585080969448605)
XLA Ops:
  1.4 0.3 copy-done
  1.7 1.1 fusion.12
  2.9 0.4 fusion.3
  3.3 2.2 %collective-permute-start.33 = (f32[512,128]{0,1:T(8,128)S(1)}, f32[512,128]{0,1:T(8,128)S(1)}, u32[]{:S(2)}, u32[]{:S(2)}) collective-permute-start(f32[512,128]{0,1:T(8,128)S(1)} %pad_maximum_fusion), channel_id=1, source_target_pairs={{0,1},{1,0},{2,3},{3,2},{4,5},{5,4},{6,7},{7,6},{8,9},{9,8},{10,11... | collective-permute-start | bytes 786440 | tf_op jit(solution)/shard_map/ppermute | solution.py:28
  5.5 10.3 %collective-permute-start.21 = (bf16[256,512]{1,0:T(8,128)(2,1)S(1)}, bf16[256,512]{1,0:T(8,128)(2,1)S(1)}, u32[]{:S(2)}, u32[]{:S(2)}) collective-permute-start(bf16[256,512]{1,0:T(8,128)(2,1)S(1)} %get-tuple-element.3), channel_id=1, source_target_pairs={{0,160},{1,176},{2,128},{3,144},{4,224},{5,240},{6,192},{7,208},{8... | collective-permute-start | bytes 786440 | tf_op jit(solution)/shard_map/ppermute | solution.py:28
  15.8 2.6 %collective-permute-start.11 = (bf16[512,512]{1,0:T(8,128)(2,1)S(1)}, bf16[512,512]{1,0:T(8,128)(2,1)S(1)}, u32[]{:S(2)}, u32[]{:S(2)}) collective-permute-start(bf16[512,512]{1,0:T(8,128)(2,1)S(1)} %copy-done.1), channel_id=1, source_target_pairs={{0,12},{1,13},{2,14},{3,15},{4,0},{5,1},{6,2},{7,3},{8,4},{9,5},{1... | collective-permute-start | bytes 1572872 | tf_op jit(solution)/shard_map/ppermute | solution.py:28
  18.4 0.7 collective-permute-start.20
  19.1 1.6 collective-permute-start.34
  20.7 6.8 %collective-permute-done.21 = bf16[256,512]{1,0:T(8,128)(2,1)S(1)} collective-permute-done((bf16[256,512]{1,0:T(8,128)(2,1)S(1)}, bf16[256,512]{1,0:T(8,128)(2,1)S(1)}, u32[]{:S(2)}, u32[]{:S(2)}) %collective-permute-start.21) | collective-permute-done | bytes 262176 | tf_op jit(solution)/shard_map/ppermute | solution.py:28
  27.5 1.9 collective-permute-start.15
  29.4 8.9 %collective-permute-done.16 = bf16[256,512]{1,0:T(8,128)(2,1)S(1)} collective-permute-done((bf16[256,512]{1,0:T(8,128)(2,1)S(1)}, bf16[256,512]{1,0:T(8,128)(2,1)S(1)}, u32[]{:S(2)}, u32[]{:S(2)}) %collective-permute-start.16) | collective-permute-done | bytes 262176 | tf_op jit(solution)/shard_map/ppermute | solution.py:28
  38.3 20.4 %collective-permute-start.7 = (bf16[512,512]{1,0:T(8,128)(2,1)S(1)}, bf16[512,512]{1,0:T(8,128)(2,1)S(1)}, u32[]{:S(2)}, u32[]{:S(2)}) collective-permute-start(bf16[512,512]{1,0:T(8,128)(2,1)S(1)} %copy-done.1), channel_id=1, source_target_pairs={{0,8},{1,9},{2,10},{3,11},{4,12},{5,13},{6,14},{7,15},{8,0},{9,1},... | collective-permute-start | bytes 1572872 | tf_op jit(solution)/shard_map/ppermute | solution.py:28
  58.7 5.5 %collective-permute-start.3 = (bf16[512,512]{1,0:T(8,128)(2,1)S(1)}, bf16[512,512]{1,0:T(8,128)(2,1)S(1)}, u32[]{:S(2)}, u32[]{:S(2)}) collective-permute-start(bf16[512,512]{1,0:T(8,128)(2,1)S(1)} %copy-done.1), channel_id=1, source_target_pairs={{0,4},{1,5},{2,6},{3,7},{4,8},{5,9},{6,10},{7,11},{8,12},{9,13},{1... | collective-permute-start | bytes 1572872 | tf_op jit(solution)/shard_map/ppermute | solution.py:28
  64.3 8.9 %collective-permute-start = (bf16[512,512]{1,0:T(8,128)(2,1)S(1)}, bf16[512,512]{1,0:T(8,128)(2,1)S(1)}, u32[]{:S(2)}, u32[]{:S(2)}) collective-permute-start(bf16[512,512]{1,0:T(8,128)(2,1)S(1)} %copy-done.1), channel_id=1, source_target_pairs={{0,1},{1,2},{2,3},{3,0},{4,5},{5,6},{6,7},{7,4},{8,9},{9,10},{10,1... | collective-permute-start | bytes 1572872 | tf_op jit(solution)/shard_map/ppermute | solution.py:28
  73.4 29.9 %collective-permute-done.7.refs_8_ = bf16[512,512]{1,0:T(8,128)(2,1)S(1)} collective-permute-done((bf16[512,512]{1,0:T(8,128)(2,1)S(1)}, bf16[512,512]{1,0:T(8,128)(2,1)S(1)}, u32[]{:S(2)}, u32[]{:S(2)}) %collective-permute-start.7) | collective-permute-done | bytes 524320 | tf_op jit(solution)/shard_map/ppermute | solution.py:28
  103.3 2.1 %collective-permute-start.25 = (bf16[512,512]{1,0:T(8,128)(2,1)S(1)}, bf16[512,512]{1,0:T(8,128)(2,1)S(1)}, u32[]{:S(2)}, u32[]{:S(2)}) collective-permute-start(bf16[512,512]{1,0:T(8,128)(2,1)S(1)} %constant_dynamic-update-slice_fusion.refs_16_), channel_id=1, source_target_pairs={{0,16},{1,17},{2,18},{3,19},{4,20},{5,21},{6,22},{7,23},{8,24},{9,... | collective-permute-start | bytes 1572872 | tf_op jit(solution)/shard_map/ppermute | solution.py:28
  105.3 4.5 %collective-permute-start.17 = (bf16[512,512]{1,0:T(8,128)(2,1)S(1)}, bf16[512,512]{1,0:T(8,128)(2,1)S(1)}, u32[]{:S(2)}, u32[]{:S(2)}) collective-permute-start(bf16[512,512]{1,0:T(8,128)(2,1)S(1)} %constant_dynamic-update-slice_fusion.refs_16_), channel_id=1, source_target_pairs={{0,64},{1,65},{2,66},{3,67},{4,68},{5,69},{6,70},{7,71},{8,72},{9,... | collective-permute-start | bytes 1572872 | tf_op jit(solution)/shard_map/ppermute | solution.py:28
  109.8 0.8 copy-done.4
  110.6 2.1 %collective-permute-start.29 = (bf16[512,512]{1,0:T(8,128)(2,1)S(1)}, bf16[512,512]{1,0:T(8,128)(2,1)S(1)}, u32[]{:S(2)}, u32[]{:S(2)}) collective-permute-start(bf16[512,512]{1,0:T(8,128)(2,1)S(1)} %constant_dynamic-update-slice_fusion.2.refs_20_), channel_id=1, source_target_pairs={{0,16},{1,17},{2,18},{3,19},{4,20},{5,21},{6,22},{7,23},{8,24},{9,... | collective-permute-start | bytes 1572872 | tf_op jit(solution)/shard_map/ppermute | solution.py:28
  112.7 9.1 %collective-permute-start.22 = (bf16[512,512]{1,0:T(8,128)(2,1)S(1)}, bf16[512,512]{1,0:T(8,128)(2,1)}, u32[]{:S(2)}, u32[]{:S(2)}) collective-permute-start(bf16[512,512]{1,0:T(8,128)(2,1)S(1)} %constant_dynamic-update-slice_fusion.2.refs_20_), channel_id=1, source_target_pairs={{0,64},{1,65},{2,66},{3,67},{4,68},{5,69},{6,70},{7,71},{8,72},{9,... | collective-permute-start | bytes 1572872 | tf_op jit(solution)/shard_map/ppermute | solution.py:28
  122.0 0.8 copy-done.8
  122.8 0.2 collective-permute-start.13
  123.0 2.5 %collective-permute-start.12 = (bf16[512,512]{1,0:T(8,128)(2,1)S(1)}, bf16[512,512]{1,0:T(8,128)(2,1)}, u32[]{:S(2)}, u32[]{:S(2)}) collective-permute-start(bf16[512,512]{1,0:T(8,128)(2,1)S(1)} %collective-permute-done.11.refs_12_), channel_id=1, source_target_pairs={{0,1},{1,2},{2,3},{3,0},{4,5},{5,6},{6,7},{7,4},{8,9},{9,10},{10,1... | collective-permute-start | bytes 1572872 | tf_op jit(solution)/shard_map/ppermute | solution.py:28
  125.5 0.8 copy-done.12
  126.3 3.8 %collective-permute-done.22.refs_21_ = bf16[512,512]{1,0:T(8,128)(2,1)} collective-permute-done((bf16[512,512]{1,0:T(8,128)(2,1)S(1)}, bf16[512,512]{1,0:T(8,128)(2,1)}, u32[]{:S(2)}, u32[]{:S(2)}) %collective-permute-start.22) | collective-permute-done | bytes 524320 | tf_op jit(solution)/shard_map/ppermute | solution.py:28
  130.1 3.6 %collective-permute-done.36 = f32[512,128]{0,1:T(8,128)} collective-permute-done((f32[512,128]{0,1:T(8,128)S(1)}, f32[512,128]{0,1:T(8,128)}, u32[]{:S(2)}, u32[]{:S(2)}) %collective-permute-start.36) | collective-permute-done | bytes 262176 | tf_op jit(solution)/shard_map/ppermute | solution.py:28
  133.7 0.2 collective-permute-start.5
  134.0 2.0 collective-permute-done.13.refs_14_
  135.9 0.8 copy-done.14
  136.7 0.5 collective-permute-start.4
  137.2 3.4 %collective-permute-start.2 = (bf16[512,512]{1,0:T(8,128)(2,1)S(1)}, bf16[512,512]{1,0:T(8,128)(2,1)S(1)}, u32[]{:S(2)}, u32[]{:S(2)}) collective-permute-start(bf16[512,512]{1,0:T(8,128)(2,1)S(1)} %collective-permute-done.refs_1_), channel_id=1, source_target_pairs={{0,1},{1,2},{2,3},{3,0},{4,5},{5,6},{6,7},{7,4},{8,9},{9,10},{10,1... | collective-permute-start | bytes 1572872 | tf_op jit(solution)/shard_map/ppermute | solution.py:28
  140.6 0.8 copy-done.6
  141.4 5.7 %collective-permute-done.9.refs_10_ = bf16[512,512]{1,0:T(8,128)(2,1)S(1)} collective-permute-done((bf16[512,512]{1,0:T(8,128)(2,1)S(1)}, bf16[512,512]{1,0:T(8,128)(2,1)S(1)}, u32[]{:S(2)}, u32[]{:S(2)}) %collective-permute-start.9) | collective-permute-done | bytes 524320 | tf_op jit(solution)/shard_map/ppermute | solution.py:28
  147.2 0.8 copy-done.16
  148.0 3.3 %collective-permute-start.26 = (bf16[512,512]{1,0:T(8,128)(2,1)S(1)}, bf16[512,512]{1,0:T(8,128)(2,1)S(1)}, u32[]{:S(2)}, u32[]{:S(2)}) collective-permute-start(bf16[512,512]{1,0:T(8,128)(2,1)S(1)} %collective-permute-done.17.refs_17_), channel_id=1, source_target_pairs={{0,16},{1,17},{2,18},{3,19},{4,20},{5,21},{6,22},{7,23},{8,24},{9,... | collective-permute-start | bytes 1572872 | tf_op jit(solution)/shard_map/ppermute | solution.py:28
  151.3 1.1 collective-permute-start.18
  152.5 0.8 copy-done.10
  153.3 5.0 %collective-permute-done.5.refs_6_ = bf16[512,512]{1,0:T(8,128)(2,1)S(1)} collective-permute-done((bf16[512,512]{1,0:T(8,128)(2,1)S(1)}, bf16[512,512]{1,0:T(8,128)(2,1)S(1)}, u32[]{:S(2)}, u32[]{:S(2)}) %collective-permute-start.5) | collective-permute-done | bytes 524320 | tf_op jit(solution)/shard_map/ppermute | solution.py:28
  158.3 0.8 copy-done.18
  159.1 4.4 %collective-permute-start.23 = (bf16[512,512]{1,0:T(8,128)(2,1)}, bf16[512,512]{1,0:T(8,128)(2,1)}, u32[]{:S(2)}, u32[]{:S(2)}) collective-permute-start(bf16[512,512]{1,0:T(8,128)(2,1)} %collective-permute-done.22.refs_21_), channel_id=1, source_target_pairs={{0,64},{1,65},{2,66},{3,67},{4,68},{5,69},{6,70},{7,71},{8,72},{9,... | collective-permute-start | bytes 1572872 | tf_op jit(solution)/shard_map/ppermute | solution.py:28
  163.6 3.8 %collective-permute-start.30 = (bf16[512,512]{1,0:T(8,128)(2,1)}, bf16[512,512]{1,0:T(8,128)(2,1)}, u32[]{:S(2)}, u32[]{:S(2)}) collective-permute-start(bf16[512,512]{1,0:T(8,128)(2,1)} %collective-permute-done.22.refs_21_), channel_id=1, source_target_pairs={{0,16},{1,17},{2,18},{3,19},{4,20},{5,21},{6,22},{7,23},{8,24},{9,... | collective-permute-start | bytes 1572872 | tf_op jit(solution)/shard_map/ppermute | solution.py:28
  167.3 0.8 copy-done.22
  168.1 0.9 collective-permute-start.14
  169.0 0.8 copy-done.24
  170.0 4.0 %collective-permute-start.24 = (bf16[512,512]{1,0:T(8,128)(2,1)}, bf16[512,512]{1,0:T(8,128)(2,1)}, u32[]{:S(2)}, u32[]{:S(2)}) collective-permute-start(bf16[512,512]{1,0:T(8,128)(2,1)} %collective-permute-done.23.refs_22_), channel_id=1, source_target_pairs={{0,64},{1,65},{2,66},{3,67},{4,68},{5,69},{6,70},{7,71},{8,72},{9,... | collective-permute-start | bytes 1572872 | tf_op jit(solution)/shard_map/ppermute | solution.py:28
  174.0 0.1 stack.195.slot_ref
  174.2 1.1 add.371
  175.3 1.5 collective-permute-start.6
  176.8 2.2 %collective-permute-start.27 = (bf16[512,512]{1,0:T(8,128)(2,1)}, bf16[512,512]{1,0:T(8,128)(2,1)S(1)}, u32[]{:S(2)}, u32[]{:S(2)}) collective-permute-start(bf16[512,512]{1,0:T(8,128)(2,1)} %collective-permute-done.18.refs_18_), channel_id=1, source_target_pairs={{0,16},{1,17},{2,18},{3,19},{4,20},{5,21},{6,22},{7,23},{8,24},{9,... | collective-permute-start | bytes 1572872 | tf_op jit(solution)/shard_map/ppermute | solution.py:28
  179.0 3.4 %collective-permute-done.10.refs_11_ = bf16[512,512]{1,0:T(8,128)(2,1)} collective-permute-done((bf16[512,512]{1,0:T(8,128)(2,1)}, bf16[512,512]{1,0:T(8,128)(2,1)}, u32[]{:S(2)}, u32[]{:S(2)}) %collective-permute-start.10) | collective-permute-done | bytes 524320 | tf_op jit(solution)/shard_map/ppermute | solution.py:28
  182.4 2.1 %collective-permute-start.31 = (bf16[512,512]{1,0:T(8,128)(2,1)}, bf16[512,512]{1,0:T(8,128)(2,1)S(1)}, u32[]{:S(2)}, u32[]{:S(2)}) collective-permute-start(bf16[512,512]{1,0:T(8,128)(2,1)} %collective-permute-done.23.refs_22_), channel_id=1, source_target_pairs={{0,16},{1,17},{2,18},{3,19},{4,20},{5,21},{6,22},{7,23},{8,24},{9,... | collective-permute-start | bytes 1572872 | tf_op jit(solution)/shard_map/ppermute | solution.py:28
  184.5 0.3 collective-permute-done.24.refs_23_
  184.8 1.7 collective-permute-start.32
  186.6 1.0 fusion.1
  187.6 1.1 fusion
  188.7 0.6 fusion.9.refs_32_
  189.5 0.3 copy-done.3
  189.8 0.2 copy-done.5
  189.9 1.0 copy-done.17
  191.0 1.0 copy-done.19
  192.0 1.0 copy-done.21
  193.0 1.0 copy-done.23
  194.1 1.0 copy-done.25
  195.1 11.1 %shard_map.85 = bf16[512,512]{1,0:T(8,128)(2,1)} custom-call(s32[48]{0:T(128)S(1)} %stack.195.slot_ref, bf16[512,512]{1,0:T(8,128)(2,1)S(1)} %copy-done.1, bf16[512,512]{1,0:T(8,128)(2,1)S(1)} %copy-done.7, bf16[512,512]{1,0:T(8,128)(2,1)S(1)} %copy-done.5, bf16[512,512]{1,0:T(8,128)(2,1)S(1)} %copy-done.23, bf16[512,512]{1,0:T(8,128)(2,1)S(1)} %copy-done.3, ...), custom_call_target="tpu_custom_call" | custom-call | flops 4294967296 | bytes 18874368 | tf_op jit(solution)/shard_map/pallas_call | solution.py:141
  (87 shorter events, 0.7 us)
Async XLA Ops:
  0.6 1.1 copy-start
  0.6 2.2 %copy-start.1 = (bf16[512,512]{1,0:T(8,128)(2,1)S(1)}, bf16[512,512]{1,0:T(8,128)(2,1)}, u32[]{:S(2)}) copy-start(bf16[512,512]{1,0:T(8,128)(2,1)} %refs_0_.1) | copy-start | bytes 1572868
  1.7 1.2 copy-start.28
  2.9 2.6 %copy-start.26 = (bf16[512,512]{1,0:T(8,128)(2,1)S(1)}, bf16[512,512]{1,0:T(8,128)(2,1)}, u32[]{:S(2)}) copy-start(bf16[512,512]{1,0:T(8,128)(2,1)} %param.8) | copy-start | bytes 1572868
  3.3 15.8 %collective-permute-start.33 = (f32[512,128]{0,1:T(8,128)S(1)}, f32[512,128]{0,1:T(8,128)S(1)}, u32[]{:S(2)}, u32[]{:S(2)}) collective-permute-start(f32[512,128]{0,1:T(8,128)S(1)} %pad_maximum_fusion), channel_id=1, source_target_pairs={{0,1},{1,0},{2,3},{3,2},{4,5},{5,4},{6,7},{7,6},{8,9},{9,8},{10,11... | collective-permute-start | bytes 786440 | tf_op jit(solution)/shard_map/ppermute | solution.py:28
  5.5 22.0 %collective-permute-start.21 = (bf16[256,512]{1,0:T(8,128)(2,1)S(1)}, bf16[256,512]{1,0:T(8,128)(2,1)S(1)}, u32[]{:S(2)}, u32[]{:S(2)}) collective-permute-start(bf16[256,512]{1,0:T(8,128)(2,1)S(1)} %get-tuple-element.3), channel_id=1, source_target_pairs={{0,160},{1,176},{2,128},{3,144},{4,224},{5,240},{6,192},{7,208},{8... | collective-permute-start | bytes 786440 | tf_op jit(solution)/shard_map/ppermute | solution.py:28
  15.8 22.5 %collective-permute-start.16 = (bf16[256,512]{1,0:T(8,128)(2,1)S(1)}, bf16[256,512]{1,0:T(8,128)(2,1)S(1)}, u32[]{:S(2)}, u32[]{:S(2)}) collective-permute-start(bf16[256,512]{1,0:T(8,128)(2,1)S(1)} %get-tuple-element.3), channel_id=1, source_target_pairs={{0,128},{1,144},{2,160},{3,176},{4,192},{5,208},{6,224},{7,240},{8... | collective-permute-start | bytes 786440 | tf_op jit(solution)/shard_map/ppermute | solution.py:28
  15.8 57.5 %collective-permute-start.11 = (bf16[512,512]{1,0:T(8,128)(2,1)S(1)}, bf16[512,512]{1,0:T(8,128)(2,1)S(1)}, u32[]{:S(2)}, u32[]{:S(2)}) collective-permute-start(bf16[512,512]{1,0:T(8,128)(2,1)S(1)} %copy-done.1), channel_id=1, source_target_pairs={{0,12},{1,13},{2,14},{3,15},{4,0},{5,1},{6,2},{7,3},{8,4},{9,5},{1... | collective-permute-start | bytes 1572872 | tf_op jit(solution)/shard_map/ppermute | solution.py:28
  18.4 40.4 %collective-permute-start.20 = (bf16[256,512]{1,0:T(8,128)(2,1)S(1)}, bf16[256,512]{1,0:T(8,128)(2,1)S(1)}, u32[]{:S(2)}, u32[]{:S(2)}) collective-permute-start(bf16[256,512]{1,0:T(8,128)(2,1)S(1)} %get-tuple-element.4), channel_id=1, source_target_pairs={{0,32},{1,48},{2,0},{3,16},{4,96},{5,112},{6,64},{7,80},{8,160},{9... | collective-permute-start | bytes 786440 | tf_op jit(solution)/shard_map/ppermute | solution.py:28
  19.1 45.2 %collective-permute-start.34 = (f32[512,128]{0,1:T(8,128)S(1)}, f32[512,128]{0,1:T(8,128)S(1)}, u32[]{:S(2)}, u32[]{:S(2)}) collective-permute-start(f32[512,128]{0,1:T(8,128)S(1)} %fusion.19), channel_id=1, source_target_pairs={{0,3},{1,2},{2,1},{3,0},{4,7},{5,6},{6,5},{7,4},{8,11},{9,10},{10,... | collective-permute-start | bytes 786440 | tf_op jit(solution)/shard_map/ppermute | solution.py:28
  27.5 36.9 %collective-permute-start.15 = (bf16[256,512]{1,0:T(8,128)(2,1)S(1)}, bf16[256,512]{1,0:T(8,128)(2,1)S(1)}, u32[]{:S(2)}, u32[]{:S(2)}) collective-permute-start(bf16[256,512]{1,0:T(8,128)(2,1)S(1)} %get-tuple-element.4), channel_id=1, source_target_pairs={{0,0},{1,16},{2,32},{3,48},{4,64},{5,80},{6,96},{7,112},{8,128},{9... | collective-permute-start | bytes 786440 | tf_op jit(solution)/shard_map/ppermute | solution.py:28
  38.3 65.0 %collective-permute-start.7 = (bf16[512,512]{1,0:T(8,128)(2,1)S(1)}, bf16[512,512]{1,0:T(8,128)(2,1)S(1)}, u32[]{:S(2)}, u32[]{:S(2)}) collective-permute-start(bf16[512,512]{1,0:T(8,128)(2,1)S(1)} %copy-done.1), channel_id=1, source_target_pairs={{0,8},{1,9},{2,10},{3,11},{4,12},{5,13},{6,14},{7,15},{8,0},{9,1},... | collective-permute-start | bytes 1572872 | tf_op jit(solution)/shard_map/ppermute | solution.py:28
  58.7 46.6 %collective-permute-start.3 = (bf16[512,512]{1,0:T(8,128)(2,1)S(1)}, bf16[512,512]{1,0:T(8,128)(2,1)S(1)}, u32[]{:S(2)}, u32[]{:S(2)}) collective-permute-start(bf16[512,512]{1,0:T(8,128)(2,1)S(1)} %copy-done.1), channel_id=1, source_target_pairs={{0,4},{1,5},{2,6},{3,7},{4,8},{5,9},{6,10},{7,11},{8,12},{9,13},{1... | collective-permute-start | bytes 1572872 | tf_op jit(solution)/shard_map/ppermute | solution.py:28
  64.3 45.5 %collective-permute-start.1 = (bf16[512,512]{1,0:T(8,128)(2,1)S(1)}, bf16[512,512]{1,0:T(8,128)(2,1)S(1)}, u32[]{:S(2)}, u32[]{:S(2)}) collective-permute-start(bf16[512,512]{1,0:T(8,128)(2,1)S(1)} %copy-done.1), channel_id=1, source_target_pairs={{0,3},{1,0},{2,1},{3,2},{4,7},{5,4},{6,5},{7,6},{8,11},{9,8},{10,9... | collective-permute-start | bytes 1572872 | tf_op jit(solution)/shard_map/ppermute | solution.py:28
  64.3 57.6 %collective-permute-start = (bf16[512,512]{1,0:T(8,128)(2,1)S(1)}, bf16[512,512]{1,0:T(8,128)(2,1)S(1)}, u32[]{:S(2)}, u32[]{:S(2)}) collective-permute-start(bf16[512,512]{1,0:T(8,128)(2,1)S(1)} %copy-done.1), channel_id=1, source_target_pairs={{0,1},{1,2},{2,3},{3,0},{4,5},{5,6},{6,7},{7,4},{8,9},{9,10},{10,1... | collective-permute-start | bytes 1572872 | tf_op jit(solution)/shard_map/ppermute | solution.py:28
  73.3 39.5 %collective-permute-start.35 = (f32[512,128]{0,1:T(8,128)S(1)}, f32[512,128]{0,1:T(8,128)S(1)}, u32[]{:S(2)}, u32[]{:S(2)}) collective-permute-start(f32[512,128]{0,1:T(8,128)S(1)} %add.369), channel_id=1, source_target_pairs={{0,4},{1,5},{2,6},{3,7},{4,0},{5,1},{6,2},{7,3},{8,12},{9,13},{10,... | collective-permute-start | bytes 786440 | tf_op jit(solution)/shard_map/ppermute | solution.py:28
  103.3 18.8 %collective-permute-start.25 = (bf16[512,512]{1,0:T(8,128)(2,1)S(1)}, bf16[512,512]{1,0:T(8,128)(2,1)S(1)}, u32[]{:S(2)}, u32[]{:S(2)}) collective-permute-start(bf16[512,512]{1,0:T(8,128)(2,1)S(1)} %constant_dynamic-update-slice_fusion.refs_16_), channel_id=1, source_target_pairs={{0,16},{1,17},{2,18},{3,19},{4,20},{5,21},{6,22},{7,23},{8,24},{9,... | collective-permute-start | bytes 1572872 | tf_op jit(solution)/shard_map/ppermute | solution.py:28
  105.3 46.0 %copy-start.2 = (bf16[512,512]{1,0:T(8,128)(2,1)}, bf16[512,512]{1,0:T(8,128)(2,1)S(1)}, u32[]{:S(2)}) copy-start(bf16[512,512]{1,0:T(8,128)(2,1)S(1)} %collective-permute-done.3.refs_4_) | copy-start | bytes 1572868
  105.3 17.7 %collective-permute-start.17 = (bf16[512,512]{1,0:T(8,128)(2,1)S(1)}, bf16[512,512]{1,0:T(8,128)(2,1)S(1)}, u32[]{:S(2)}, u32[]{:S(2)}) collective-permute-start(bf16[512,512]{1,0:T(8,128)(2,1)S(1)} %constant_dynamic-update-slice_fusion.refs_16_), channel_id=1, source_target_pairs={{0,64},{1,65},{2,66},{3,67},{4,68},{5,69},{6,70},{7,71},{8,72},{9,... | collective-permute-start | bytes 1572872 | tf_op jit(solution)/shard_map/ppermute | solution.py:28
  109.8 0.8 copy-start.4
  110.6 14.9 %collective-permute-start.29 = (bf16[512,512]{1,0:T(8,128)(2,1)S(1)}, bf16[512,512]{1,0:T(8,128)(2,1)S(1)}, u32[]{:S(2)}, u32[]{:S(2)}) collective-permute-start(bf16[512,512]{1,0:T(8,128)(2,1)S(1)} %constant_dynamic-update-slice_fusion.2.refs_20_), channel_id=1, source_target_pairs={{0,16},{1,17},{2,18},{3,19},{4,20},{5,21},{6,22},{7,23},{8,24},{9,... | collective-permute-start | bytes 1572872 | tf_op jit(solution)/shard_map/ppermute | solution.py:28
  112.7 17.4 %collective-permute-start.22 = (bf16[512,512]{1,0:T(8,128)(2,1)S(1)}, bf16[512,512]{1,0:T(8,128)(2,1)}, u32[]{:S(2)}, u32[]{:S(2)}) collective-permute-start(bf16[512,512]{1,0:T(8,128)(2,1)S(1)} %constant_dynamic-update-slice_fusion.2.refs_20_), channel_id=1, source_target_pairs={{0,64},{1,65},{2,66},{3,67},{4,68},{5,69},{6,70},{7,71},{8,72},{9,... | collective-permute-start | bytes 1572872 | tf_op jit(solution)/shard_map/ppermute | solution.py:28
  121.9 11.8 %collective-permute-start.36 = (f32[512,128]{0,1:T(8,128)S(1)}, f32[512,128]{0,1:T(8,128)}, u32[]{:S(2)}, u32[]{:S(2)}) collective-permute-start(f32[512,128]{0,1:T(8,128)S(1)} %add.370), channel_id=1, source_target_pairs={{0,8},{1,9},{2,10},{3,11},{4,12},{5,13},{6,14},{7,15},{8,0},{9,1},... | collective-permute-start | bytes 786440 | tf_op jit(solution)/shard_map/ppermute | solution.py:28
  122.8 13.1 %collective-permute-start.13 = (bf16[512,512]{1,0:T(8,128)(2,1)S(1)}, bf16[512,512]{1,0:T(8,128)(2,1)S(1)}, u32[]{:S(2)}, u32[]{:S(2)}) collective-permute-start(bf16[512,512]{1,0:T(8,128)(2,1)S(1)} %collective-permute-done.11.refs_12_), channel_id=1, source_target_pairs={{0,3},{1,0},{2,1},{3,2},{4,7},{5,4},{6,5},{7,6},{8,11},{9,8},{10,9... | collective-permute-start | bytes 1572872 | tf_op jit(solution)/shard_map/ppermute | solution.py:28
  123.0 14.2 %collective-permute-start.12 = (bf16[512,512]{1,0:T(8,128)(2,1)S(1)}, bf16[512,512]{1,0:T(8,128)(2,1)}, u32[]{:S(2)}, u32[]{:S(2)}) collective-permute-start(bf16[512,512]{1,0:T(8,128)(2,1)S(1)} %collective-permute-done.11.refs_12_), channel_id=1, source_target_pairs={{0,1},{1,2},{2,3},{3,0},{4,5},{5,6},{6,7},{7,4},{8,9},{9,10},{10,1... | collective-permute-start | bytes 1572872 | tf_op jit(solution)/shard_map/ppermute | solution.py:28
  125.5 0.8 copy-start.12
  126.3 20.8 %collective-permute-start.9 = (bf16[512,512]{1,0:T(8,128)(2,1)S(1)}, bf16[512,512]{1,0:T(8,128)(2,1)S(1)}, u32[]{:S(2)}, u32[]{:S(2)}) collective-permute-start(bf16[512,512]{1,0:T(8,128)(2,1)S(1)} %collective-permute-done.7.refs_8_), channel_id=1, source_target_pairs={{0,3},{1,0},{2,1},{3,2},{4,7},{5,4},{6,5},{7,6},{8,11},{9,8},{10,9... | collective-permute-start | bytes 1572872 | tf_op jit(solution)/shard_map/ppermute | solution.py:28
  130.1 21.2 %collective-permute-start.8 = (bf16[512,512]{1,0:T(8,128)(2,1)S(1)}, bf16[512,512]{1,0:T(8,128)(2,1)}, u32[]{:S(2)}, u32[]{:S(2)}) collective-permute-start(bf16[512,512]{1,0:T(8,128)(2,1)S(1)} %collective-permute-done.7.refs_8_), channel_id=1, source_target_pairs={{0,1},{1,2},{2,3},{3,0},{4,5},{5,6},{6,7},{7,4},{8,9},{9,10},{10,1... | collective-permute-start | bytes 1572872 | tf_op jit(solution)/shard_map/ppermute | solution.py:28
  133.7 24.5 %collective-permute-start.5 = (bf16[512,512]{1,0:T(8,128)(2,1)S(1)}, bf16[512,512]{1,0:T(8,128)(2,1)S(1)}, u32[]{:S(2)}, u32[]{:S(2)}) collective-permute-start(bf16[512,512]{1,0:T(8,128)(2,1)S(1)} %collective-permute-done.3.refs_4_), channel_id=1, source_target_pairs={{0,3},{1,0},{2,1},{3,2},{4,7},{5,4},{6,5},{7,6},{8,11},{9,8},{10,9... | collective-permute-start | bytes 1572872 | tf_op jit(solution)/shard_map/ppermute | solution.py:28
  135.9 0.8 copy-start.14
  136.7 26.8 %collective-permute-start.4 = (bf16[512,512]{1,0:T(8,128)(2,1)S(1)}, bf16[512,512]{1,0:T(8,128)(2,1)S(1)}, u32[]{:S(2)}, u32[]{:S(2)}) collective-permute-start(bf16[512,512]{1,0:T(8,128)(2,1)S(1)} %collective-permute-done.3.refs_4_), channel_id=1, source_target_pairs={{0,1},{1,2},{2,3},{3,0},{4,5},{5,6},{6,7},{7,4},{8,9},{9,10},{10,1... | collective-permute-start | bytes 1572872 | tf_op jit(solution)/shard_map/ppermute | solution.py:28
  137.2 30.1 %collective-permute-start.2 = (bf16[512,512]{1,0:T(8,128)(2,1)S(1)}, bf16[512,512]{1,0:T(8,128)(2,1)S(1)}, u32[]{:S(2)}, u32[]{:S(2)}) collective-permute-start(bf16[512,512]{1,0:T(8,128)(2,1)S(1)} %collective-permute-done.refs_1_), channel_id=1, source_target_pairs={{0,1},{1,2},{2,3},{3,0},{4,5},{5,6},{6,7},{7,4},{8,9},{9,10},{10,1... | collective-permute-start | bytes 1572872 | tf_op jit(solution)/shard_map/ppermute | solution.py:28
  140.6 0.8 copy-start.6
  147.2 0.8 copy-start.16
  148.0 21.0 %collective-permute-start.26 = (bf16[512,512]{1,0:T(8,128)(2,1)S(1)}, bf16[512,512]{1,0:T(8,128)(2,1)S(1)}, u32[]{:S(2)}, u32[]{:S(2)}) collective-permute-start(bf16[512,512]{1,0:T(8,128)(2,1)S(1)} %collective-permute-done.17.refs_17_), channel_id=1, source_target_pairs={{0,16},{1,17},{2,18},{3,19},{4,20},{5,21},{6,22},{7,23},{8,24},{9,... | collective-permute-start | bytes 1572872 | tf_op jit(solution)/shard_map/ppermute | solution.py:28
  151.3 18.5 %collective-permute-start.18 = (bf16[512,512]{1,0:T(8,128)(2,1)S(1)}, bf16[512,512]{1,0:T(8,128)(2,1)}, u32[]{:S(2)}, u32[]{:S(2)}) collective-permute-start(bf16[512,512]{1,0:T(8,128)(2,1)S(1)} %collective-permute-done.17.refs_17_), channel_id=1, source_target_pairs={{0,64},{1,65},{2,66},{3,67},{4,68},{5,69},{6,70},{7,71},{8,72},{9,... | collective-permute-start | bytes 1572872 | tf_op jit(solution)/shard_map/ppermute | solution.py:28
  152.5 0.8 copy-start.10
  158.3 0.8 copy-start.18
  159.1 10.9 %collective-permute-start.23 = (bf16[512,512]{1,0:T(8,128)(2,1)}, bf16[512,512]{1,0:T(8,128)(2,1)}, u32[]{:S(2)}, u32[]{:S(2)}) collective-permute-start(bf16[512,512]{1,0:T(8,128)(2,1)} %collective-permute-done.22.refs_21_), channel_id=1, source_target_pairs={{0,64},{1,65},{2,66},{3,67},{4,68},{5,69},{6,70},{7,71},{8,72},{9,... | collective-permute-start | bytes 1572872 | tf_op jit(solution)/shard_map/ppermute | solution.py:28
  163.6 6.3 %copy-start.20 = (bf16[512,512]{1,0:T(8,128)(2,1)}, bf16[512,512]{1,0:T(8,128)(2,1)S(1)}, u32[]{:S(2)}) copy-start(bf16[512,512]{1,0:T(8,128)(2,1)S(1)} %collective-permute-done.4.refs_5_) | copy-start | bytes 1572868
  163.6 11.7 %collective-permute-start.30 = (bf16[512,512]{1,0:T(8,128)(2,1)}, bf16[512,512]{1,0:T(8,128)(2,1)}, u32[]{:S(2)}, u32[]{:S(2)}) collective-permute-start(bf16[512,512]{1,0:T(8,128)(2,1)} %collective-permute-done.22.refs_21_), channel_id=1, source_target_pairs={{0,16},{1,17},{2,18},{3,19},{4,20},{5,21},{6,22},{7,23},{8,24},{9,... | collective-permute-start | bytes 1572872 | tf_op jit(solution)/shard_map/ppermute | solution.py:28
  168.1 8.7 %collective-permute-start.14 = (bf16[512,512]{1,0:T(8,128)(2,1)}, bf16[512,512]{1,0:T(8,128)(2,1)}, u32[]{:S(2)}, u32[]{:S(2)}) collective-permute-start(bf16[512,512]{1,0:T(8,128)(2,1)} %collective-permute-done.12.refs_13_), channel_id=1, source_target_pairs={{0,1},{1,2},{2,3},{3,0},{4,5},{5,6},{6,7},{7,4},{8,9},{9,10},{10,1... | collective-permute-start | bytes 1572872 | tf_op jit(solution)/shard_map/ppermute | solution.py:28
  169.0 0.8 copy-start.24
  169.8 12.5 %collective-permute-start.10 = (bf16[512,512]{1,0:T(8,128)(2,1)}, bf16[512,512]{1,0:T(8,128)(2,1)}, u32[]{:S(2)}, u32[]{:S(2)}) collective-permute-start(bf16[512,512]{1,0:T(8,128)(2,1)} %collective-permute-done.8.refs_9_), channel_id=1, source_target_pairs={{0,1},{1,2},{2,3},{3,0},{4,5},{5,6},{6,7},{7,4},{8,9},{9,10},{10,1... | collective-permute-start | bytes 1572872 | tf_op jit(solution)/shard_map/ppermute | solution.py:28
  169.8 14.6 %collective-permute-start.19 = (bf16[512,512]{1,0:T(8,128)(2,1)}, bf16[512,512]{1,0:T(8,128)(2,1)}, u32[]{:S(2)}, u32[]{:S(2)}) collective-permute-start(bf16[512,512]{1,0:T(8,128)(2,1)} %collective-permute-done.18.refs_18_), channel_id=1, source_target_pairs={{0,64},{1,65},{2,66},{3,67},{4,68},{5,69},{6,70},{7,71},{8,72},{9,... | collective-permute-start | bytes 1572872 | tf_op jit(solution)/shard_map/ppermute | solution.py:28
  170.0 14.8 %collective-permute-start.24 = (bf16[512,512]{1,0:T(8,128)(2,1)}, bf16[512,512]{1,0:T(8,128)(2,1)}, u32[]{:S(2)}, u32[]{:S(2)}) collective-permute-start(bf16[512,512]{1,0:T(8,128)(2,1)} %collective-permute-done.23.refs_22_), channel_id=1, source_target_pairs={{0,64},{1,65},{2,66},{3,67},{4,68},{5,69},{6,70},{7,71},{8,72},{9,... | collective-permute-start | bytes 1572872 | tf_op jit(solution)/shard_map/ppermute | solution.py:28
  174.2 15.3 %copy-start.15 = (bf16[512,512]{1,0:T(8,128)(2,1)S(1)}, bf16[512,512]{1,0:T(8,128)(2,1)}, u32[]{:S(2)}) copy-start(bf16[512,512]{1,0:T(8,128)(2,1)} %copy-done.14) | copy-start | bytes 1572868
  174.2 15.2 %copy-start.13 = (bf16[512,512]{1,0:T(8,128)(2,1)S(1)}, bf16[512,512]{1,0:T(8,128)(2,1)}, u32[]{:S(2)}) copy-start(bf16[512,512]{1,0:T(8,128)(2,1)} %copy-done.12) | copy-start | bytes 1572868
  175.3 14.1 %collective-permute-start.6 = (bf16[512,512]{1,0:T(8,128)(2,1)}, bf16[512,512]{1,0:T(8,128)(2,1)S(1)}, u32[]{:S(2)}, u32[]{:S(2)}) collective-permute-start(bf16[512,512]{1,0:T(8,128)(2,1)} %copy-done.20), channel_id=1, source_target_pairs={{0,1},{1,2},{2,3},{3,0},{4,5},{5,6},{6,7},{7,4},{8,9},{9,10},{10,1... | collective-permute-start | bytes 1572872 | tf_op jit(solution)/shard_map/ppermute | solution.py:28
  176.8 12.6 %collective-permute-start.27 = (bf16[512,512]{1,0:T(8,128)(2,1)}, bf16[512,512]{1,0:T(8,128)(2,1)S(1)}, u32[]{:S(2)}, u32[]{:S(2)}) collective-permute-start(bf16[512,512]{1,0:T(8,128)(2,1)} %collective-permute-done.18.refs_18_), channel_id=1, source_target_pairs={{0,16},{1,17},{2,18},{3,19},{4,20},{5,21},{6,22},{7,23},{8,24},{9,... | collective-permute-start | bytes 1572872 | tf_op jit(solution)/shard_map/ppermute | solution.py:28
  182.4 7.0 %collective-permute-start.31 = (bf16[512,512]{1,0:T(8,128)(2,1)}, bf16[512,512]{1,0:T(8,128)(2,1)S(1)}, u32[]{:S(2)}, u32[]{:S(2)}) collective-permute-start(bf16[512,512]{1,0:T(8,128)(2,1)} %collective-permute-done.23.refs_22_), channel_id=1, source_target_pairs={{0,16},{1,17},{2,18},{3,19},{4,20},{5,21},{6,22},{7,23},{8,24},{9,... | collective-permute-start | bytes 1572872 | tf_op jit(solution)/shard_map/ppermute | solution.py:28
  184.5 4.9 %collective-permute-start.28 = (bf16[512,512]{1,0:T(8,128)(2,1)}, bf16[512,512]{1,0:T(8,128)(2,1)S(1)}, u32[]{:S(2)}, u32[]{:S(2)}) collective-permute-start(bf16[512,512]{1,0:T(8,128)(2,1)} %collective-permute-done.19.refs_19_), channel_id=1, source_target_pairs={{0,16},{1,17},{2,18},{3,19},{4,20},{5,21},{6,22},{7,23},{8,24},{9,... | collective-permute-start | bytes 1572872 | tf_op jit(solution)/shard_map/ppermute | solution.py:28
  184.8 4.6 %collective-permute-start.32 = (bf16[512,512]{1,0:T(8,128)(2,1)}, bf16[512,512]{1,0:T(8,128)(2,1)S(1)}, u32[]{:S(2)}, u32[]{:S(2)}) collective-permute-start(bf16[512,512]{1,0:T(8,128)(2,1)} %collective-permute-done.24.refs_23_), channel_id=1, source_target_pairs={{0,16},{1,17},{2,18},{3,19},{4,20},{5,21},{6,22},{7,23},{8,24},{9,... | collective-permute-start | bytes 1572872 | tf_op jit(solution)/shard_map/ppermute | solution.py:28
  186.5 2.2 %copy-start.27 = (bf16[1,64,512]{2,1,0:T(8,128)(2,1)S(1)}, bf16[1,64,512]{2,1,0:T(8,128)(2,1)}, u32[]{:S(2)}) copy-start(bf16[1,64,512]{2,1,0:T(8,128)(2,1)} %param.9) | copy-start | bytes 196612
  186.5 2.9 %copy-start.9 = (bf16[512,512]{1,0:T(8,128)(2,1)S(1)}, bf16[512,512]{1,0:T(8,128)(2,1)}, u32[]{:S(2)}) copy-start(bf16[512,512]{1,0:T(8,128)(2,1)} %copy-done.8) | copy-start | bytes 1572868
  186.6 2.9 %copy-start.11 = (bf16[512,512]{1,0:T(8,128)(2,1)S(1)}, bf16[512,512]{1,0:T(8,128)(2,1)}, u32[]{:S(2)}) copy-start(bf16[512,512]{1,0:T(8,128)(2,1)} %copy-done.10) | copy-start | bytes 1572868
  187.6 1.9 copy-start.7
  188.7 1.0 copy-start.3
  188.7 1.2 copy-start.5
  189.9 1.0 copy-start.17
  191.0 1.0 copy-start.19
  192.0 1.0 copy-start.21
  193.0 1.0 copy-start.23
  194.1 1.0 copy-start.25
  (2 other events, 1.6 us)

commit v2 on v0

v2 whole, which is shorter than its diff:
```python
import itertools

import jax
import jax.numpy as jnp
from jax import lax
from jax.experimental import pallas as pl
from jax.experimental.pallas import tpu as pltpu
from jax.sharding import Mesh, PartitionSpec as P

adapter_scale = 2.0
AXES = ("x", "zh", "c", "zl", "y")
SIZES = (4, 2, 2, 4, 4)
DIM = 512


def moves(target):
    pairs = []
    for source, place in enumerate(itertools.product(*[range(n) for n in SIZES])):
        index = 0
        for n, i in zip(SIZES, target(*place)):
            index = index * n + i % n
        pairs.append((source, index))
    return pairs


def send(value, target):
    return lax.ppermute(value, AXES, moves(target))


def after(value, *others):
    return lax.optimization_barrier((value, *others))[0]


def way(c):
    return 1 - 2 * c


def halved(value, bit, swap):
    rows = value.shape[0] // 2
    kept = lax.dynamic_slice_in_dim(value, bit * rows, rows)
    return kept + swap(lax.dynamic_slice_in_dim(value, (1 - bit) * rows, rows))


def doubled(value, bit, swap):
    there = swap(value)
    return jnp.where(
        bit == 0,
        jnp.concatenate([value, there], axis=0),
        jnp.concatenate([there, value], axis=0),
    )


def early_kernel(slot_ref, *refs):
    g_refs, w_refs = refs[:12], refs[12:20]
    w_out, acc_ref, gs, ws, g_sems, w_sems, out_sems = refs[20:]
    g_copies = [pltpu.make_async_copy(ref, gs.at[i], g_sems.at[i]) for i, ref in enumerate(g_refs)]
    for copy in g_copies:
        copy.start()
    for i in range(8):
        for s in range(2):
            slot = slot_ref[16 + 2 * i + s]
            pltpu.make_async_copy(
                w_refs[i].at[pl.ds(s * DIM, DIM)], ws.at[slot], w_sems.at[slot]
            ).start()
    acc_ref[...] = jnp.zeros_like(acc_ref)
    for copy in g_copies:
        copy.wait()

    def arrive(slot, carry):
        pltpu.make_async_copy(ws.at[slot], ws.at[slot], w_sems.at[slot]).wait()
        pltpu.make_async_copy(ws.at[slot], w_out.at[slot], out_sems.at[slot]).start()
        return carry

    lax.fori_loop(0, 16, arrive, 0)

    def step(i, carry):
        acc_ref[...] += lax.dot_general(
            gs[i],
            ws[slot_ref[i]],
            (((1,), (1,)), ((), ())),
            preferred_element_type=jnp.float32,
        )
        return carry

    lax.fori_loop(0, 12, step, 0)

    def leave(slot, carry):
        pltpu.make_async_copy(ws.at[slot], w_out.at[slot], out_sems.at[slot]).wait()
        return carry

    lax.fori_loop(0, 16, leave, 0)


def late_kernel(slot_ref, g0, g1, g2, g3, w_ref, acc_ref, add_ref, kept_ref, out_ref, gs, ws, g_sems, w_sems):
    copies = []
    for i, ref in enumerate((g0, g1, g2, g3)):
        g_copy = pltpu.make_async_copy(ref, gs.at[i], g_sems.at[i])
        w_copy = pltpu.make_async_copy(w_ref.at[slot_ref[12 + i]], ws.at[i], w_sems.at[i])
        g_copy.start()
        w_copy.start()
        copies += [g_copy, w_copy]
    for copy in copies:
        copy.wait()
    total = acc_ref[...]
    for i in range(4):
        total += lax.dot_general(gs[i], ws[i], (((1,), (1,)), ((), ())), preferred_element_type=jnp.float32)
    out_ref[...] = (total * kept_ref[...] + add_ref[...]).astype(out_ref.dtype)


def shards(projection_input, output_gradient, frozen_weight, down_adapters, up_adapters, lengths):
    tokens = output_gradient.shape[0]
    highest = lax.Precision.HIGHEST
    x, zh, c, zl, y = (lax.axis_index(a) for a in AXES)
    turn = way(c)

    positions = lax.iota(jnp.int32, tokens)
    kept = positions < lengths[0]
    masked_rows = output_gradient * kept.astype(output_gradient.dtype)[:, None]
    down_adapter = down_adapters[0]
    up_adapter = up_adapters[0]
    rank_width = down_adapter.shape[0]
    lowered_part = jnp.dot(projection_input, down_adapter.T, preferred_element_type=jnp.float32)
    pulled_part = jnp.dot(masked_rows, up_adapter.T, preferred_element_type=jnp.float32)
    rank_both = jnp.concatenate([lowered_part, pulled_part], axis=1)

    def place(s):
        return send(
            frozen_weight,
            lambda x, zh, c, zl, y: (zl + 2 * (y % 2), (y // 2) ^ s, y % 2, x, 2 * zh + c),
        )

    def along_x(held):
        return send(held, lambda x, zh, c, zl, y: (x + way(c), zh, c, zl, y))

    def to_sibling(held):
        return send(held, lambda x, zh, c, zl, y: (x, zh, 1 - c, zl, y))

    def along_z(here, j):
        return send(here, lambda x, zh, c, zl, y: (x, zh, c, zl + j, y))

    def onward(here):
        return send(here, lambda x, zh, c, zl, y: (x, zh, c, zl, y + way(c)))

    def backward(here):
        return send(here, lambda x, zh, c, zl, y: (x, zh, c, zl, y - way(c)))

    def in_rank(piece, dz, dy):
        return send(piece, lambda x, zh, c, zl, y: (x, zh, c, zl ^ dz, y ^ dy))

    placed = [place(0), place(1)]
    z1 = along_z(output_gradient, 1)
    behind_0, ahead_0 = onward(output_gradient), backward(output_gradient)
    across_0 = onward(behind_0)
    rank = halved(rank_both, (y & 1) ^ (y >> 1), lambda v: in_rank(v, 0, 1))
    own = [after(jnp.concatenate(placed, axis=0), ahead_0, across_0, z1, rank)]
    own.append(along_x(own[0]))
    z3 = along_z(after(output_gradient, z1, *placed), 3)
    behind_1, ahead_1 = onward(z1), backward(z1)
    rank = halved(rank, y >> 1, lambda v: in_rank(v, 0, 3))
    other = [to_sibling(own[0])]
    own.append(along_x(after(own[1], behind_1, ahead_1, z3, rank, other[0])))
    z2 = along_z(after(output_gradient, z3, own[1]), 2)
    across_1 = onward(behind_1)
    behind_3, ahead_3 = onward(z3), backward(z3)
    rank = rank + in_rank(rank, 1, 0)
    rank = rank + in_rank(rank, 2, 0)
    other.append(to_sibling(own[1]))
    own.append(along_x(after(own[2], behind_3, ahead_3, across_1, z2, rank, other[1])))
    behind_2, ahead_2 = onward(z2), backward(z2)
    across_3 = onward(behind_3)
    rank = doubled(rank, y >> 1, lambda v: in_rank(v, 0, 3))
    other.append(to_sibling(after(own[2], behind_2, ahead_2, across_3, rank)))
    other.append(to_sibling(own[3]))
    across_2 = onward(behind_2)
    rank_both = doubled(rank, (y & 1) ^ (y >> 1), lambda v: in_rank(v, 0, 1))
    first = [output_gradient, behind_0, ahead_0, across_0]
    second = [z1, behind_1, ahead_1, across_1, z3, behind_3, ahead_3, across_3]
    third = [z2, behind_2, ahead_2, across_2]

    places = [y, (y - turn) % 4, (y + turn) % 4, (y + 2) % 4]
    slots = [4 * ((zl - j) % 4) + place for j in (0, 1, 3, 2) for place in places]
    for core, direction in ((c, turn), (1 - c, -turn)):
        for t in range(4):
            for s in range(2):
                slots.append(4 * ((x - t * direction - 2 * core) % 4) + 2 * (zh ^ s) + core)
    slots = jnp.stack([jnp.asarray(v, jnp.int32) for v in slots])

    rank_projected = rank_both[:, :rank_width]
    scaled_gradient = adapter_scale * rank_both[:, rank_width:]
    adapter_part = jnp.dot(scaled_gradient, down_adapter.astype(jnp.float32), precision=highest)
    inverse_order = 1.0 / lengths[0].astype(jnp.float32)
    down_gradient = (
        jnp.dot(scaled_gradient.T, projection_input.astype(jnp.float32), precision=highest)
        * inverse_order
    )[None]
    up_gradient = (
        adapter_scale
        * jnp.dot(rank_projected.T, masked_rows.astype(jnp.float32), precision=highest)
        * inverse_order
    )[None]

    anywhere = pl.BlockSpec(memory_space=pl.ANY)
    in_vmem = pl.BlockSpec(memory_space=pltpu.VMEM)
    in_smem = pl.BlockSpec(memory_space=pltpu.SMEM)
    w_blocks, early = pl.pallas_call(
        early_kernel,
        out_shape=(
            jax.ShapeDtypeStruct((16, DIM, DIM), jnp.bfloat16),
            jax.ShapeDtypeStruct((tokens, DIM), jnp.float32),
        ),
        in_specs=[in_smem] + [anywhere] * 20,
        out_specs=(anywhere, in_vmem),
        scratch_shapes=[
            pltpu.VMEM((12, tokens, DIM), jnp.bfloat16),
            pltpu.VMEM((16, DIM, DIM), jnp.bfloat16),
            pltpu.SemaphoreType.DMA((12,)),
            pltpu.SemaphoreType.DMA((16,)),
            pltpu.SemaphoreType.DMA((16,)),
        ],
        compiler_params=pltpu.CompilerParams(vmem_limit_bytes=24 * 1024 * 1024),
        cost_estimate=pl.CostEstimate(
            flops=2 * tokens * DIM * DIM * 12, bytes_accessed=24 * 1024 * 1024, transcendentals=0
        ),
    )(slots, *first, *second, *own, *other)
    grad_input = pl.pallas_call(
        late_kernel,
        out_shape=jax.ShapeDtypeStruct((tokens, DIM), jnp.bfloat16),
        in_specs=[in_smem] + [anywhere] * 5 + [in_vmem] * 3,
        out_specs=in_vmem,
        scratch_shapes=[
            pltpu.VMEM((4, tokens, DIM), jnp.bfloat16),
            pltpu.VMEM((4, DIM, DIM), jnp.bfloat16),
            pltpu.SemaphoreType.DMA((4,)),
            pltpu.SemaphoreType.DMA((4,)),
        ],
        compiler_params=pltpu.CompilerParams(vmem_limit_bytes=24 * 1024 * 1024),
        cost_estimate=pl.CostEstimate(
            flops=2 * tokens * DIM * DIM * 4, bytes_accessed=6 * 1024 * 1024, transcendentals=0
        ),
    )(slots, *third, w_blocks, early, adapter_part, kept.astype(jnp.float32)[:, None])
    return (grad_input, down_gradient, up_gradient)


def solution(mesh):
    parts = Mesh(mesh.devices.reshape(SIZES), AXES)
    tenant, tensor = ("x", "zh", "c"), ("zl", "y")
    placed = (
        P(tenant, tensor),
        P(tenant, tensor),
        P(tenant, tensor),
        P(tenant, None, tensor),
        P(tenant, None, tensor),
        P(tenant),
    )
    return jax.shard_map(
        shards,
        mesh=parts,
        in_specs=placed,
        out_specs=(P(tenant, tensor), P(tenant, None, tensor), P(tenant, None, tensor)),
        check_vma=False,
    )
```

time: 424 us -> 186 us (0.44)
  waiting for transfers between devices: 384 us -> 85 us
  starting transfers between devices: 0.13 us -> 72.3 us
  matrix products: 23.1 us -> 5.34 us
  Pallas kernels: 0 us -> 14.9 us
  between operations: 16.2 us -> 1.94 us
    reduce_scatter x1 -> x0, waiting for transfers between devices: 194 us -> none  [shards(): lax.psum_scatter(partial_value, 'tensor', scatter_dimension=1, tiled=True)]
    all_gather x1 -> x0, waiting for transfers between devices: 109 us -> none  [shards(): lax.all_gather(frozen_weight, 'tenant', axis=0, tiled=True)]
    ppermute x0 -> x30, waiting for transfers between devices: none -> 85 us  [send(): return lax.ppermute(value, AXES, moves(target))]
    psum x1 -> x0, waiting for transfers between devices: 79.6 us -> none  [shards(): lax.psum(jnp.concatenate([lowered_part, pulled_part], axis=1), 'tensor')]
    ppermute x0 -> x30, starting transfers between devices: none -> 72.3 us  [send(): return lax.ppermute(value, AXES, moves(target))]
    pallas_call x0 -> x2, Pallas kernels: none -> 14.9 us  [the longest x1 10.8 us: shards(): pl.pallas_call(early_kernel, out_shape=(jax.ShapeDtypeStruct((16, DIM, DI...]
    dot_general x1 -> x0, matrix products: 13.9 us -> none  [shards(): lax.dot_general(masked_rows, lax.all_gather(frozen_weight, 'tenant', axis...]
  transfers between devices with their start and end apart: 3 -> 30, of which waited for: 3 -> 13; matrix products, arithmetic and copies ran while one was open for 5% -> 4% of each run, Pallas kernels for 0% -> 6%
where the time goes in v2:
time: 186 us; the launch traced here: 185 us
  waiting for transfers between devices  85 us (46%)
  starting transfers between devices  72.3 us (39%)
  Pallas kernels  14.9 us (8%)
  matrix products  5.34 us (3%)
  local copies, waits for them, and re-layouts  3.56 us (2%)
  between operations  1.94 us (1%)
    ppermute x30, waiting for transfers between devices, send(): return lax.ppermute(value, AXES, moves(target))  85 us
    ppermute x30, starting transfers between devices, send(): return lax.ppermute(value, AXES, moves(target))  72.3 us
    pallas_call x1, Pallas kernels, shards(): pl.pallas_call(early_kernel, out_shape=(jax.ShapeDtypeStruct((16, DIM, DI...  10.8 us
    pallas_call x1, Pallas kernels, shards(): pl.pallas_call(late_kernel, out_shape=jax.ShapeDtypeStruct((tokens, DIM),...  4.07 us
  transfers between devices with their start and end apart: 30, of which 13 were waited for; matrix products, arithmetic and copies ran while one was open for 4% of the time, Pallas kernels for 6%

profile of v2, /device:TPU:1, one launch (start us, length us, event | category | flops | bytes accessed | tf_op | source)
XLA Modules:
  0.0 184.5 jit_solution(828327386159332908)
XLA Ops:
  0.6 0.0 copy-start
  0.6 4.7 %collective-permute-start.1 = (bf16[512,512]{1,0:T(8,128)(2,1)}, bf16[512,512]{1,0:T(8,128)(2,1)}, u32[]{:S(2)}, u32[]{:S(2)}) collective-permute-start(bf16[512,512]{1,0:T(8,128)(2,1)} %param.8), channel_id=1, source_target_pairs={{0,0},{1,144},{2,32},{3,176},{4,64},{5,208},{6,96},{7,240},{8,128}... | collective-permute-start | bytes 1572872 | tf_op jit(solution)/shard_map/ppermute | solution.py:27
  5.4 8.4 %collective-permute-start.2 = (bf16[512,512]{1,0:T(8,128)(2,1)}, bf16[512,512]{1,0:T(8,128)(2,1)}, u32[]{:S(2)}, u32[]{:S(2)}) collective-permute-start(bf16[512,512]{1,0:T(8,128)(2,1)} %param.8), channel_id=1, source_target_pairs={{0,32},{1,176},{2,0},{3,144},{4,96},{5,240},{6,64},{7,208},{8,160}... | collective-permute-start | bytes 1572872 | tf_op jit(solution)/shard_map/ppermute | solution.py:27
  13.7 2.7 %collective-permute-start.5 = (bf16[512,512]{1,0:T(8,128)(2,1)}, bf16[512,512]{1,0:T(8,128)(2,1)S(1)}, u32[]{:S(2)}, u32[]{:S(2)}) collective-permute-start(bf16[512,512]{1,0:T(8,128)(2,1)} %refs_0_.1), channel_id=1, source_target_pairs={{0,1},{1,2},{2,3},{3,0},{4,5},{5,6},{6,7},{7,4},{8,9},{9,10},{10,1... | collective-permute-start | bytes 1572872 | tf_op jit(solution)/shard_map/ppermute | solution.py:27
  17.1 1.1 fusion.15
  18.2 0.0 copy-start.1
  18.3 1.4 fusion.3
  19.8 0.1 collective-permute-start.7
  19.9 0.1 collective-permute-start
  20.0 5.4 %collective-permute-done.7 = f32[256,128]{0,1:T(8,128)S(1)} collective-permute-done((f32[256,128]{0,1:T(8,128)S(1)}, f32[256,128]{0,1:T(8,128)S(1)}, u32[]{:S(2)}, u32[]{:S(2)}) %collective-permute-start.7) | collective-permute-done | bytes 131104 | tf_op jit(solution)/shard_map/ppermute | solution.py:27
  25.3 2.2 %collective-permute-start.4 = (bf16[512,512]{1,0:T(8,128)(2,1)}, bf16[512,512]{1,0:T(8,128)(2,1)}, u32[]{:S(2)}, u32[]{:S(2)}) collective-permute-start(bf16[512,512]{1,0:T(8,128)(2,1)} %refs_0_.1), channel_id=1, source_target_pairs={{0,3},{1,0},{2,1},{3,2},{4,7},{5,4},{6,5},{7,6},{8,11},{9,8},{10,9... | collective-permute-start | bytes 1572872 | tf_op jit(solution)/shard_map/ppermute | solution.py:27
  27.5 1.8 collective-permute-start.6
  29.3 21.2 %collective-permute-done.1 = bf16[512,512]{1,0:T(8,128)(2,1)} collective-permute-done((bf16[512,512]{1,0:T(8,128)(2,1)}, bf16[512,512]{1,0:T(8,128)(2,1)}, u32[]{:S(2)}, u32[]{:S(2)}) %collective-permute-start.1) | collective-permute-done | bytes 524320 | tf_op jit(solution)/shard_map/ppermute | solution.py:27
  50.6 3.8 %collective-permute-done.2 = bf16[512,512]{1,0:T(8,128)(2,1)} collective-permute-done((bf16[512,512]{1,0:T(8,128)(2,1)}, bf16[512,512]{1,0:T(8,128)(2,1)}, u32[]{:S(2)}, u32[]{:S(2)}) %collective-permute-start.2) | collective-permute-done | bytes 524320 | tf_op jit(solution)/shard_map/ppermute | solution.py:27
  54.4 1.3 pad_maximum_fusion.refs_12_
  55.6 0.0 copy-start.12
  55.7 0.8 copy-done.6
  56.5 0.0 collective-permute-done.6.refs_3_
  56.5 7.7 %collective-permute-start.8 = (bf16[1024,512]{1,0:T(8,128)(2,1)S(1)}, bf16[1024,512]{1,0:T(8,128)(2,1)S(1)}, u32[]{:S(2)}, u32[]{:S(2)}) collective-permute-start(bf16[1024,512]{1,0:T(8,128)(2,1)S(1)} %pad_maximum_fusion.refs_12_), channel_id=1, source_target_pairs={{0,64},{1,65},{2,66},{3,67},{4,68},{5,69},{6,70},{7,71},{8,72},{9,... | collective-permute-start | bytes 3145736 | tf_op jit(solution)/shard_map/ppermute | solution.py:27
  64.1 13.4 %collective-permute-start.20 = (bf16[1024,512]{1,0:T(8,128)(2,1)S(1)}, bf16[1024,512]{1,0:T(8,128)(2,1)}, u32[]{:S(2)}, u32[]{:S(2)}) collective-permute-start(bf16[1024,512]{1,0:T(8,128)(2,1)S(1)} %pad_maximum_fusion.refs_12_), channel_id=1, source_target_pairs={{0,16},{1,17},{2,18},{3,19},{4,20},{5,21},{6,22},{7,23},{8,24},{9,... | collective-permute-start | bytes 3145736 | tf_op jit(solution)/shard_map/ppermute | solution.py:27
  77.6 0.0 collective-permute-start.19
  77.6 2.7 %collective-permute-start.13 = (bf16[512,512]{1,0:T(8,128)(2,1)}, bf16[512,512]{1,0:T(8,128)(2,1)}, u32[]{:S(2)}, u32[]{:S(2)}) collective-permute-start(bf16[512,512]{1,0:T(8,128)(2,1)} %copy-done.6), channel_id=1, source_target_pairs={{0,1},{1,2},{2,3},{3,0},{4,5},{5,6},{6,7},{7,4},{8,9},{9,10},{10,1... | collective-permute-start | bytes 1572872 | tf_op jit(solution)/shard_map/ppermute | solution.py:27
  80.3 2.2 %collective-permute-done.19 = f32[128,128]{0,1:T(8,128)S(1)} collective-permute-done((f32[128,128]{0,1:T(8,128)S(1)}, f32[128,128]{0,1:T(8,128)S(1)}, u32[]{:S(2)}, u32[]{:S(2)}) %collective-permute-start.19) | collective-permute-done | bytes 65568 | tf_op jit(solution)/shard_map/ppermute | solution.py:27
  82.5 0.1 collective-permute-start.14
  82.5 6.3 %collective-permute-done.13.refs_5_ = bf16[512,512]{1,0:T(8,128)(2,1)} collective-permute-done((bf16[512,512]{1,0:T(8,128)(2,1)}, bf16[512,512]{1,0:T(8,128)(2,1)}, u32[]{:S(2)}, u32[]{:S(2)}) %collective-permute-start.13) | collective-permute-done | bytes 524320 | tf_op jit(solution)/shard_map/ppermute | solution.py:27
  88.8 3.4 %collective-permute-start.15 = (bf16[512,512]{1,0:T(8,128)(2,1)}, bf16[512,512]{1,0:T(8,128)(2,1)S(1)}, u32[]{:S(2)}, u32[]{:S(2)}) collective-permute-start(bf16[512,512]{1,0:T(8,128)(2,1)} %collective-permute-done.13.refs_5_), channel_id=1, source_target_pairs={{0,1},{1,2},{2,3},{3,0},{4,5},{5,6},{6,7},{7,4},{8,9},{9,10},{10,1... | collective-permute-start | bytes 1572872 | tf_op jit(solution)/shard_map/ppermute | solution.py:27
  92.2 0.8 collective-permute-done.3.refs_8_
  93.0 1.0 collective-permute-done.14.refs_6_
  94.0 0.0 collective-permute-done.20.refs_16_
  94.0 3.0 %collective-permute-start.21 = (bf16[1024,512]{1,0:T(8,128)(2,1)S(1)}, bf16[1024,512]{1,0:T(8,128)(2,1)}, u32[]{:S(2)}, u32[]{:S(2)}) collective-permute-start(bf16[1024,512]{1,0:T(8,128)(2,1)S(1)} %collective-permute-done.8.refs_13_), channel_id=1, source_target_pairs={{0,64},{1,65},{2,66},{3,67},{4,68},{5,69},{6,70},{7,71},{8,72},{9,... | collective-permute-start | bytes 3145736 | tf_op jit(solution)/shard_map/ppermute | solution.py:27
  97.0 1.7 collective-permute-start.24
  98.7 1.9 %collective-permute-start.22 = (f32[128,128]{0,1:T(8,128)S(1)}, f32[128,128]{0,1:T(8,128)S(1)}, u32[]{:S(2)}, u32[]{:S(2)}) collective-permute-start(f32[128,128]{0,1:T(8,128)S(1)} %dynamic-slice_add_fusion), channel_id=1, source_target_pairs={{0,4},{1,5},{2,6},{3,7},{4,0},{5,1},{6,2},{7,3},{8,12},{9,13},{10,... | collective-permute-start | bytes 196616 | tf_op jit(solution)/shard_map/ppermute | solution.py:27
  100.6 2.1 %collective-permute-done.22 = f32[128,128]{0,1:T(8,128)S(1)} collective-permute-done((f32[128,128]{0,1:T(8,128)S(1)}, f32[128,128]{0,1:T(8,128)S(1)}, u32[]{:S(2)}, u32[]{:S(2)}) %collective-permute-start.22) | collective-permute-done | bytes 65568 | tf_op jit(solution)/shard_map/ppermute | solution.py:27
  102.7 3.4 %collective-permute-start.23 = (f32[128,128]{0,1:T(8,128)S(1)}, f32[128,128]{0,1:T(8,128)S(1)}, u32[]{:S(2)}, u32[]{:S(2)}) collective-permute-start(f32[128,128]{0,1:T(8,128)S(1)} %add.314), channel_id=1, source_target_pairs={{0,8},{1,9},{2,10},{3,11},{4,12},{5,13},{6,14},{7,15},{8,0},{9,1},... | collective-permute-start | bytes 196616 | tf_op jit(solution)/shard_map/ppermute | solution.py:27
  106.1 3.9 %collective-permute-start.16 = (bf16[512,512]{1,0:T(8,128)(2,1)}, bf16[512,512]{1,0:T(8,128)(2,1)}, u32[]{:S(2)}, u32[]{:S(2)}) collective-permute-start(bf16[512,512]{1,0:T(8,128)(2,1)} %collective-permute-done.3.refs_8_), channel_id=1, source_target_pairs={{0,1},{1,2},{2,3},{3,0},{4,5},{5,6},{6,7},{7,4},{8,9},{9,10},{10,1... | collective-permute-start | bytes 1572872 | tf_op jit(solution)/shard_map/ppermute | solution.py:27
  110.0 0.0 collective-permute-done.23
  110.0 0.0 collective-permute-start.17
  110.0 0.0 collective-permute-done.15.refs_7_
  110.0 0.8 copy-done.8
  110.8 0.5 collective-permute-start.9
  111.3 5.7 %collective-permute-done.16.refs_9_ = bf16[512,512]{1,0:T(8,128)(2,1)} collective-permute-done((bf16[512,512]{1,0:T(8,128)(2,1)}, bf16[512,512]{1,0:T(8,128)(2,1)}, u32[]{:S(2)}, u32[]{:S(2)}) %collective-permute-start.16) | collective-permute-done | bytes 524320 | tf_op jit(solution)/shard_map/ppermute | solution.py:27
  117.0 6.3 %collective-permute-done.17.refs_10_ = bf16[512,512]{1,0:T(8,128)(2,1)S(1)} collective-permute-done((bf16[512,512]{1,0:T(8,128)(2,1)}, bf16[512,512]{1,0:T(8,128)(2,1)S(1)}, u32[]{:S(2)}, u32[]{:S(2)}) %collective-permute-start.17) | collective-permute-done | bytes 524320 | tf_op jit(solution)/shard_map/ppermute | solution.py:27
  123.3 0.8 copy-done.10
  124.1 11.7 %collective-permute-done.9.g0 = bf16[512,512]{1,0:T(8,128)(2,1)} collective-permute-done((bf16[512,512]{1,0:T(8,128)(2,1)S(1)}, bf16[512,512]{1,0:T(8,128)(2,1)}, u32[]{:S(2)}, u32[]{:S(2)}) %collective-permute-start.9) | collective-permute-done | bytes 524320 | tf_op jit(solution)/shard_map/ppermute | solution.py:27
  135.8 0.0 collective-permute-done.24.refs_17_
  135.8 1.0 copy-done.2
  136.8 0.0 collective-permute-start.25
  136.9 1.7 collective-permute-start.18
  138.6 2.4 %collective-permute-start.10 = (bf16[512,512]{1,0:T(8,128)(2,1)}, bf16[512,512]{1,0:T(8,128)(2,1)}, u32[]{:S(2)}, u32[]{:S(2)}) collective-permute-start(bf16[512,512]{1,0:T(8,128)(2,1)} %collective-permute-done.9.g0), channel_id=1, source_target_pairs={{0,1},{1,2},{2,3},{3,0},{4,5},{5,6},{6,7},{7,4},{8,9},{9,10},{10,1... | collective-permute-start | bytes 1572872 | tf_op jit(solution)/shard_map/ppermute | solution.py:27
  141.0 2.7 %collective-permute-start.26 = (f32[128,128]{0,1:T(8,128)S(1)}, f32[128,128]{0,1:T(8,128)S(1)}, u32[]{:S(2)}, u32[]{:S(2)}) collective-permute-start(f32[128,128]{0,1:T(8,128)S(1)} %add.315), channel_id=1, source_target_pairs={{0,3},{1,2},{2,1},{3,0},{4,7},{5,6},{6,5},{7,4},{8,11},{9,10},{10,... | collective-permute-start | bytes 196616 | tf_op jit(solution)/shard_map/ppermute | solution.py:27
  143.7 14.3 %collective-permute-done.26 = f32[128,128]{0,1:T(8,128)S(1)} collective-permute-done((f32[128,128]{0,1:T(8,128)S(1)}, f32[128,128]{0,1:T(8,128)S(1)}, u32[]{:S(2)}, u32[]{:S(2)}) %collective-permute-start.26) | collective-permute-done | bytes 65568 | tf_op jit(solution)/shard_map/ppermute | solution.py:27
  158.0 0.0 collective-permute-done.10.g1
  158.0 3.8 %collective-permute-start.27 = (bf16[1024,512]{1,0:T(8,128)(2,1)}, bf16[1024,512]{1,0:T(8,128)(2,1)}, u32[]{:S(2)}, u32[]{:S(2)}) collective-permute-start(bf16[1024,512]{1,0:T(8,128)(2,1)} %collective-permute-done.21.refs_14_), channel_id=1, source_target_pairs={{0,16},{1,17},{2,18},{3,19},{4,20},{5,21},{6,22},{7,23},{8,24},{9,... | collective-permute-start | bytes 3145736 | tf_op jit(solution)/shard_map/ppermute | solution.py:27
  161.8 0.0 collective-permute-done.25.refs_15_
  161.8 0.1 collective-permute-start.28
  161.9 0.0 collective-permute-start.29
  162.0 0.1 stack.131.slot_ref
  162.2 0.0 copy-start.5
  162.2 4.3 %collective-permute-done.29 = f32[256,128]{0,1:T(8,128)S(1)} collective-permute-done((f32[256,128]{0,1:T(8,128)S(1)}, f32[256,128]{0,1:T(8,128)S(1)}, u32[]{:S(2)}, u32[]{:S(2)}) %collective-permute-start.29) | collective-permute-done | bytes 131104 | tf_op jit(solution)/shard_map/ppermute | solution.py:27
  166.6 1.0 fusion.1
  167.6 1.1 fusion
  168.7 0.6 fusion.12.add_ref
  169.4 10.8 %shard_map.85 = (bf16[16,512,512]{2,1,0:T(8,128)(2,1)S(1)}, f32[512,512]{1,0:T(8,128)S(1)}) custom-call(s32[32]{0:T(128)S(1)} %stack.131.slot_ref, bf16[512,512]{1,0:T(8,128)(2,1)S(1)} %copy-done.1, bf16[512,512]{1,0:T(8,128)(2,1)S(1)} %copy-done.5, bf16[512,512]{1,0:T(8,128)(2,1)} %collective-permute-done.4.refs_2_, ...), custom_call_target="tpu_custom_call" | custom-call | flops 3221225472 | bytes 25165824 | tf_op jit(solution)/shard_map/pallas_call | solution.py:205
  180.3 4.1 %shard_map.86 = bf16[512,512]{1,0:T(8,128)(2,1)} custom-call(s32[32]{0:T(128)S(1)} %stack.131.slot_ref, bf16[512,512]{1,0:T(8,128)(2,1)} %collective-permute-done.9.g0, bf16[512,512]{1,0:T(8,128)(2,1)} %collective-permute-done.10.g1, bf16[512,512]{1,0:T(8,128)(2,1)} %collective-permute-done.11.g2, bf16[512,512]{1,0:T(8,128)(2,1)S(1)} %collective-permute-done.12.g3, ...), custom_call_target="tpu_custom_call" | custom-call | flops 1073741824 | bytes 6291456 | tf_op jit(solution)/shard_map/pallas_call | solution.py:225
  (41 shorter events, 0.2 us)
Async XLA Ops:
  0.6 16.5 %copy-start = (bf16[512,512]{1,0:T(8,128)(2,1)S(1)}, bf16[512,512]{1,0:T(8,128)(2,1)}, u32[]{:S(2)}) copy-start(bf16[512,512]{1,0:T(8,128)(2,1)} %param.6) | copy-start | bytes 1572868
  0.6 49.9 %collective-permute-start.1 = (bf16[512,512]{1,0:T(8,128)(2,1)}, bf16[512,512]{1,0:T(8,128)(2,1)}, u32[]{:S(2)}, u32[]{:S(2)}) collective-permute-start(bf16[512,512]{1,0:T(8,128)(2,1)} %param.8), channel_id=1, source_target_pairs={{0,0},{1,144},{2,32},{3,176},{4,64},{5,208},{6,96},{7,240},{8,128}... | collective-permute-start | bytes 1572872 | tf_op jit(solution)/shard_map/ppermute | solution.py:27
  5.4 49.0 %collective-permute-start.2 = (bf16[512,512]{1,0:T(8,128)(2,1)}, bf16[512,512]{1,0:T(8,128)(2,1)}, u32[]{:S(2)}, u32[]{:S(2)}) collective-permute-start(bf16[512,512]{1,0:T(8,128)(2,1)} %param.8), channel_id=1, source_target_pairs={{0,32},{1,176},{2,0},{3,144},{4,96},{5,240},{6,64},{7,208},{8,160}... | collective-permute-start | bytes 1572872 | tf_op jit(solution)/shard_map/ppermute | solution.py:27
  13.7 13.8 %collective-permute-start.5 = (bf16[512,512]{1,0:T(8,128)(2,1)}, bf16[512,512]{1,0:T(8,128)(2,1)S(1)}, u32[]{:S(2)}, u32[]{:S(2)}) collective-permute-start(bf16[512,512]{1,0:T(8,128)(2,1)} %refs_0_.1), channel_id=1, source_target_pairs={{0,1},{1,2},{2,3},{3,0},{4,5},{5,6},{6,7},{7,4},{8,9},{9,10},{10,1... | collective-permute-start | bytes 1572872 | tf_op jit(solution)/shard_map/ppermute | solution.py:27
  18.2 62.0 %copy-start.1 = (bf16[512,512]{1,0:T(8,128)(2,1)S(1)}, bf16[512,512]{1,0:T(8,128)(2,1)}, u32[]{:S(2)}) copy-start(bf16[512,512]{1,0:T(8,128)(2,1)} %refs_0_.1) | copy-start | bytes 1572868
  19.8 5.6 %collective-permute-start.7 = (f32[256,128]{0,1:T(8,128)S(1)}, f32[256,128]{0,1:T(8,128)S(1)}, u32[]{:S(2)}, u32[]{:S(2)}) collective-permute-start(f32[256,128]{0,1:T(8,128)S(1)} %fusion.8), channel_id=1, source_target_pairs={{0,1},{1,0},{2,3},{3,2},{4,5},{5,4},{6,7},{7,6},{8,9},{9,8},{10,11... | collective-permute-start | bytes 393224 | tf_op jit(solution)/shard_map/ppermute | solution.py:27
  19.9 35.8 %collective-permute-start = (bf16[512,512]{1,0:T(8,128)(2,1)}, bf16[512,512]{1,0:T(8,128)(2,1)S(1)}, u32[]{:S(2)}, u32[]{:S(2)}) collective-permute-start(bf16[512,512]{1,0:T(8,128)(2,1)} %refs_0_.1), channel_id=1, source_target_pairs={{0,4},{1,5},{2,6},{3,7},{4,8},{5,9},{6,10},{7,11},{8,12},{9,13},{1... | collective-permute-start | bytes 1572872 | tf_op jit(solution)/shard_map/ppermute | solution.py:27
  25.3 30.3 %collective-permute-start.4 = (bf16[512,512]{1,0:T(8,128)(2,1)}, bf16[512,512]{1,0:T(8,128)(2,1)}, u32[]{:S(2)}, u32[]{:S(2)}) collective-permute-start(bf16[512,512]{1,0:T(8,128)(2,1)} %refs_0_.1), channel_id=1, source_target_pairs={{0,3},{1,0},{2,1},{3,2},{4,7},{5,4},{6,5},{7,6},{8,11},{9,8},{10,9... | collective-permute-start | bytes 1572872 | tf_op jit(solution)/shard_map/ppermute | solution.py:27
  27.5 28.1 %copy-start.4 = (bf16[512,512]{1,0:T(8,128)(2,1)}, bf16[512,512]{1,0:T(8,128)(2,1)S(1)}, u32[]{:S(2)}) copy-start(bf16[512,512]{1,0:T(8,128)(2,1)S(1)} %collective-permute-done.5.refs_1_) | copy-start | bytes 1572868
  27.5 28.9 %collective-permute-start.6 = (bf16[512,512]{1,0:T(8,128)(2,1)S(1)}, bf16[512,512]{1,0:T(8,128)(2,1)}, u32[]{:S(2)}, u32[]{:S(2)}) collective-permute-start(bf16[512,512]{1,0:T(8,128)(2,1)S(1)} %collective-permute-done.5.refs_1_), channel_id=1, source_target_pairs={{0,1},{1,2},{2,3},{3,0},{4,5},{5,6},{6,7},{7,4},{8,9},{9,10},{10,1... | collective-permute-start | bytes 1572872 | tf_op jit(solution)/shard_map/ppermute | solution.py:27
  55.6 113.1 %copy-start.12 = (bf16[1,64,512]{2,1,0:T(8,128)(2,1)S(1)}, bf16[1,64,512]{2,1,0:T(8,128)(2,1)}, u32[]{:S(2)}) copy-start(bf16[1,64,512]{2,1,0:T(8,128)(2,1)} %param.9) | copy-start | bytes 196612
  55.7 0.8 copy-start.6
  56.5 37.5 %collective-permute-start.8 = (bf16[1024,512]{1,0:T(8,128)(2,1)S(1)}, bf16[1024,512]{1,0:T(8,128)(2,1)S(1)}, u32[]{:S(2)}, u32[]{:S(2)}) collective-permute-start(bf16[1024,512]{1,0:T(8,128)(2,1)S(1)} %pad_maximum_fusion.refs_12_), channel_id=1, source_target_pairs={{0,64},{1,65},{2,66},{3,67},{4,68},{5,69},{6,70},{7,71},{8,72},{9,... | collective-permute-start | bytes 3145736 | tf_op jit(solution)/shard_map/ppermute | solution.py:27
  64.1 29.8 %collective-permute-start.20 = (bf16[1024,512]{1,0:T(8,128)(2,1)S(1)}, bf16[1024,512]{1,0:T(8,128)(2,1)}, u32[]{:S(2)}, u32[]{:S(2)}) collective-permute-start(bf16[1024,512]{1,0:T(8,128)(2,1)S(1)} %pad_maximum_fusion.refs_12_), channel_id=1, source_target_pairs={{0,16},{1,17},{2,18},{3,19},{4,20},{5,21},{6,22},{7,23},{8,24},{9,... | collective-permute-start | bytes 3145736 | tf_op jit(solution)/shard_map/ppermute | solution.py:27
  77.6 4.9 %collective-permute-start.19 = (f32[128,128]{0,1:T(8,128)S(1)}, f32[128,128]{0,1:T(8,128)S(1)}, u32[]{:S(2)}, u32[]{:S(2)}) collective-permute-start(f32[128,128]{0,1:T(8,128)S(1)} %constant_dynamic-slice_fusion), channel_id=1, source_target_pairs={{0,3},{1,2},{2,1},{3,0},{4,7},{5,6},{6,5},{7,4},{8,11},{9,10},{10,... | collective-permute-start | bytes 196616 | tf_op jit(solution)/shard_map/ppermute | solution.py:27
  77.6 11.2 %collective-permute-start.13 = (bf16[512,512]{1,0:T(8,128)(2,1)}, bf16[512,512]{1,0:T(8,128)(2,1)}, u32[]{:S(2)}, u32[]{:S(2)}) collective-permute-start(bf16[512,512]{1,0:T(8,128)(2,1)} %copy-done.6), channel_id=1, source_target_pairs={{0,1},{1,2},{2,3},{3,0},{4,5},{5,6},{6,7},{7,4},{8,9},{9,10},{10,1... | collective-permute-start | bytes 1572872 | tf_op jit(solution)/shard_map/ppermute | solution.py:27
  80.3 12.7 %collective-permute-start.3 = (bf16[512,512]{1,0:T(8,128)(2,1)S(1)}, bf16[512,512]{1,0:T(8,128)(2,1)}, u32[]{:S(2)}, u32[]{:S(2)}) collective-permute-start(bf16[512,512]{1,0:T(8,128)(2,1)S(1)} %copy-done.1), channel_id=1, source_target_pairs={{0,12},{1,13},{2,14},{3,15},{4,0},{5,1},{6,2},{7,3},{8,4},{9,5},{1... | collective-permute-start | bytes 1572872 | tf_op jit(solution)/shard_map/ppermute | solution.py:27
  82.5 11.5 %collective-permute-start.14 = (bf16[512,512]{1,0:T(8,128)(2,1)}, bf16[512,512]{1,0:T(8,128)(2,1)}, u32[]{:S(2)}, u32[]{:S(2)}) collective-permute-start(bf16[512,512]{1,0:T(8,128)(2,1)} %copy-done.6), channel_id=1, source_target_pairs={{0,3},{1,0},{2,1},{3,2},{4,7},{5,4},{6,5},{7,6},{8,11},{9,8},{10,9... | collective-permute-start | bytes 1572872 | tf_op jit(solution)/shard_map/ppermute | solution.py:27
  88.8 21.2 %collective-permute-start.15 = (bf16[512,512]{1,0:T(8,128)(2,1)}, bf16[512,512]{1,0:T(8,128)(2,1)S(1)}, u32[]{:S(2)}, u32[]{:S(2)}) collective-permute-start(bf16[512,512]{1,0:T(8,128)(2,1)} %collective-permute-done.13.refs_5_), channel_id=1, source_target_pairs={{0,1},{1,2},{2,3},{3,0},{4,5},{5,6},{6,7},{7,4},{8,9},{9,10},{10,1... | collective-permute-start | bytes 1572872 | tf_op jit(solution)/shard_map/ppermute | solution.py:27
  94.0 41.8 %collective-permute-start.21 = (bf16[1024,512]{1,0:T(8,128)(2,1)S(1)}, bf16[1024,512]{1,0:T(8,128)(2,1)}, u32[]{:S(2)}, u32[]{:S(2)}) collective-permute-start(bf16[1024,512]{1,0:T(8,128)(2,1)S(1)} %collective-permute-done.8.refs_13_), channel_id=1, source_target_pairs={{0,64},{1,65},{2,66},{3,67},{4,68},{5,69},{6,70},{7,71},{8,72},{9,... | collective-permute-start | bytes 3145736 | tf_op jit(solution)/shard_map/ppermute | solution.py:27
  97.0 38.9 %collective-permute-start.24 = (bf16[1024,512]{1,0:T(8,128)(2,1)S(1)}, bf16[1024,512]{1,0:T(8,128)(2,1)S(1)}, u32[]{:S(2)}, u32[]{:S(2)}) collective-permute-start(bf16[1024,512]{1,0:T(8,128)(2,1)S(1)} %collective-permute-done.8.refs_13_), channel_id=1, source_target_pairs={{0,16},{1,17},{2,18},{3,19},{4,20},{5,21},{6,22},{7,23},{8,24},{9,... | collective-permute-start | bytes 3145736 | tf_op jit(solution)/shard_map/ppermute | solution.py:27
  98.7 4.0 %collective-permute-start.22 = (f32[128,128]{0,1:T(8,128)S(1)}, f32[128,128]{0,1:T(8,128)S(1)}, u32[]{:S(2)}, u32[]{:S(2)}) collective-permute-start(f32[128,128]{0,1:T(8,128)S(1)} %dynamic-slice_add_fusion), channel_id=1, source_target_pairs={{0,4},{1,5},{2,6},{3,7},{4,0},{5,1},{6,2},{7,3},{8,12},{9,13},{10,... | collective-permute-start | bytes 196616 | tf_op jit(solution)/shard_map/ppermute | solution.py:27
  102.7 7.3 %collective-permute-start.23 = (f32[128,128]{0,1:T(8,128)S(1)}, f32[128,128]{0,1:T(8,128)S(1)}, u32[]{:S(2)}, u32[]{:S(2)}) collective-permute-start(f32[128,128]{0,1:T(8,128)S(1)} %add.314), channel_id=1, source_target_pairs={{0,8},{1,9},{2,10},{3,11},{4,12},{5,13},{6,14},{7,15},{8,0},{9,1},... | collective-permute-start | bytes 196616 | tf_op jit(solution)/shard_map/ppermute | solution.py:27
  106.1 11.0 %collective-permute-start.16 = (bf16[512,512]{1,0:T(8,128)(2,1)}, bf16[512,512]{1,0:T(8,128)(2,1)}, u32[]{:S(2)}, u32[]{:S(2)}) collective-permute-start(bf16[512,512]{1,0:T(8,128)(2,1)} %collective-permute-done.3.refs_8_), channel_id=1, source_target_pairs={{0,1},{1,2},{2,3},{3,0},{4,5},{5,6},{6,7},{7,4},{8,9},{9,10},{10,1... | collective-permute-start | bytes 1572872 | tf_op jit(solution)/shard_map/ppermute | solution.py:27
  110.0 13.3 %collective-permute-start.17 = (bf16[512,512]{1,0:T(8,128)(2,1)}, bf16[512,512]{1,0:T(8,128)(2,1)S(1)}, u32[]{:S(2)}, u32[]{:S(2)}) collective-permute-start(bf16[512,512]{1,0:T(8,128)(2,1)} %collective-permute-done.3.refs_8_), channel_id=1, source_target_pairs={{0,3},{1,0},{2,1},{3,2},{4,7},{5,4},{6,5},{7,6},{8,11},{9,8},{10,9... | collective-permute-start | bytes 1572872 | tf_op jit(solution)/shard_map/ppermute | solution.py:27
  110.0 0.8 copy-start.8
  110.8 25.0 %collective-permute-start.9 = (bf16[512,512]{1,0:T(8,128)(2,1)S(1)}, bf16[512,512]{1,0:T(8,128)(2,1)}, u32[]{:S(2)}, u32[]{:S(2)}) collective-permute-start(bf16[512,512]{1,0:T(8,128)(2,1)S(1)} %copy-done.1), channel_id=1, source_target_pairs={{0,8},{1,9},{2,10},{3,11},{4,12},{5,13},{6,14},{7,15},{8,0},{9,1},... | collective-permute-start | bytes 1572872 | tf_op jit(solution)/shard_map/ppermute | solution.py:27
  123.3 0.8 copy-start.10
  135.8 1.0 copy-start.2
  136.8 24.9 %collective-permute-start.25 = (bf16[1024,512]{1,0:T(8,128)(2,1)}, bf16[1024,512]{1,0:T(8,128)(2,1)}, u32[]{:S(2)}, u32[]{:S(2)}) collective-permute-start(bf16[1024,512]{1,0:T(8,128)(2,1)} %collective-permute-done.21.refs_14_), channel_id=1, source_target_pairs={{0,64},{1,65},{2,66},{3,67},{4,68},{5,69},{6,70},{7,71},{8,72},{9,... | collective-permute-start | bytes 3145736 | tf_op jit(solution)/shard_map/ppermute | solution.py:27
  136.9 21.1 %collective-permute-start.18 = (bf16[512,512]{1,0:T(8,128)(2,1)}, bf16[512,512]{1,0:T(8,128)(2,1)}, u32[]{:S(2)}, u32[]{:S(2)}) collective-permute-start(bf16[512,512]{1,0:T(8,128)(2,1)} %collective-permute-done.16.refs_9_), channel_id=1, source_target_pairs={{0,1},{1,2},{2,3},{3,0},{4,5},{5,6},{6,7},{7,4},{8,9},{9,10},{10,1... | collective-permute-start | bytes 1572872 | tf_op jit(solution)/shard_map/ppermute | solution.py:27
  138.6 19.4 %collective-permute-start.10 = (bf16[512,512]{1,0:T(8,128)(2,1)}, bf16[512,512]{1,0:T(8,128)(2,1)}, u32[]{:S(2)}, u32[]{:S(2)}) collective-permute-start(bf16[512,512]{1,0:T(8,128)(2,1)} %collective-permute-done.9.g0), channel_id=1, source_target_pairs={{0,1},{1,2},{2,3},{3,0},{4,5},{5,6},{6,7},{7,4},{8,9},{9,10},{10,1... | collective-permute-start | bytes 1572872 | tf_op jit(solution)/shard_map/ppermute | solution.py:27
  141.0 17.0 %collective-permute-start.11 = (bf16[512,512]{1,0:T(8,128)(2,1)}, bf16[512,512]{1,0:T(8,128)(2,1)}, u32[]{:S(2)}, u32[]{:S(2)}) collective-permute-start(bf16[512,512]{1,0:T(8,128)(2,1)} %collective-permute-done.9.g0), channel_id=1, source_target_pairs={{0,3},{1,0},{2,1},{3,2},{4,7},{5,4},{6,5},{7,6},{8,11},{9,8},{10,9... | collective-permute-start | bytes 1572872 | tf_op jit(solution)/shard_map/ppermute | solution.py:27
  141.0 16.9 %collective-permute-start.26 = (f32[128,128]{0,1:T(8,128)S(1)}, f32[128,128]{0,1:T(8,128)S(1)}, u32[]{:S(2)}, u32[]{:S(2)}) collective-permute-start(f32[128,128]{0,1:T(8,128)S(1)} %add.315), channel_id=1, source_target_pairs={{0,3},{1,2},{2,1},{3,0},{4,7},{5,6},{6,5},{7,4},{8,11},{9,10},{10,... | collective-permute-start | bytes 196616 | tf_op jit(solution)/shard_map/ppermute | solution.py:27
  158.0 11.4 %collective-permute-start.27 = (bf16[1024,512]{1,0:T(8,128)(2,1)}, bf16[1024,512]{1,0:T(8,128)(2,1)}, u32[]{:S(2)}, u32[]{:S(2)}) collective-permute-start(bf16[1024,512]{1,0:T(8,128)(2,1)} %collective-permute-done.21.refs_14_), channel_id=1, source_target_pairs={{0,16},{1,17},{2,18},{3,19},{4,20},{5,21},{6,22},{7,23},{8,24},{9,... | collective-permute-start | bytes 3145736 | tf_op jit(solution)/shard_map/ppermute | solution.py:27
  161.8 7.6 %collective-permute-start.28 = (bf16[1024,512]{1,0:T(8,128)(2,1)}, bf16[1024,512]{1,0:T(8,128)(2,1)}, u32[]{:S(2)}, u32[]{:S(2)}) collective-permute-start(bf16[1024,512]{1,0:T(8,128)(2,1)} %collective-permute-done.25.refs_15_), channel_id=1, source_target_pairs={{0,16},{1,17},{2,18},{3,19},{4,20},{5,21},{6,22},{7,23},{8,24},{9,... | collective-permute-start | bytes 3145736 | tf_op jit(solution)/shard_map/ppermute | solution.py:27
  161.9 4.7 %collective-permute-start.29 = (f32[256,128]{0,1:T(8,128)S(1)}, f32[256,128]{0,1:T(8,128)S(1)}, u32[]{:S(2)}, u32[]{:S(2)}) collective-permute-start(f32[256,128]{0,1:T(8,128)S(1)} %maximum_select_fusion.1), channel_id=1, source_target_pairs={{0,1},{1,0},{2,3},{3,2},{4,5},{5,4},{6,7},{7,6},{8,9},{9,8},{10,11... | collective-permute-start | bytes 393224 | tf_op jit(solution)/shard_map/ppermute | solution.py:27
  162.2 7.2 %copy-start.3 = (bf16[1024,512]{1,0:T(8,128)(2,1)S(1)}, bf16[1024,512]{1,0:T(8,128)(2,1)}, u32[]{:S(2)}) copy-start(bf16[1024,512]{1,0:T(8,128)(2,1)} %copy-done.2) | copy-start | bytes 3145732
  162.2 7.2 %copy-start.5 = (bf16[512,512]{1,0:T(8,128)(2,1)S(1)}, bf16[512,512]{1,0:T(8,128)(2,1)}, u32[]{:S(2)}) copy-start(bf16[512,512]{1,0:T(8,128)(2,1)} %copy-done.4) | copy-start | bytes 1572868
  162.2 7.2 %copy-start.7 = (bf16[512,512]{1,0:T(8,128)(2,1)S(1)}, bf16[512,512]{1,0:T(8,128)(2,1)}, u32[]{:S(2)}) copy-start(bf16[512,512]{1,0:T(8,128)(2,1)} %copy-done.6) | copy-start | bytes 1572868
  162.2 7.2 %copy-start.9 = (bf16[512,512]{1,0:T(8,128)(2,1)S(1)}, bf16[512,512]{1,0:T(8,128)(2,1)}, u32[]{:S(2)}) copy-start(bf16[512,512]{1,0:T(8,128)(2,1)} %copy-done.8) | copy-start | bytes 1572868
  162.2 7.2 %copy-start.11 = (bf16[512,512]{1,0:T(8,128)(2,1)S(1)}, bf16[512,512]{1,0:T(8,128)(2,1)}, u32[]{:S(2)}) copy-start(bf16[512,512]{1,0:T(8,128)(2,1)} %copy-done.10) | copy-start | bytes 1572868
  168.7 11.6 %collective-permute-start.12 = (bf16[512,512]{1,0:T(8,128)(2,1)}, bf16[512,512]{1,0:T(8,128)(2,1)S(1)}, u32[]{:S(2)}, u32[]{:S(2)}) collective-permute-start(bf16[512,512]{1,0:T(8,128)(2,1)} %collective-permute-done.10.g1), channel_id=1, source_target_pairs={{0,1},{1,2},{2,3},{3,0},{4,5},{5,6},{6,7},{7,4},{8,9},{9,10},{10,1... | collective-permute-start | bytes 1572872 | tf_op jit(solution)/shard_map/ppermute | solution.py:27

commit v3 on v0

v3 whole, which is shorter than its diff:
```python
import functools
import itertools

import jax
import jax.numpy as jnp
from jax import lax
from jax.experimental import pallas as pl
from jax.experimental.pallas import tpu as pltpu
from jax.sharding import Mesh, PartitionSpec as P

adapter_scale = 2.0
AXES = ("x", "zh", "c", "zl", "y")
SIZES = (4, 2, 2, 4, 4)
DIM = 512
VMEM = 56 * 1024 * 1024
ORDER = (
    "a A0 B0 Z1 Z3 Ry1:A0 | b0 b1 +Z A13 B13 Rz1 | +X XA XB Z2 +F F013 Ry3 | "
    "XF A2 B2 +S S1 Rz2 | F2 SF"
)
HELD = {"G": 0, "A0": 1, "B0": 1, "+Z": 1, "A13": 2, "B13": 2, "F013": 3, "Z2": 3, "A2": 4, "B2": 4, "F2": 5}
WEIGHTS = {"+X": 2, "XA": 3, "XB": 3, "S1": 4, "XF": 4, "SF": 5}
STAGES = (3, 4, 5)


def moves(target):
    pairs = []
    for source, place in enumerate(itertools.product(*[range(n) for n in SIZES])):
        index = 0
        for n, i in zip(SIZES, target(*place)):
            index = index * n + i % n
        pairs.append((source, index))
    return pairs


def send(value, target):
    return lax.ppermute(value, AXES, moves(target))


def after(value, *others):
    return lax.optimization_barrier((value, *others))[0]


def way(c):
    return 1 - 2 * c


def times(g, w):
    return lax.dot_general(g, w, (((1,), (1,)), ((), ())), preferred_element_type=jnp.float32)


def product_kernel(pairs, n_g, n_w, first, final, which_ref, *refs):
    g_refs, w_refs, rest = refs[:n_g], refs[n_g : n_g + n_w], refs[n_g + n_w :]
    if not first:
        sum_ref, rest = rest[0], rest[1:]
    if final:
        kept_ref, add_ref, rest = rest[0], rest[1], rest[2:]
    out_ref, gs, ws, acc, g_sems, w_sems = rest
    for k, (i, w_array, w_place, choices) in enumerate(pairs):
        for n, g_array, g_place in choices:

            @pl.when(which_ref[i] == n)
            def _():
                pltpu.make_async_copy(
                    g_refs[g_array].at[pl.ds(g_place * DIM, DIM)], gs.at[k], g_sems.at[k]
                ).start()
                pltpu.make_async_copy(
                    w_refs[w_array].at[pl.ds(w_place * DIM, DIM)], ws.at[k], w_sems.at[k]
                ).start()

    acc[...] = jnp.zeros_like(acc) if first else sum_ref[...]
    for k, (i, _, _, choices) in enumerate(pairs):
        hit = which_ref[i] == choices[0][0]
        for n, _, _ in choices[1:]:
            hit = jnp.logical_or(hit, which_ref[i] == n)

        @pl.when(hit)
        def _():
            pltpu.make_async_copy(gs.at[k], gs.at[k], g_sems.at[k]).wait()
            pltpu.make_async_copy(ws.at[k], ws.at[k], w_sems.at[k]).wait()
            acc[...] += times(gs[k], ws[k])

    if final:
        out_ref[...] = (acc[...] * kept_ref[...] + add_ref[...]).astype(out_ref.dtype)
    else:
        out_ref[...] = acc[...]


def partial_sum(stage, which, value, g_places, w_places, total, *ends):
    place = STAGES.index(stage)
    ahead = STAGES[place - 1] if place else -1
    g_names = [n for n in HELD if HELD[n] <= stage]
    w_names = [n for n in WEIGHTS if WEIGHTS[n] <= stage]
    pairs = []
    for i, (w_name, w_place) in enumerate(w_places):
        if w_name not in w_names:
            continue
        choices = [
            (n, g_name, g_place)
            for n, (g_name, g_place) in enumerate(g_places)
            if g_name in g_names and max(HELD[g_name], WEIGHTS[w_name]) > ahead
        ]
        if choices:
            pairs.append((i, w_name, w_place, choices))
    g_names = [n for n in g_names if any(g == n for p in pairs for _, g, _ in p[3])]
    w_names = [n for n in w_names if any(p[1] == n for p in pairs)]
    pairs = [
        (i, w_names.index(w), w_place, [(n, g_names.index(g), g_place) for n, g, g_place in choices])
        for i, w, w_place, choices in pairs
    ]
    rows = value["G"].shape[0]
    anywhere = pl.BlockSpec(memory_space=pl.ANY)
    in_vmem = pl.BlockSpec(memory_space=pltpu.VMEM)
    more = [v for v in (total, *ends) if v is not None]
    count = 16 if stage == STAGES[0] else 8
    return pl.pallas_call(
        functools.partial(product_kernel, pairs, len(g_names), len(w_names), total is None, bool(ends)),
        out_shape=jax.ShapeDtypeStruct((rows, DIM), jnp.bfloat16 if ends else jnp.float32),
        in_specs=[pl.BlockSpec(memory_space=pltpu.SMEM)]
        + [anywhere] * (len(g_names) + len(w_names))
        + [in_vmem] * len(more),
        out_specs=in_vmem,
        scratch_shapes=[
            pltpu.VMEM((len(pairs), rows, DIM), jnp.bfloat16),
            pltpu.VMEM((len(pairs), DIM, DIM), jnp.bfloat16),
            pltpu.VMEM((rows, DIM), jnp.float32),
            pltpu.SemaphoreType.DMA((len(pairs),)),
            pltpu.SemaphoreType.DMA((len(pairs),)),
        ],
        compiler_params=pltpu.CompilerParams(vmem_limit_bytes=VMEM),
        cost_estimate=pl.CostEstimate(
            flops=2 * rows * DIM * DIM * count,
            bytes_accessed=count * 1024 * 1024,
            transcendentals=0,
        ),
    )(which, *[value[n] for n in g_names], *[value[n] for n in w_names], *more)


def shards(projection_input, output_gradient, frozen_weight, down_adapters, up_adapters, lengths):
    tokens = output_gradient.shape[0]
    highest = lax.Precision.HIGHEST
    x, zh, c, zl, y = (lax.axis_index(a) for a in AXES)
    turn = way(c)

    positions = lax.iota(jnp.int32, tokens)
    kept = positions < lengths[0]
    masked_rows = output_gradient * kept.astype(output_gradient.dtype)[:, None]
    down_adapter = down_adapters[0]
    up_adapter = up_adapters[0]
    rank_width = down_adapter.shape[0]
    lowered_part = jnp.dot(projection_input, down_adapter.T, preferred_element_type=jnp.float32)
    pulled_part = jnp.dot(masked_rows, up_adapter.T, preferred_element_type=jnp.float32)
    rank_both = jnp.concatenate([lowered_part, pulled_part], axis=1)

    def to_half(s):
        return lambda x, zh, c, zl, y: (x, (y // 2) ^ s, c, zl + way(c) * x, 2 * zh + y % 2)

    def join(*parts):
        return jnp.concatenate(parts, axis=0)

    def swap(dz, dy):
        return lambda v: send(v, lambda x, zh, c, zl, y: (x, zh, c, zl ^ dz, y ^ dy))

    def add_from(dz, dy):
        return lambda v: v + swap(dz, dy)(v)

    def on(v):
        return send(v, lambda x, zh, c, zl, y: (x, zh, c, zl, y + way(c)))

    def back(v):
        return send(v, lambda x, zh, c, zl, y: (x, zh, c, zl, y - way(c)))

    def sibling(v):
        return send(v, lambda x, zh, c, zl, y: (x, zh, 1 - c, zl, y))

    steps = {
        "a": (("W",), lambda v: send(v, lambda x, zh, c, zl, y: (way(y % 2) * (x - zl), zh, y % 2, zl, 2 * (y // 2) + c))),
        "b0": (("a",), lambda v: send(v, to_half(0))),
        "b1": (("a",), lambda v: send(v, to_half(1))),
        "+X": (("b0", "b1"), join),
        "XA": (("+X",), lambda v: send(v, lambda x, zh, c, zl, y: (x + way(c), zh, c, zl, y))),
        "XB": (("+X",), lambda v: send(v, lambda x, zh, c, zl, y: (x - way(c), zh, c, zl, y))),
        "XF": (("XA",), lambda v: send(v, lambda x, zh, c, zl, y: (x + way(c), zh, c, zl, y))),
        "+S": (("+X", "XA", "XB"), join),
        "S1": (("+S",), sibling),
        "SF": (("XF",), sibling),
        "Z1": (("G",), lambda v: send(v, lambda x, zh, c, zl, y: (x, zh, c, zl + 1, y))),
        "Z2": (("G",), lambda v: send(v, lambda x, zh, c, zl, y: (x, zh, c, zl + 2, y))),
        "Z3": (("G",), lambda v: send(v, lambda x, zh, c, zl, y: (x, zh, c, zl + 3, y))),
        "+Z": (("Z1", "Z3"), join),
        "A0": (("G",), on),
        "B0": (("G",), back),
        "A13": (("+Z",), on),
        "B13": (("+Z",), back),
        "+F": (("A0", "A13"), join),
        "F013": (("+F",), on),
        "A2": (("Z2",), on),
        "B2": (("Z2",), back),
        "F2": (("A2",), on),
        "Ry1": (("R",), add_from(0, 1)),
        "Rz1": (("Ry1",), add_from(1, 0)),
        "Ry3": (("Rz1",), add_from(0, 3)),
        "Rz2": (("Ry3",), add_from(2, 0)),
    }
    value = {"W": frozen_weight, "G": output_gradient, "R": rank_both}
    g_places, g_slots = [], []
    for name in HELD:
        e = {"A": -turn, "B": turn, "F": 2}.get(name[0], 0)
        js = {"0": (0,), "G": (0,), "2": (2,)}.get(name[-1], (1, 3))
        js = (0, 1, 3) if name == "F013" else js
        for i, j in enumerate(js):
            g_places.append((name, i))
            g_slots.append(4 * ((zl - j) % 4) + (y + e) % 4)
    w_places, w_slots = [], []
    for name, core, froms in (
        ("+X", c, (x,)),
        ("XA", c, (x - turn,)),
        ("XB", c, (x + turn,)),
        ("S1", 1 - c, (x, x + turn, x - turn)),
        ("XF", c, (x + 2,)),
        ("SF", 1 - c, (x + 2,)),
    ):
        for i, from_x in enumerate(froms):
            for s in range(2):
                w_places.append((name, 2 * i + s))
                w_slots.append(4 * ((zl - way(core) * from_x) % 4) + 2 * (zh ^ s) + core)
    same = jnp.stack(w_slots)[:, None] == jnp.stack(g_slots)[None, :]
    which = jnp.sum(jnp.where(same, jnp.arange(16)[None, :], 0), axis=1).astype(jnp.int32)

    def ends(rank_both):
        rank_projected = rank_both[:, :rank_width]
        scaled_gradient = adapter_scale * rank_both[:, rank_width:]
        adapter_part = jnp.dot(scaled_gradient, down_adapter.astype(jnp.float32), precision=highest)
        inverse_order = 1.0 / lengths[0].astype(jnp.float32)
        down_gradient = (
            jnp.dot(scaled_gradient.T, projection_input.astype(jnp.float32), precision=highest)
            * inverse_order
        )[None]
        up_gradient = (
            adapter_scale
            * jnp.dot(rank_projected.T, masked_rows.astype(jnp.float32), precision=highest)
            * inverse_order
        )[None]
        return adapter_part, down_gradient, up_gradient

    before, beside = [], []
    for number, group in enumerate(ORDER.split("|"), 1):
        names = []
        for entry in group.split():
            name, mark, waits = entry.replace("=", ":=").partition(":")
            takes, act = steps[name]
            given = [value[n] for n in takes]
            if name[0] != "+":
                ahead = [] if waits[:1] == "=" else before
                ahead = ahead + [value[n] for n in waits.strip("=").split(",") if n]
                given[0] = after(given[0], *ahead) if ahead else given[0]
                names.append(name)
            value[name] = act(*given)
        before, beside = [value[n] for n in names] + beside, []
        if number == 3:
            total = partial_sum(number, which, value, g_places, w_places, None)
            beside = [total]
        if number == 4:
            total = partial_sum(number, which, value, g_places, w_places, total)
    adapter_part, down_gradient, up_gradient = ends(value["Rz2"])
    grad_input = partial_sum(5, which, value, g_places, w_places, total, kept.astype(jnp.float32)[:, None], adapter_part)
    return (grad_input, down_gradient, up_gradient)


def solution(mesh):
    parts = Mesh(mesh.devices.reshape(SIZES), AXES)
    tenant, tensor = ("x", "zh", "c"), ("zl", "y")
    placed = (
        P(tenant, tensor),
        P(tenant, tensor),
        P(tenant, tensor),
        P(tenant, None, tensor),
        P(tenant, None, tensor),
        P(tenant),
    )
    return jax.shard_map(
        shards,
        mesh=parts,
        in_specs=placed,
        out_specs=(P(tenant, tensor), P(tenant, None, tensor), P(tenant, None, tensor)),
        check_vma=False,
    )
```

time: 424 us -> 144 us (0.34)
  waiting for transfers between devices: 384 us -> 67 us
  starting transfers between devices: 0.13 us -> 43.8 us
  Pallas kernels: 0 us -> 18.7 us
  matrix products: 23.1 us -> 6.27 us
  between operations: 16.2 us -> 1.81 us
    reduce_scatter x1 -> x0, waiting for transfers between devices: 194 us -> none  [shards(): lax.psum_scatter(partial_value, 'tensor', scatter_dimension=1, tiled=True)]
    all_gather x1 -> x0, waiting for transfers between devices: 109 us -> none  [shards(): lax.all_gather(frozen_weight, 'tenant', axis=0, tiled=True)]
    psum x1 -> x0, waiting for transfers between devices: 79.6 us -> none  [shards(): lax.psum(jnp.concatenate([lowered_part, pulled_part], axis=1), 'tensor')]
    ppermute x0 -> x23, waiting for transfers between devices: none -> 67 us  [send(): return lax.ppermute(value, AXES, moves(target))]
    ppermute x0 -> x23, starting transfers between devices: none -> 43.8 us  [send(): return lax.ppermute(value, AXES, moves(target))]
    pallas_call x0 -> x3, Pallas kernels: none -> 18.7 us  [partial_sum(): pl.pallas_call(functools.partial(product_kernel, pairs, len(g_names), len...]
    dot_general x4 -> x3, matrix products: 20.6 us -> 3.76 us  [the longest x1 1.6 us: ends(): jnp.dot(scaled_gradient, down_adapter.astype(jnp.float32), precision=high...]
  transfers between devices with their start and end apart: 3 -> 23, of which waited for: 3 -> 8; matrix products, arithmetic and copies ran while one was open for 5% -> 7% of each run, Pallas kernels for 0% -> 9%
where the time goes in v3:
time: 144 us; the launch traced here: 143 us
  waiting for transfers between devices  67 us (47%)
  starting transfers between devices  43.8 us (30%)
  Pallas kernels  18.7 us (13%)
  matrix products  6.27 us (4%)
  other arithmetic  3.59 us (2%)
  local copies, waits for them, and re-layouts  2.31 us (2%)
  between operations  1.81 us (1%)
    ppermute x23, waiting for transfers between devices, send(): return lax.ppermute(value, AXES, moves(target))  67 us
    ppermute x23, starting transfers between devices, send(): return lax.ppermute(value, AXES, moves(target))  43.8 us
    pallas_call x3, Pallas kernels, partial_sum(): pl.pallas_call(functools.partial(product_kernel, pairs, len(g_names), len...  18.7 us
  transfers between devices with their start and end apart: 23, of which 8 were waited for; matrix products, arithmetic and copies ran while one was open for 7% of the time, Pallas kernels for 9%

profile of v3, /device:TPU:1, one launch (start us, length us, event | category | flops | bytes accessed | tf_op | source)
XLA Modules:
  0.0 143.5 jit_solution(6093922756866457386)
XLA Ops:
  0.6 0.0 copy-start
  0.6 3.6 %collective-permute-start = (bf16[512,512]{1,0:T(8,128)(2,1)}, bf16[512,512]{1,0:T(8,128)(2,1)S(1)}, u32[]{:S(2)}, u32[]{:S(2)}) collective-permute-start(bf16[512,512]{1,0:T(8,128)(2,1)} %refs_0_.5), channel_id=1, source_target_pairs={{0,1},{1,2},{2,3},{3,0},{4,5},{5,6},{6,7},{7,4},{8,9},{9,10},{10,1... | collective-permute-start | bytes 1572872 | tf_op jit(solution)/shard_map/ppermute | solution.py:36
  4.3 0.0 collective-permute-start.1
  4.3 1.6 %collective-permute-start.2 = (bf16[512,512]{1,0:T(8,128)(2,1)}, bf16[512,512]{1,0:T(8,128)(2,1)S(1)}, u32[]{:S(2)}, u32[]{:S(2)}) collective-permute-start(bf16[512,512]{1,0:T(8,128)(2,1)} %refs_0_.5), channel_id=1, source_target_pairs={{0,4},{1,5},{2,6},{3,7},{4,8},{5,9},{6,10},{7,11},{8,12},{9,13},{1... | collective-permute-start | bytes 1572872 | tf_op jit(solution)/shard_map/ppermute | solution.py:36
  5.9 2.7 %collective-permute-start.3 = (bf16[512,512]{1,0:T(8,128)(2,1)}, bf16[512,512]{1,0:T(8,128)(2,1)S(1)}, u32[]{:S(2)}, u32[]{:S(2)}) collective-permute-start(bf16[512,512]{1,0:T(8,128)(2,1)} %refs_0_.5), channel_id=1, source_target_pairs={{0,12},{1,13},{2,14},{3,15},{4,0},{5,1},{6,2},{7,3},{8,4},{9,5},{1... | collective-permute-start | bytes 1572872 | tf_op jit(solution)/shard_map/ppermute | solution.py:36
  8.6 3.3 %collective-permute-start.4 = (bf16[512,512]{1,0:T(8,128)(2,1)}, bf16[512,512]{1,0:T(8,128)(2,1)S(1)}, u32[]{:S(2)}, u32[]{:S(2)}) collective-permute-start(bf16[512,512]{1,0:T(8,128)(2,1)} %param.8), channel_id=1, source_target_pairs={{0,0},{1,16},{2,2},{3,18},{4,196},{5,84},{6,198},{7,86},{8,136},{9... | collective-permute-start | bytes 1572872 | tf_op jit(solution)/shard_map/ppermute | solution.py:36
  12.6 1.4 fusion.3
  14.0 1.1 fusion.12
  15.2 0.0 collective-permute-done.refs_1_
  15.2 0.1 collective-permute-start.5
  15.3 3.9 %collective-permute-done.2 = bf16[512,512]{1,0:T(8,128)(2,1)S(1)} collective-permute-done((bf16[512,512]{1,0:T(8,128)(2,1)}, bf16[512,512]{1,0:T(8,128)(2,1)S(1)}, u32[]{:S(2)}, u32[]{:S(2)}) %collective-permute-start.2) | collective-permute-done | bytes 524320 | tf_op jit(solution)/shard_map/ppermute | solution.py:36
  19.2 11.0 %collective-permute-done.3 = bf16[512,512]{1,0:T(8,128)(2,1)S(1)} collective-permute-done((bf16[512,512]{1,0:T(8,128)(2,1)}, bf16[512,512]{1,0:T(8,128)(2,1)S(1)}, u32[]{:S(2)}, u32[]{:S(2)}) %collective-permute-start.3) | collective-permute-done | bytes 524320 | tf_op jit(solution)/shard_map/ppermute | solution.py:36
  30.3 0.0 collective-permute-done.5
  30.4 0.0 copy-start.7
  30.4 0.0 collective-permute-done.1.refs_2_
  30.4 0.0 collective-permute-done.4
  30.4 3.5 %collective-permute-start.6 = (bf16[1024,512]{1,0:T(8,128)(2,1)S(1)}, bf16[1024,512]{1,0:T(8,128)(2,1)S(1)}, u32[]{:S(2)}, u32[]{:S(2)}) collective-permute-start(bf16[1024,512]{1,0:T(8,128)(2,1)S(1)} %constant_dynamic-update-slice_fusion.refs_3_), channel_id=1, source_target_pairs={{0,1},{1,2},{2,3},{3,0},{4,5},{5,6},{6,7},{7,4},{8,9},{9,10},{10,1... | collective-permute-start | bytes 3145736 | tf_op jit(solution)/shard_map/ppermute | solution.py:36
  33.9 0.0 collective-permute-start.7
  33.9 0.7 collective-permute-start.8
  34.6 1.9 %collective-permute-start.10 = (f32[512,128]{0,1:T(8,128)S(1)}, f32[512,128]{0,1:T(8,128)S(1)}, u32[]{:S(2)}, u32[]{:S(2)}) collective-permute-start(f32[512,128]{0,1:T(8,128)S(1)} %add.335), channel_id=1, source_target_pairs={{0,4},{1,5},{2,6},{3,7},{4,0},{5,1},{6,2},{7,3},{8,12},{9,13},{10,... | collective-permute-start | bytes 786440 | tf_op jit(solution)/shard_map/ppermute | solution.py:36
  36.5 7.6 %collective-permute-start.9 = (bf16[512,512]{1,0:T(8,128)(2,1)S(1)}, bf16[512,512]{1,0:T(8,128)(2,1)S(1)}, u32[]{:S(2)}, u32[]{:S(2)}) collective-permute-start(bf16[512,512]{1,0:T(8,128)(2,1)S(1)} %collective-permute-done.4), channel_id=1, source_target_pairs={{0,32},{1,33},{2,0},{3,1},{4,36},{5,37},{6,4},{7,5},{8,40},{9,41},... | collective-permute-start | bytes 1572872 | tf_op jit(solution)/shard_map/ppermute | solution.py:36
  44.1 0.0 collective-permute-done.10
  44.1 0.0 collective-permute-done.8
  44.2 22.3 %collective-permute-done.6.refs_4_ = bf16[1024,512]{1,0:T(8,128)(2,1)S(1)} collective-permute-done((bf16[1024,512]{1,0:T(8,128)(2,1)S(1)}, bf16[1024,512]{1,0:T(8,128)(2,1)S(1)}, u32[]{:S(2)}, u32[]{:S(2)}) %collective-permute-start.6) | collective-permute-done | bytes 1048608 | tf_op jit(solution)/shard_map/ppermute | solution.py:36
  66.4 0.1 pad_maximum_fusion.1
  66.6 2.3 %collective-permute-done.9 = bf16[512,512]{1,0:T(8,128)(2,1)S(1)} collective-permute-done((bf16[512,512]{1,0:T(8,128)(2,1)S(1)}, bf16[512,512]{1,0:T(8,128)(2,1)S(1)}, u32[]{:S(2)}, u32[]{:S(2)}) %collective-permute-start.9) | collective-permute-done | bytes 524320 | tf_op jit(solution)/shard_map/ppermute | solution.py:36
  68.9 0.0 collective-permute-done.7.refs_5_
  68.9 3.6 %collective-permute-start.11 = (bf16[1536,512]{1,0:T(8,128)(2,1)S(1)}, bf16[1536,512]{1,0:T(8,128)(2,1)S(1)}, u32[]{:S(2)}, u32[]{:S(2)}) collective-permute-start(bf16[1536,512]{1,0:T(8,128)(2,1)S(1)} %pad_maximum_fusion.1), channel_id=1, source_target_pairs={{0,1},{1,2},{2,3},{3,0},{4,5},{5,6},{6,7},{7,4},{8,9},{9,10},{10,1... | collective-permute-start | bytes 4718600 | tf_op jit(solution)/shard_map/ppermute | solution.py:36
  72.5 3.4 %collective-permute-start.13 = (bf16[1024,512]{1,0:T(8,128)(2,1)S(1)}, bf16[1024,512]{1,0:T(8,128)(2,1)S(1)}, u32[]{:S(2)}, u32[]{:S(2)}) collective-permute-start(bf16[1024,512]{1,0:T(8,128)(2,1)S(1)} %constant_dynamic-update-slice_fusion.2.refs_8_.refs_10_.refs_11_), channel_id=1, source_target_pairs={{0,64},{1,65},{2,66},{3,67},{4,68},{5,69},{6,70},{7,71},{8,72},{9,... | collective-permute-start | bytes 3145736 | tf_op jit(solution)/shard_map/ppermute | solution.py:36
  76.0 0.0 collective-permute-start.14
  76.0 0.4 collective-permute-start.15
  76.4 1.7 %collective-permute-start.12 = (bf16[512,512]{1,0:T(8,128)(2,1)S(1)}, bf16[512,512]{1,0:T(8,128)(2,1)S(1)}, u32[]{:S(2)}, u32[]{:S(2)}) collective-permute-start(bf16[512,512]{1,0:T(8,128)(2,1)S(1)} %copy-done.7), channel_id=1, source_target_pairs={{0,8},{1,9},{2,10},{3,11},{4,12},{5,13},{6,14},{7,15},{8,0},{9,1},... | collective-permute-start | bytes 1572872 | tf_op jit(solution)/shard_map/ppermute | solution.py:36
  78.2 17.3 %collective-permute-done.15 = f32[512,128]{0,1:T(8,128)S(1)} collective-permute-done((f32[512,128]{0,1:T(8,128)S(1)}, f32[512,128]{0,1:T(8,128)S(1)}, u32[]{:S(2)}, u32[]{:S(2)}) %collective-permute-start.15) | collective-permute-done | bytes 262176 | tf_op jit(solution)/shard_map/ppermute | solution.py:36
  95.5 0.0 copy-start.15
  95.5 1.8 %collective-permute-done.13.refs_9_.refs_11_.refs_12_ = bf16[1024,512]{1,0:T(8,128)(2,1)S(1)} collective-permute-done((bf16[1024,512]{1,0:T(8,128)(2,1)S(1)}, bf16[1024,512]{1,0:T(8,128)(2,1)S(1)}, u32[]{:S(2)}, u32[]{:S(2)}) %collective-permute-start.13) | collective-permute-done | bytes 1048608 | tf_op jit(solution)/shard_map/ppermute | solution.py:36
  97.3 3.5 %collective-permute-done.14.refs_10_.refs_12_.refs_13_ = bf16[1024,512]{1,0:T(8,128)(2,1)S(1)} collective-permute-done((bf16[1024,512]{1,0:T(8,128)(2,1)S(1)}, bf16[1024,512]{1,0:T(8,128)(2,1)S(1)}, u32[]{:S(2)}, u32[]{:S(2)}) %collective-permute-start.14) | collective-permute-done | bytes 1048608 | tf_op jit(solution)/shard_map/ppermute | solution.py:36
  100.8 1.8 %pad_maximum_fusion = bf16[3072,512]{1,0:T(8,128)(2,1)} fusion(bf16[1024,512]{1,0:T(8,128)(2,1)S(1)} %collective-permute-done.14.refs_10_.refs_12_.refs_13_, bf16[1024,512]{1,0:T(8,128)(2,1)S(1)} %collective-permute-done.13.refs_9_.refs_11_.refs_12_, bf16[512,512]{1,0:T(8,128)(2,1)S(1)} %collective-permute-done.9, bf16[512,512]{1,0:T(8,128)(2,1)S(1)} %collective-permute-done.8), kind=kLoop, calls=%fused_computation | loop fusion | flops 12582912 | bytes 6291456 | tf_op jit(solution)/shard_map/concatenate | solution.py:158
  102.6 0.1 copy-done.3
  102.7 0.0 collective-permute-done.12.refs_7_
  102.7 0.0 collective-permute-done.11.refs_6_
  102.7 0.2 collective-permute-start.19
  103.0 3.4 %collective-permute-start.18 = (bf16[1024,512]{1,0:T(8,128)(2,1)S(1)}, bf16[1024,512]{1,0:T(8,128)(2,1)}, u32[]{:S(2)}, u32[]{:S(2)}) collective-permute-start(bf16[1024,512]{1,0:T(8,128)(2,1)S(1)} %collective-permute-done.13.refs_9_.refs_11_.refs_12_), channel_id=1, source_target_pairs={{0,64},{1,65},{2,66},{3,67},{4,68},{5,69},{6,70},{7,71},{8,72},{9,... | collective-permute-start | bytes 3145736 | tf_op jit(solution)/shard_map/ppermute | solution.py:36
  106.4 1.2 collective-permute-start.16
  107.5 0.3 collective-permute-start.17
  107.8 0.1 stack.118
  107.9 0.1 stack.135
  108.0 0.8 select_reduce_fusion.which_ref
  108.8 1.9 %collective-permute-start.20 = (f32[512,128]{0,1:T(8,128)S(1)}, f32[512,128]{0,1:T(8,128)S(1)}, u32[]{:S(2)}, u32[]{:S(2)}) collective-permute-start(f32[512,128]{0,1:T(8,128)S(1)} %add.337), channel_id=1, source_target_pairs={{0,8},{1,9},{2,10},{3,11},{4,12},{5,13},{6,14},{7,15},{8,0},{9,1},... | collective-permute-start | bytes 786440 | tf_op jit(solution)/shard_map/ppermute | solution.py:36
  110.7 6.0 %shard_map.85.refs_15_ = f32[512,512]{1,0:T(8,128)} custom-call(s32[16]{0:T(128)} %select_reduce_fusion.which_ref, bf16[512,512]{1,0:T(8,128)(2,1)} %refs_0_.5, bf16[512,512]{1,0:T(8,128)(2,1)} %copy-done.9, bf16[512,512]{1,0:T(8,128)(2,1)} %copy-done.11, bf16[1024,512]{1,0:T(8,128)(2,1)} %copy-done.5, bf16[1024,512]{1,0:T(8,128)(2,1)} %copy-done.1, ...), custom_call_target="tpu_custom_call" | custom-call | flops 4294967296 | bytes 16777216 | tf_op jit(solution)/shard_map/pallas_call | solution.py:115
  116.7 4.9 %collective-permute-done.20 = f32[512,128]{0,1:T(8,128)S(1)} collective-permute-done((f32[512,128]{0,1:T(8,128)S(1)}, f32[512,128]{0,1:T(8,128)S(1)}, u32[]{:S(2)}, u32[]{:S(2)}) %collective-permute-start.20) | collective-permute-done | bytes 262176 | tf_op jit(solution)/shard_map/ppermute | solution.py:36
  121.6 0.0 collective-permute-done.16.refs_8_
  121.7 0.0 collective-permute-done.17.refs_9_
  121.7 0.0 collective-permute-done.18.refs_14_.refs_15_
  121.7 0.0 collective-permute-done.19.refs_13_.refs_14_
  121.7 1.2 collective-permute-start.22
  122.9 0.7 fusion.7.refs_18_
  123.7 1.1 fusion
  124.8 1.4 collective-permute-start.21
  126.2 1.0 fusion.1
  127.2 1.6 %fusion.9.refs_19_ = f32[512,512]{1,0:T(8,128)} fusion(f32[512,128]{0,1:T(8,128)S(1)} %add.338, bf16[1,64,512]{2,1,0:T(8,128)(2,1)S(1)} %copy-done.18), kind=kOutput, calls=%fused_computation.16 | convolution fusion | flops 201359360 | bytes 1245184 | tf_op jit(solution)/shard_map/dot_general | solution.py:232
  128.8 7.6 %shard_map.86.refs_17_ = f32[512,512]{1,0:T(8,128)} custom-call(s32[16]{0:T(128)} %select_reduce_fusion.which_ref, bf16[512,512]{1,0:T(8,128)(2,1)} %refs_0_.5, bf16[512,512]{1,0:T(8,128)(2,1)} %copy-done.9, bf16[512,512]{1,0:T(8,128)(2,1)} %copy-done.11, bf16[1024,512]{1,0:T(8,128)(2,1)} %copy-done.5, bf16[1024,512]{1,0:T(8,128)(2,1)} %copy-done.1, ...), custom_call_target="tpu_custom_call" | custom-call | flops 2147483648 | bytes 8388608 | tf_op jit(solution)/shard_map/pallas_call | solution.py:115
  136.4 0.8 copy-done.17
  137.2 1.0 copy-done.14
  138.2 5.1 %shard_map.87 = bf16[512,512]{1,0:T(8,128)(2,1)} custom-call(s32[16]{0:T(128)} %select_reduce_fusion.which_ref, bf16[512,512]{1,0:T(8,128)(2,1)} %refs_0_.5, bf16[512,512]{1,0:T(8,128)(2,1)} %copy-done.9, bf16[512,512]{1,0:T(8,128)(2,1)} %copy-done.11, bf16[1024,512]{1,0:T(8,128)(2,1)} %copy-done.5, bf16[1024,512]{1,0:T(8,128)(2,1)} %copy-done.1, ...), custom_call_target="tpu_custom_call" | custom-call | flops 2147483648 | bytes 8388608 | tf_op jit(solution)/shard_map/pallas_call | solution.py:115
  (44 shorter events, 0.4 us)
Async XLA Ops:
  0.6 13.4 %copy-start = (bf16[512,512]{1,0:T(8,128)(2,1)S(1)}, bf16[512,512]{1,0:T(8,128)(2,1)}, u32[]{:S(2)}) copy-start(bf16[512,512]{1,0:T(8,128)(2,1)} %param.6) | copy-start | bytes 1572868
  0.6 14.5 %collective-permute-start = (bf16[512,512]{1,0:T(8,128)(2,1)}, bf16[512,512]{1,0:T(8,128)(2,1)S(1)}, u32[]{:S(2)}, u32[]{:S(2)}) collective-permute-start(bf16[512,512]{1,0:T(8,128)(2,1)} %refs_0_.5), channel_id=1, source_target_pairs={{0,1},{1,2},{2,3},{3,0},{4,5},{5,6},{6,7},{7,4},{8,9},{9,10},{10,1... | collective-permute-start | bytes 1572872 | tf_op jit(solution)/shard_map/ppermute | solution.py:36
  4.3 26.1 %collective-permute-start.1 = (bf16[512,512]{1,0:T(8,128)(2,1)}, bf16[512,512]{1,0:T(8,128)(2,1)S(1)}, u32[]{:S(2)}, u32[]{:S(2)}) collective-permute-start(bf16[512,512]{1,0:T(8,128)(2,1)} %refs_0_.5), channel_id=1, source_target_pairs={{0,3},{1,0},{2,1},{3,2},{4,7},{5,4},{6,5},{7,6},{8,11},{9,8},{10,9... | collective-permute-start | bytes 1572872 | tf_op jit(solution)/shard_map/ppermute | solution.py:36
  4.3 14.9 %collective-permute-start.2 = (bf16[512,512]{1,0:T(8,128)(2,1)}, bf16[512,512]{1,0:T(8,128)(2,1)S(1)}, u32[]{:S(2)}, u32[]{:S(2)}) collective-permute-start(bf16[512,512]{1,0:T(8,128)(2,1)} %refs_0_.5), channel_id=1, source_target_pairs={{0,4},{1,5},{2,6},{3,7},{4,8},{5,9},{6,10},{7,11},{8,12},{9,13},{1... | collective-permute-start | bytes 1572872 | tf_op jit(solution)/shard_map/ppermute | solution.py:36
  5.9 24.3 %collective-permute-start.3 = (bf16[512,512]{1,0:T(8,128)(2,1)}, bf16[512,512]{1,0:T(8,128)(2,1)S(1)}, u32[]{:S(2)}, u32[]{:S(2)}) collective-permute-start(bf16[512,512]{1,0:T(8,128)(2,1)} %refs_0_.5), channel_id=1, source_target_pairs={{0,12},{1,13},{2,14},{3,15},{4,0},{5,1},{6,2},{7,3},{8,4},{9,5},{1... | collective-permute-start | bytes 1572872 | tf_op jit(solution)/shard_map/ppermute | solution.py:36
  8.6 21.8 %collective-permute-start.4 = (bf16[512,512]{1,0:T(8,128)(2,1)}, bf16[512,512]{1,0:T(8,128)(2,1)S(1)}, u32[]{:S(2)}, u32[]{:S(2)}) collective-permute-start(bf16[512,512]{1,0:T(8,128)(2,1)} %param.8), channel_id=1, source_target_pairs={{0,0},{1,16},{2,2},{3,18},{4,196},{5,84},{6,198},{7,86},{8,136},{9... | collective-permute-start | bytes 1572872 | tf_op jit(solution)/shard_map/ppermute | solution.py:36
  15.2 51.4 %copy-start.9 = (bf16[512,512]{1,0:T(8,128)(2,1)}, bf16[512,512]{1,0:T(8,128)(2,1)S(1)}, u32[]{:S(2)}) copy-start(bf16[512,512]{1,0:T(8,128)(2,1)S(1)} %collective-permute-done.refs_1_) | copy-start | bytes 1572868
  15.2 15.1 %collective-permute-start.5 = (f32[512,128]{0,1:T(8,128)S(1)}, f32[512,128]{0,1:T(8,128)S(1)}, u32[]{:S(2)}, u32[]{:S(2)}) collective-permute-start(f32[512,128]{0,1:T(8,128)S(1)} %pad_maximum_fusion.2), channel_id=1, source_target_pairs={{0,1},{1,0},{2,3},{3,2},{4,5},{5,4},{6,7},{7,6},{8,9},{9,8},{10,11... | collective-permute-start | bytes 786440 | tf_op jit(solution)/shard_map/ppermute | solution.py:36
  30.3 42.2 %copy-start.5 = (bf16[1024,512]{1,0:T(8,128)(2,1)}, bf16[1024,512]{1,0:T(8,128)(2,1)S(1)}, u32[]{:S(2)}) copy-start(bf16[1024,512]{1,0:T(8,128)(2,1)S(1)} %constant_dynamic-update-slice_fusion.refs_3_) | copy-start | bytes 3145732
  30.4 46.0 %copy-start.7 = (bf16[512,512]{1,0:T(8,128)(2,1)S(1)}, bf16[512,512]{1,0:T(8,128)(2,1)}, u32[]{:S(2)}) copy-start(bf16[512,512]{1,0:T(8,128)(2,1)} %refs_0_.5) | copy-start | bytes 1572868
  30.4 42.1 %copy-start.11 = (bf16[512,512]{1,0:T(8,128)(2,1)}, bf16[512,512]{1,0:T(8,128)(2,1)S(1)}, u32[]{:S(2)}) copy-start(bf16[512,512]{1,0:T(8,128)(2,1)S(1)} %collective-permute-done.1.refs_2_) | copy-start | bytes 1572868
  30.4 36.0 %collective-permute-start.6 = (bf16[1024,512]{1,0:T(8,128)(2,1)S(1)}, bf16[1024,512]{1,0:T(8,128)(2,1)S(1)}, u32[]{:S(2)}, u32[]{:S(2)}) collective-permute-start(bf16[1024,512]{1,0:T(8,128)(2,1)S(1)} %constant_dynamic-update-slice_fusion.refs_3_), channel_id=1, source_target_pairs={{0,1},{1,2},{2,3},{3,0},{4,5},{5,6},{6,7},{7,4},{8,9},{9,10},{10,1... | collective-permute-start | bytes 3145736 | tf_op jit(solution)/shard_map/ppermute | solution.py:36
  33.9 35.0 %collective-permute-start.7 = (bf16[1024,512]{1,0:T(8,128)(2,1)S(1)}, bf16[1024,512]{1,0:T(8,128)(2,1)S(1)}, u32[]{:S(2)}, u32[]{:S(2)}) collective-permute-start(bf16[1024,512]{1,0:T(8,128)(2,1)S(1)} %constant_dynamic-update-slice_fusion.refs_3_), channel_id=1, source_target_pairs={{0,3},{1,0},{2,1},{3,2},{4,7},{5,4},{6,5},{7,6},{8,11},{9,8},{10,9... | collective-permute-start | bytes 3145736 | tf_op jit(solution)/shard_map/ppermute | solution.py:36
  33.9 10.2 %collective-permute-start.8 = (bf16[512,512]{1,0:T(8,128)(2,1)S(1)}, bf16[512,512]{1,0:T(8,128)(2,1)S(1)}, u32[]{:S(2)}, u32[]{:S(2)}) collective-permute-start(bf16[512,512]{1,0:T(8,128)(2,1)S(1)} %collective-permute-done.4), channel_id=1, source_target_pairs={{0,0},{1,1},{2,32},{3,33},{4,4},{5,5},{6,36},{7,37},{8,8},{9,9},{1... | collective-permute-start | bytes 1572872 | tf_op jit(solution)/shard_map/ppermute | solution.py:36
  34.6 9.5 %collective-permute-start.10 = (f32[512,128]{0,1:T(8,128)S(1)}, f32[512,128]{0,1:T(8,128)S(1)}, u32[]{:S(2)}, u32[]{:S(2)}) collective-permute-start(f32[512,128]{0,1:T(8,128)S(1)} %add.335), channel_id=1, source_target_pairs={{0,4},{1,5},{2,6},{3,7},{4,0},{5,1},{6,2},{7,3},{8,12},{9,13},{10,... | collective-permute-start | bytes 786440 | tf_op jit(solution)/shard_map/ppermute | solution.py:36
  36.5 32.4 %collective-permute-start.9 = (bf16[512,512]{1,0:T(8,128)(2,1)S(1)}, bf16[512,512]{1,0:T(8,128)(2,1)S(1)}, u32[]{:S(2)}, u32[]{:S(2)}) collective-permute-start(bf16[512,512]{1,0:T(8,128)(2,1)S(1)} %collective-permute-done.4), channel_id=1, source_target_pairs={{0,32},{1,33},{2,0},{3,1},{4,36},{5,37},{6,4},{7,5},{8,40},{9,41},... | collective-permute-start | bytes 1572872 | tf_op jit(solution)/shard_map/ppermute | solution.py:36
  66.4 36.1 %copy-start.1 = (bf16[1024,512]{1,0:T(8,128)(2,1)}, bf16[1024,512]{1,0:T(8,128)(2,1)S(1)}, u32[]{:S(2)}) copy-start(bf16[1024,512]{1,0:T(8,128)(2,1)S(1)} %collective-permute-done.6.refs_4_) | copy-start | bytes 3145732
  68.9 28.4 %copy-start.10 = (bf16[1024,512]{1,0:T(8,128)(2,1)}, bf16[1024,512]{1,0:T(8,128)(2,1)S(1)}, u32[]{:S(2)}) copy-start(bf16[1024,512]{1,0:T(8,128)(2,1)S(1)} %collective-permute-done.7.refs_5_) | copy-start | bytes 3145732
  68.9 33.8 %collective-permute-start.11 = (bf16[1536,512]{1,0:T(8,128)(2,1)S(1)}, bf16[1536,512]{1,0:T(8,128)(2,1)S(1)}, u32[]{:S(2)}, u32[]{:S(2)}) collective-permute-start(bf16[1536,512]{1,0:T(8,128)(2,1)S(1)} %pad_maximum_fusion.1), channel_id=1, source_target_pairs={{0,1},{1,2},{2,3},{3,0},{4,5},{5,6},{6,7},{7,4},{8,9},{9,10},{10,1... | collective-permute-start | bytes 4718600 | tf_op jit(solution)/shard_map/ppermute | solution.py:36
  72.5 24.8 %copy-start.4 = (bf16[1024,512]{1,0:T(8,128)(2,1)}, bf16[1024,512]{1,0:T(8,128)(2,1)S(1)}, u32[]{:S(2)}) copy-start(bf16[1024,512]{1,0:T(8,128)(2,1)S(1)} %constant_dynamic-update-slice_fusion.2.refs_8_.refs_10_.refs_11_) | copy-start | bytes 3145732
  72.5 24.7 %collective-permute-start.13 = (bf16[1024,512]{1,0:T(8,128)(2,1)S(1)}, bf16[1024,512]{1,0:T(8,128)(2,1)S(1)}, u32[]{:S(2)}, u32[]{:S(2)}) collective-permute-start(bf16[1024,512]{1,0:T(8,128)(2,1)S(1)} %constant_dynamic-update-slice_fusion.2.refs_8_.refs_10_.refs_11_), channel_id=1, source_target_pairs={{0,64},{1,65},{2,66},{3,67},{4,68},{5,69},{6,70},{7,71},{8,72},{9,... | collective-permute-start | bytes 3145736 | tf_op jit(solution)/shard_map/ppermute | solution.py:36
  76.0 24.8 %collective-permute-start.14 = (bf16[1024,512]{1,0:T(8,128)(2,1)S(1)}, bf16[1024,512]{1,0:T(8,128)(2,1)S(1)}, u32[]{:S(2)}, u32[]{:S(2)}) collective-permute-start(bf16[1024,512]{1,0:T(8,128)(2,1)S(1)} %constant_dynamic-update-slice_fusion.2.refs_8_.refs_10_.refs_11_), channel_id=1, source_target_pairs={{0,192},{1,193},{2,194},{3,195},{4,196},{5,197},{6,198},{7,199},{8... | collective-permute-start | bytes 3145736 | tf_op jit(solution)/shard_map/ppermute | solution.py:36
  76.0 19.5 %collective-permute-start.15 = (f32[512,128]{0,1:T(8,128)S(1)}, f32[512,128]{0,1:T(8,128)S(1)}, u32[]{:S(2)}, u32[]{:S(2)}) collective-permute-start(f32[512,128]{0,1:T(8,128)S(1)} %add.336), channel_id=1, source_target_pairs={{0,3},{1,2},{2,1},{3,0},{4,7},{5,6},{6,5},{7,4},{8,11},{9,10},{10,... | collective-permute-start | bytes 786440 | tf_op jit(solution)/shard_map/ppermute | solution.py:36
  76.4 26.3 %collective-permute-start.12 = (bf16[512,512]{1,0:T(8,128)(2,1)S(1)}, bf16[512,512]{1,0:T(8,128)(2,1)S(1)}, u32[]{:S(2)}, u32[]{:S(2)}) collective-permute-start(bf16[512,512]{1,0:T(8,128)(2,1)S(1)} %copy-done.7), channel_id=1, source_target_pairs={{0,8},{1,9},{2,10},{3,11},{4,12},{5,13},{6,14},{7,15},{8,0},{9,1},... | collective-permute-start | bytes 1572872 | tf_op jit(solution)/shard_map/ppermute | solution.py:36
  95.5 13.3 %copy-start.15 = (f32[512,128]{0,1:T(8,128)}, f32[512,128]{0,1:T(8,128)S(1)}, u32[]{:S(2)}) copy-start(f32[512,128]{0,1:T(8,128)S(1)} %add.337) | copy-start | bytes 786436
  97.3 5.7 %copy-start.2 = (bf16[1024,512]{1,0:T(8,128)(2,1)}, bf16[1024,512]{1,0:T(8,128)(2,1)S(1)}, u32[]{:S(2)}) copy-start(bf16[1024,512]{1,0:T(8,128)(2,1)S(1)} %collective-permute-done.13.refs_9_.refs_11_.refs_12_) | copy-start | bytes 3145732
  100.8 2.0 %copy-start.3 = (bf16[1024,512]{1,0:T(8,128)(2,1)}, bf16[1024,512]{1,0:T(8,128)(2,1)S(1)}, u32[]{:S(2)}) copy-start(bf16[1024,512]{1,0:T(8,128)(2,1)S(1)} %collective-permute-done.14.refs_10_.refs_12_.refs_13_) | copy-start | bytes 3145732
  102.7 8.0 %copy-start.12 = (bf16[512,512]{1,0:T(8,128)(2,1)}, bf16[512,512]{1,0:T(8,128)(2,1)S(1)}, u32[]{:S(2)}) copy-start(bf16[512,512]{1,0:T(8,128)(2,1)S(1)} %collective-permute-done.12.refs_7_) | copy-start | bytes 1572868
  102.7 3.6 %copy-start.6 = (bf16[1536,512]{1,0:T(8,128)(2,1)}, bf16[1536,512]{1,0:T(8,128)(2,1)S(1)}, u32[]{:S(2)}) copy-start(bf16[1536,512]{1,0:T(8,128)(2,1)S(1)} %collective-permute-done.11.refs_6_) | copy-start | bytes 4718596
  102.7 19.0 %collective-permute-start.19 = (bf16[3072,512]{1,0:T(8,128)(2,1)}, bf16[3072,512]{1,0:T(8,128)(2,1)}, u32[]{:S(2)}, u32[]{:S(2)}) collective-permute-start(bf16[3072,512]{1,0:T(8,128)(2,1)} %pad_maximum_fusion), channel_id=1, source_target_pairs={{0,16},{1,17},{2,18},{3,19},{4,20},{5,21},{6,22},{7,23},{8,24},{9,... | collective-permute-start | bytes 9437192 | tf_op jit(solution)/shard_map/ppermute | solution.py:36
  103.0 18.7 %collective-permute-start.18 = (bf16[1024,512]{1,0:T(8,128)(2,1)S(1)}, bf16[1024,512]{1,0:T(8,128)(2,1)}, u32[]{:S(2)}, u32[]{:S(2)}) collective-permute-start(bf16[1024,512]{1,0:T(8,128)(2,1)S(1)} %collective-permute-done.13.refs_9_.refs_11_.refs_12_), channel_id=1, source_target_pairs={{0,64},{1,65},{2,66},{3,67},{4,68},{5,69},{6,70},{7,71},{8,72},{9,... | collective-permute-start | bytes 3145736 | tf_op jit(solution)/shard_map/ppermute | solution.py:36
  106.4 15.3 %collective-permute-start.16 = (bf16[512,512]{1,0:T(8,128)(2,1)S(1)}, bf16[512,512]{1,0:T(8,128)(2,1)S(1)}, u32[]{:S(2)}, u32[]{:S(2)}) collective-permute-start(bf16[512,512]{1,0:T(8,128)(2,1)S(1)} %collective-permute-done.12.refs_7_), channel_id=1, source_target_pairs={{0,1},{1,2},{2,3},{3,0},{4,5},{5,6},{6,7},{7,4},{8,9},{9,10},{10,1... | collective-permute-start | bytes 1572872 | tf_op jit(solution)/shard_map/ppermute | solution.py:36
  107.5 14.2 %collective-permute-start.17 = (bf16[512,512]{1,0:T(8,128)(2,1)S(1)}, bf16[512,512]{1,0:T(8,128)(2,1)}, u32[]{:S(2)}, u32[]{:S(2)}) collective-permute-start(bf16[512,512]{1,0:T(8,128)(2,1)S(1)} %collective-permute-done.12.refs_7_), channel_id=1, source_target_pairs={{0,3},{1,0},{2,1},{3,2},{4,7},{5,4},{6,5},{7,6},{8,11},{9,8},{10,9... | collective-permute-start | bytes 1572872 | tf_op jit(solution)/shard_map/ppermute | solution.py:36
  108.8 14.9 %copy-start.8 = (bf16[512,512]{1,0:T(8,128)(2,1)S(1)}, bf16[512,512]{1,0:T(8,128)(2,1)}, u32[]{:S(2)}) copy-start(bf16[512,512]{1,0:T(8,128)(2,1)} %refs_0_.5) | copy-start | bytes 1572868
  108.8 18.4 %copy-start.18 = (bf16[1,64,512]{2,1,0:T(8,128)(2,1)S(1)}, bf16[1,64,512]{2,1,0:T(8,128)(2,1)}, u32[]{:S(2)}) copy-start(bf16[1,64,512]{2,1,0:T(8,128)(2,1)} %param.9) | copy-start | bytes 196612
  108.8 12.8 %collective-permute-start.20 = (f32[512,128]{0,1:T(8,128)S(1)}, f32[512,128]{0,1:T(8,128)S(1)}, u32[]{:S(2)}, u32[]{:S(2)}) collective-permute-start(f32[512,128]{0,1:T(8,128)S(1)} %add.337), channel_id=1, source_target_pairs={{0,8},{1,9},{2,10},{3,11},{4,12},{5,13},{6,14},{7,15},{8,0},{9,1},... | collective-permute-start | bytes 786440 | tf_op jit(solution)/shard_map/ppermute | solution.py:36
  110.7 10.9 %copy-start.16 = (f32[512,128]{0,1:T(8,128)S(1)}, f32[512,128]{0,1:T(8,128)}, u32[]{:S(2)}) copy-start(f32[512,128]{0,1:T(8,128)} %copy-done.15) | copy-start | bytes 786436
  121.6 7.2 %copy-start.13 = (bf16[512,512]{1,0:T(8,128)(2,1)}, bf16[512,512]{1,0:T(8,128)(2,1)S(1)}, u32[]{:S(2)}) copy-start(bf16[512,512]{1,0:T(8,128)(2,1)S(1)} %collective-permute-done.16.refs_8_) | copy-start | bytes 1572868
  121.7 14.7 %collective-permute-start.22 = (bf16[1024,512]{1,0:T(8,128)(2,1)}, bf16[1024,512]{1,0:T(8,128)(2,1)S(1)}, u32[]{:S(2)}, u32[]{:S(2)}) collective-permute-start(bf16[1024,512]{1,0:T(8,128)(2,1)} %collective-permute-done.18.refs_14_.refs_15_), channel_id=1, source_target_pairs={{0,16},{1,17},{2,18},{3,19},{4,20},{5,21},{6,22},{7,23},{8,24},{9,... | collective-permute-start | bytes 3145736 | tf_op jit(solution)/shard_map/ppermute | solution.py:36
  124.8 11.6 %collective-permute-start.21 = (bf16[512,512]{1,0:T(8,128)(2,1)S(1)}, bf16[512,512]{1,0:T(8,128)(2,1)S(1)}, u32[]{:S(2)}, u32[]{:S(2)}) collective-permute-start(bf16[512,512]{1,0:T(8,128)(2,1)S(1)} %collective-permute-done.16.refs_8_), channel_id=1, source_target_pairs={{0,1},{1,2},{2,3},{3,0},{4,5},{5,6},{6,7},{7,4},{8,9},{9,10},{10,1... | collective-permute-start | bytes 1572872 | tf_op jit(solution)/shard_map/ppermute | solution.py:36
  136.4 0.8 copy-start.17
  137.2 1.0 copy-start.14

commit v4 on v3

--- a/solution.py
+++ b/solution.py
@@ -14,8 +14,11 @@
 DIM = 512
 VMEM = 56 * 1024 * 1024
 ORDER = (
-    "a A0 B0 Z1 Z3 Ry1:A0 | b0 b1 +Z A13 B13 Rz1 | +X XA XB Z2 +F F013 Ry3 | "
-    "XF A2 B2 +S S1 Rz2 | F2 SF"
+    ("a", "A0", "B0", "Z1", "Z3", "Ry1:A0"),
+    ("b0", "b1", "+Z", "A13", "B13", "Rz1"),
+    ("+X", "XA", "XB", "Z2", "+F", "F013", "Ry3"),
+    ("XF", "A2", "B2", "+S", "S1", "Rz2"),
+    ("F2", "SF"),
 )
 HELD = {"G": 0, "A0": 1, "B0": 1, "+Z": 1, "A13": 2, "B13": 2, "F013": 3, "Z2": 3, "A2": 4, "B2": 4, "F2": 5}
 WEIGHTS = {"+X": 2, "XA": 3, "XB": 3, "S1": 4, "XF": 4, "SF": 5}
@@ -243,16 +246,14 @@
         return adapter_part, down_gradient, up_gradient
 
     before, beside = [], []
-    for number, group in enumerate(ORDER.split("|"), 1):
+    for number, group in enumerate(ORDER, 1):
         names = []
-        for entry in group.split():
-            name, mark, waits = entry.replace("=", ":=").partition(":")
+        for entry in group:
+            name, _, waits = entry.partition(":")
             takes, act = steps[name]
             given = [value[n] for n in takes]
             if name[0] != "+":
-                ahead = [] if waits[:1] == "=" else before
-                ahead = ahead + [value[n] for n in waits.strip("=").split(",") if n]
-                given[0] = after(given[0], *ahead) if ahead else given[0]
+                given[0] = after(given[0], *before, *[value[n] for n in waits.split(",") if n])
                 names.append(name)
             value[name] = act(*given)
         before, beside = [value[n] for n in names] + beside, []

time: 144 us -> 144 us (level)
  no operation moved by 1% of the time
where the time goes in v4:
time: 144 us; the launch traced here: 143 us
  waiting for transfers between devices  67 us (47%)
  starting transfers between devices  43.8 us (30%)
  Pallas kernels  18.7 us (13%)
  matrix products  6.27 us (4%)
  other arithmetic  3.59 us (2%)
  local copies, waits for them, and re-layouts  2.31 us (2%)
  between operations  1.81 us (1%)
    ppermute x23, waiting for transfers between devices, send(): return lax.ppermute(value, AXES, moves(target))  67 us
    ppermute x23, starting transfers between devices, send(): return lax.ppermute(value, AXES, moves(target))  43.8 us
    pallas_call x3, Pallas kernels, partial_sum(): pl.pallas_call(functools.partial(product_kernel, pairs, len(g_names), len...  18.7 us
  transfers between devices with their start and end apart: 23, of which 8 were waited for; matrix products, arithmetic and copies ran while one was open for 7% of the time, Pallas kernels for 9%

profile of v4, /device:TPU:1, one launch (start us, length us, event | category | flops | bytes accessed | tf_op | source)
XLA Modules:
  0.0 143.5 jit_solution(6093922756866457386)
XLA Ops:
  0.6 0.0 copy-start
  0.6 3.6 %collective-permute-start = (bf16[512,512]{1,0:T(8,128)(2,1)}, bf16[512,512]{1,0:T(8,128)(2,1)S(1)}, u32[]{:S(2)}, u32[]{:S(2)}) collective-permute-start(bf16[512,512]{1,0:T(8,128)(2,1)} %refs_0_.5), channel_id=1, source_target_pairs={{0,1},{1,2},{2,3},{3,0},{4,5},{5,6},{6,7},{7,4},{8,9},{9,10},{10,1... | collective-permute-start | bytes 1572872 | tf_op jit(solution)/shard_map/ppermute | solution.py:39
  4.3 0.0 collective-permute-start.1
  4.3 1.6 %collective-permute-start.2 = (bf16[512,512]{1,0:T(8,128)(2,1)}, bf16[512,512]{1,0:T(8,128)(2,1)S(1)}, u32[]{:S(2)}, u32[]{:S(2)}) collective-permute-start(bf16[512,512]{1,0:T(8,128)(2,1)} %refs_0_.5), channel_id=1, source_target_pairs={{0,4},{1,5},{2,6},{3,7},{4,8},{5,9},{6,10},{7,11},{8,12},{9,13},{1... | collective-permute-start | bytes 1572872 | tf_op jit(solution)/shard_map/ppermute | solution.py:39
  5.9 2.7 %collective-permute-start.3 = (bf16[512,512]{1,0:T(8,128)(2,1)}, bf16[512,512]{1,0:T(8,128)(2,1)S(1)}, u32[]{:S(2)}, u32[]{:S(2)}) collective-permute-start(bf16[512,512]{1,0:T(8,128)(2,1)} %refs_0_.5), channel_id=1, source_target_pairs={{0,12},{1,13},{2,14},{3,15},{4,0},{5,1},{6,2},{7,3},{8,4},{9,5},{1... | collective-permute-start | bytes 1572872 | tf_op jit(solution)/shard_map/ppermute | solution.py:39
  8.6 3.3 %collective-permute-start.4 = (bf16[512,512]{1,0:T(8,128)(2,1)}, bf16[512,512]{1,0:T(8,128)(2,1)S(1)}, u32[]{:S(2)}, u32[]{:S(2)}) collective-permute-start(bf16[512,512]{1,0:T(8,128)(2,1)} %param.8), channel_id=1, source_target_pairs={{0,0},{1,16},{2,2},{3,18},{4,196},{5,84},{6,198},{7,86},{8,136},{9... | collective-permute-start | bytes 1572872 | tf_op jit(solution)/shard_map/ppermute | solution.py:39
  12.6 1.4 fusion.3
  14.0 1.1 fusion.12
  15.2 0.0 collective-permute-done.refs_1_
  15.2 0.1 collective-permute-start.5
  15.3 3.9 %collective-permute-done.2 = bf16[512,512]{1,0:T(8,128)(2,1)S(1)} collective-permute-done((bf16[512,512]{1,0:T(8,128)(2,1)}, bf16[512,512]{1,0:T(8,128)(2,1)S(1)}, u32[]{:S(2)}, u32[]{:S(2)}) %collective-permute-start.2) | collective-permute-done | bytes 524320 | tf_op jit(solution)/shard_map/ppermute | solution.py:39
  19.2 11.0 %collective-permute-done.3 = bf16[512,512]{1,0:T(8,128)(2,1)S(1)} collective-permute-done((bf16[512,512]{1,0:T(8,128)(2,1)}, bf16[512,512]{1,0:T(8,128)(2,1)S(1)}, u32[]{:S(2)}, u32[]{:S(2)}) %collective-permute-start.3) | collective-permute-done | bytes 524320 | tf_op jit(solution)/shard_map/ppermute | solution.py:39
  30.3 0.0 collective-permute-done.5
  30.4 0.0 copy-start.7
  30.4 0.0 collective-permute-done.1.refs_2_
  30.4 0.0 collective-permute-done.4
  30.4 3.5 %collective-permute-start.6 = (bf16[1024,512]{1,0:T(8,128)(2,1)S(1)}, bf16[1024,512]{1,0:T(8,128)(2,1)S(1)}, u32[]{:S(2)}, u32[]{:S(2)}) collective-permute-start(bf16[1024,512]{1,0:T(8,128)(2,1)S(1)} %constant_dynamic-update-slice_fusion.refs_3_), channel_id=1, source_target_pairs={{0,1},{1,2},{2,3},{3,0},{4,5},{5,6},{6,7},{7,4},{8,9},{9,10},{10,1... | collective-permute-start | bytes 3145736 | tf_op jit(solution)/shard_map/ppermute | solution.py:39
  33.9 0.0 collective-permute-start.7
  33.9 0.7 collective-permute-start.8
  34.6 1.9 %collective-permute-start.10 = (f32[512,128]{0,1:T(8,128)S(1)}, f32[512,128]{0,1:T(8,128)S(1)}, u32[]{:S(2)}, u32[]{:S(2)}) collective-permute-start(f32[512,128]{0,1:T(8,128)S(1)} %add.335), channel_id=1, source_target_pairs={{0,4},{1,5},{2,6},{3,7},{4,0},{5,1},{6,2},{7,3},{8,12},{9,13},{10,... | collective-permute-start | bytes 786440 | tf_op jit(solution)/shard_map/ppermute | solution.py:39
  36.5 7.6 %collective-permute-start.9 = (bf16[512,512]{1,0:T(8,128)(2,1)S(1)}, bf16[512,512]{1,0:T(8,128)(2,1)S(1)}, u32[]{:S(2)}, u32[]{:S(2)}) collective-permute-start(bf16[512,512]{1,0:T(8,128)(2,1)S(1)} %collective-permute-done.4), channel_id=1, source_target_pairs={{0,32},{1,33},{2,0},{3,1},{4,36},{5,37},{6,4},{7,5},{8,40},{9,41},... | collective-permute-start | bytes 1572872 | tf_op jit(solution)/shard_map/ppermute | solution.py:39
  44.1 0.0 collective-permute-done.10
  44.1 0.0 collective-permute-done.8
  44.2 22.3 %collective-permute-done.6.refs_4_ = bf16[1024,512]{1,0:T(8,128)(2,1)S(1)} collective-permute-done((bf16[1024,512]{1,0:T(8,128)(2,1)S(1)}, bf16[1024,512]{1,0:T(8,128)(2,1)S(1)}, u32[]{:S(2)}, u32[]{:S(2)}) %collective-permute-start.6) | collective-permute-done | bytes 1048608 | tf_op jit(solution)/shard_map/ppermute | solution.py:39
  66.4 0.1 pad_maximum_fusion.1
  66.6 2.3 %collective-permute-done.9 = bf16[512,512]{1,0:T(8,128)(2,1)S(1)} collective-permute-done((bf16[512,512]{1,0:T(8,128)(2,1)S(1)}, bf16[512,512]{1,0:T(8,128)(2,1)S(1)}, u32[]{:S(2)}, u32[]{:S(2)}) %collective-permute-start.9) | collective-permute-done | bytes 524320 | tf_op jit(solution)/shard_map/ppermute | solution.py:39
  68.9 0.0 collective-permute-done.7.refs_5_
  68.9 3.6 %collective-permute-start.11 = (bf16[1536,512]{1,0:T(8,128)(2,1)S(1)}, bf16[1536,512]{1,0:T(8,128)(2,1)S(1)}, u32[]{:S(2)}, u32[]{:S(2)}) collective-permute-start(bf16[1536,512]{1,0:T(8,128)(2,1)S(1)} %pad_maximum_fusion.1), channel_id=1, source_target_pairs={{0,1},{1,2},{2,3},{3,0},{4,5},{5,6},{6,7},{7,4},{8,9},{9,10},{10,1... | collective-permute-start | bytes 4718600 | tf_op jit(solution)/shard_map/ppermute | solution.py:39
  72.5 3.4 %collective-permute-start.13 = (bf16[1024,512]{1,0:T(8,128)(2,1)S(1)}, bf16[1024,512]{1,0:T(8,128)(2,1)S(1)}, u32[]{:S(2)}, u32[]{:S(2)}) collective-permute-start(bf16[1024,512]{1,0:T(8,128)(2,1)S(1)} %constant_dynamic-update-slice_fusion.2.refs_8_.refs_10_.refs_11_), channel_id=1, source_target_pairs={{0,64},{1,65},{2,66},{3,67},{4,68},{5,69},{6,70},{7,71},{8,72},{9,... | collective-permute-start | bytes 3145736 | tf_op jit(solution)/shard_map/ppermute | solution.py:39
  76.0 0.0 collective-permute-start.14
  76.0 0.4 collective-permute-start.15
  76.4 1.7 %collective-permute-start.12 = (bf16[512,512]{1,0:T(8,128)(2,1)S(1)}, bf16[512,512]{1,0:T(8,128)(2,1)S(1)}, u32[]{:S(2)}, u32[]{:S(2)}) collective-permute-start(bf16[512,512]{1,0:T(8,128)(2,1)S(1)} %copy-done.7), channel_id=1, source_target_pairs={{0,8},{1,9},{2,10},{3,11},{4,12},{5,13},{6,14},{7,15},{8,0},{9,1},... | collective-permute-start | bytes 1572872 | tf_op jit(solution)/shard_map/ppermute | solution.py:39
  78.2 17.3 %collective-permute-done.15 = f32[512,128]{0,1:T(8,128)S(1)} collective-permute-done((f32[512,128]{0,1:T(8,128)S(1)}, f32[512,128]{0,1:T(8,128)S(1)}, u32[]{:S(2)}, u32[]{:S(2)}) %collective-permute-start.15) | collective-permute-done | bytes 262176 | tf_op jit(solution)/shard_map/ppermute | solution.py:39
  95.5 0.0 copy-start.15
  95.5 1.8 %collective-permute-done.13.refs_9_.refs_11_.refs_12_ = bf16[1024,512]{1,0:T(8,128)(2,1)S(1)} collective-permute-done((bf16[1024,512]{1,0:T(8,128)(2,1)S(1)}, bf16[1024,512]{1,0:T(8,128)(2,1)S(1)}, u32[]{:S(2)}, u32[]{:S(2)}) %collective-permute-start.13) | collective-permute-done | bytes 1048608 | tf_op jit(solution)/shard_map/ppermute | solution.py:39
  97.3 3.5 %collective-permute-done.14.refs_10_.refs_12_.refs_13_ = bf16[1024,512]{1,0:T(8,128)(2,1)S(1)} collective-permute-done((bf16[1024,512]{1,0:T(8,128)(2,1)S(1)}, bf16[1024,512]{1,0:T(8,128)(2,1)S(1)}, u32[]{:S(2)}, u32[]{:S(2)}) %collective-permute-start.14) | collective-permute-done | bytes 1048608 | tf_op jit(solution)/shard_map/ppermute | solution.py:39
  100.8 1.8 %pad_maximum_fusion = bf16[3072,512]{1,0:T(8,128)(2,1)} fusion(bf16[1024,512]{1,0:T(8,128)(2,1)S(1)} %collective-permute-done.14.refs_10_.refs_12_.refs_13_, bf16[1024,512]{1,0:T(8,128)(2,1)S(1)} %collective-permute-done.13.refs_9_.refs_11_.refs_12_, bf16[512,512]{1,0:T(8,128)(2,1)S(1)} %collective-permute-done.9, bf16[512,512]{1,0:T(8,128)(2,1)S(1)} %collective-permute-done.8), kind=kLoop, calls=%fused_computation | loop fusion | flops 12582912 | bytes 6291456 | tf_op jit(solution)/shard_map/concatenate | solution.py:161
  102.6 0.1 copy-done.3
  102.7 0.0 collective-permute-done.12.refs_7_
  102.7 0.0 collective-permute-done.11.refs_6_
  102.7 0.2 collective-permute-start.19
  103.0 3.4 %collective-permute-start.18 = (bf16[1024,512]{1,0:T(8,128)(2,1)S(1)}, bf16[1024,512]{1,0:T(8,128)(2,1)}, u32[]{:S(2)}, u32[]{:S(2)}) collective-permute-start(bf16[1024,512]{1,0:T(8,128)(2,1)S(1)} %collective-permute-done.13.refs_9_.refs_11_.refs_12_), channel_id=1, source_target_pairs={{0,64},{1,65},{2,66},{3,67},{4,68},{5,69},{6,70},{7,71},{8,72},{9,... | collective-permute-start | bytes 3145736 | tf_op jit(solution)/shard_map/ppermute | solution.py:39
  106.4 1.2 collective-permute-start.16
  107.5 0.3 collective-permute-start.17
  107.8 0.1 stack.118
  107.9 0.1 stack.135
  108.0 0.8 select_reduce_fusion.which_ref
  108.8 1.9 %collective-permute-start.20 = (f32[512,128]{0,1:T(8,128)S(1)}, f32[512,128]{0,1:T(8,128)S(1)}, u32[]{:S(2)}, u32[]{:S(2)}) collective-permute-start(f32[512,128]{0,1:T(8,128)S(1)} %add.337), channel_id=1, source_target_pairs={{0,8},{1,9},{2,10},{3,11},{4,12},{5,13},{6,14},{7,15},{8,0},{9,1},... | collective-permute-start | bytes 786440 | tf_op jit(solution)/shard_map/ppermute | solution.py:39
  110.7 6.0 %shard_map.85.refs_15_ = f32[512,512]{1,0:T(8,128)} custom-call(s32[16]{0:T(128)} %select_reduce_fusion.which_ref, bf16[512,512]{1,0:T(8,128)(2,1)} %refs_0_.5, bf16[512,512]{1,0:T(8,128)(2,1)} %copy-done.9, bf16[512,512]{1,0:T(8,128)(2,1)} %copy-done.11, bf16[1024,512]{1,0:T(8,128)(2,1)} %copy-done.5, bf16[1024,512]{1,0:T(8,128)(2,1)} %copy-done.1, ...), custom_call_target="tpu_custom_call" | custom-call | flops 4294967296 | bytes 16777216 | tf_op jit(solution)/shard_map/pallas_call | solution.py:118
  116.7 4.9 %collective-permute-done.20 = f32[512,128]{0,1:T(8,128)S(1)} collective-permute-done((f32[512,128]{0,1:T(8,128)S(1)}, f32[512,128]{0,1:T(8,128)S(1)}, u32[]{:S(2)}, u32[]{:S(2)}) %collective-permute-start.20) | collective-permute-done | bytes 262176 | tf_op jit(solution)/shard_map/ppermute | solution.py:39
  121.6 0.0 collective-permute-done.16.refs_8_
  121.7 0.0 collective-permute-done.17.refs_9_
  121.7 0.0 collective-permute-done.18.refs_14_.refs_15_
  121.7 0.0 collective-permute-done.19.refs_13_.refs_14_
  121.7 1.2 collective-permute-start.22
  122.9 0.7 fusion.7.refs_18_
  123.7 1.1 fusion
  124.8 1.4 collective-permute-start.21
  126.2 1.0 fusion.1
  127.2 1.6 %fusion.9.refs_19_ = f32[512,512]{1,0:T(8,128)} fusion(f32[512,128]{0,1:T(8,128)S(1)} %add.338, bf16[1,64,512]{2,1,0:T(8,128)(2,1)S(1)} %copy-done.18), kind=kOutput, calls=%fused_computation.16 | convolution fusion | flops 201359360 | bytes 1245184 | tf_op jit(solution)/shard_map/dot_general | solution.py:235
  128.8 7.6 %shard_map.86.refs_17_ = f32[512,512]{1,0:T(8,128)} custom-call(s32[16]{0:T(128)} %select_reduce_fusion.which_ref, bf16[512,512]{1,0:T(8,128)(2,1)} %refs_0_.5, bf16[512,512]{1,0:T(8,128)(2,1)} %copy-done.9, bf16[512,512]{1,0:T(8,128)(2,1)} %copy-done.11, bf16[1024,512]{1,0:T(8,128)(2,1)} %copy-done.5, bf16[1024,512]{1,0:T(8,128)(2,1)} %copy-done.1, ...), custom_call_target="tpu_custom_call" | custom-call | flops 2147483648 | bytes 8388608 | tf_op jit(solution)/shard_map/pallas_call | solution.py:118
  136.4 0.8 copy-done.17
  137.2 1.0 copy-done.14
  138.2 5.1 %shard_map.87 = bf16[512,512]{1,0:T(8,128)(2,1)} custom-call(s32[16]{0:T(128)} %select_reduce_fusion.which_ref, bf16[512,512]{1,0:T(8,128)(2,1)} %refs_0_.5, bf16[512,512]{1,0:T(8,128)(2,1)} %copy-done.9, bf16[512,512]{1,0:T(8,128)(2,1)} %copy-done.11, bf16[1024,512]{1,0:T(8,128)(2,1)} %copy-done.5, bf16[1024,512]{1,0:T(8,128)(2,1)} %copy-done.1, ...), custom_call_target="tpu_custom_call" | custom-call | flops 2147483648 | bytes 8388608 | tf_op jit(solution)/shard_map/pallas_call | solution.py:118
  (44 shorter events, 0.4 us)
Async XLA Ops:
  0.6 13.4 %copy-start = (bf16[512,512]{1,0:T(8,128)(2,1)S(1)}, bf16[512,512]{1,0:T(8,128)(2,1)}, u32[]{:S(2)}) copy-start(bf16[512,512]{1,0:T(8,128)(2,1)} %param.6) | copy-start | bytes 1572868
  0.6 14.5 %collective-permute-start = (bf16[512,512]{1,0:T(8,128)(2,1)}, bf16[512,512]{1,0:T(8,128)(2,1)S(1)}, u32[]{:S(2)}, u32[]{:S(2)}) collective-permute-start(bf16[512,512]{1,0:T(8,128)(2,1)} %refs_0_.5), channel_id=1, source_target_pairs={{0,1},{1,2},{2,3},{3,0},{4,5},{5,6},{6,7},{7,4},{8,9},{9,10},{10,1... | collective-permute-start | bytes 1572872 | tf_op jit(solution)/shard_map/ppermute | solution.py:39
  4.3 26.1 %collective-permute-start.1 = (bf16[512,512]{1,0:T(8,128)(2,1)}, bf16[512,512]{1,0:T(8,128)(2,1)S(1)}, u32[]{:S(2)}, u32[]{:S(2)}) collective-permute-start(bf16[512,512]{1,0:T(8,128)(2,1)} %refs_0_.5), channel_id=1, source_target_pairs={{0,3},{1,0},{2,1},{3,2},{4,7},{5,4},{6,5},{7,6},{8,11},{9,8},{10,9... | collective-permute-start | bytes 1572872 | tf_op jit(solution)/shard_map/ppermute | solution.py:39
  4.3 14.9 %collective-permute-start.2 = (bf16[512,512]{1,0:T(8,128)(2,1)}, bf16[512,512]{1,0:T(8,128)(2,1)S(1)}, u32[]{:S(2)}, u32[]{:S(2)}) collective-permute-start(bf16[512,512]{1,0:T(8,128)(2,1)} %refs_0_.5), channel_id=1, source_target_pairs={{0,4},{1,5},{2,6},{3,7},{4,8},{5,9},{6,10},{7,11},{8,12},{9,13},{1... | collective-permute-start | bytes 1572872 | tf_op jit(solution)/shard_map/ppermute | solution.py:39
  5.9 24.3 %collective-permute-start.3 = (bf16[512,512]{1,0:T(8,128)(2,1)}, bf16[512,512]{1,0:T(8,128)(2,1)S(1)}, u32[]{:S(2)}, u32[]{:S(2)}) collective-permute-start(bf16[512,512]{1,0:T(8,128)(2,1)} %refs_0_.5), channel_id=1, source_target_pairs={{0,12},{1,13},{2,14},{3,15},{4,0},{5,1},{6,2},{7,3},{8,4},{9,5},{1... | collective-permute-start | bytes 1572872 | tf_op jit(solution)/shard_map/ppermute | solution.py:39
  8.6 21.8 %collective-permute-start.4 = (bf16[512,512]{1,0:T(8,128)(2,1)}, bf16[512,512]{1,0:T(8,128)(2,1)S(1)}, u32[]{:S(2)}, u32[]{:S(2)}) collective-permute-start(bf16[512,512]{1,0:T(8,128)(2,1)} %param.8), channel_id=1, source_target_pairs={{0,0},{1,16},{2,2},{3,18},{4,196},{5,84},{6,198},{7,86},{8,136},{9... | collective-permute-start | bytes 1572872 | tf_op jit(solution)/shard_map/ppermute | solution.py:39
  15.2 51.4 %copy-start.9 = (bf16[512,512]{1,0:T(8,128)(2,1)}, bf16[512,512]{1,0:T(8,128)(2,1)S(1)}, u32[]{:S(2)}) copy-start(bf16[512,512]{1,0:T(8,128)(2,1)S(1)} %collective-permute-done.refs_1_) | copy-start | bytes 1572868
  15.2 15.1 %collective-permute-start.5 = (f32[512,128]{0,1:T(8,128)S(1)}, f32[512,128]{0,1:T(8,128)S(1)}, u32[]{:S(2)}, u32[]{:S(2)}) collective-permute-start(f32[512,128]{0,1:T(8,128)S(1)} %pad_maximum_fusion.2), channel_id=1, source_target_pairs={{0,1},{1,0},{2,3},{3,2},{4,5},{5,4},{6,7},{7,6},{8,9},{9,8},{10,11... | collective-permute-start | bytes 786440 | tf_op jit(solution)/shard_map/ppermute | solution.py:39
  30.3 42.2 %copy-start.5 = (bf16[1024,512]{1,0:T(8,128)(2,1)}, bf16[1024,512]{1,0:T(8,128)(2,1)S(1)}, u32[]{:S(2)}) copy-start(bf16[1024,512]{1,0:T(8,128)(2,1)S(1)} %constant_dynamic-update-slice_fusion.refs_3_) | copy-start | bytes 3145732
  30.4 46.0 %copy-start.7 = (bf16[512,512]{1,0:T(8,128)(2,1)S(1)}, bf16[512,512]{1,0:T(8,128)(2,1)}, u32[]{:S(2)}) copy-start(bf16[512,512]{1,0:T(8,128)(2,1)} %refs_0_.5) | copy-start | bytes 1572868
  30.4 42.1 %copy-start.11 = (bf16[512,512]{1,0:T(8,128)(2,1)}, bf16[512,512]{1,0:T(8,128)(2,1)S(1)}, u32[]{:S(2)}) copy-start(bf16[512,512]{1,0:T(8,128)(2,1)S(1)} %collective-permute-done.1.refs_2_) | copy-start | bytes 1572868
  30.4 36.0 %collective-permute-start.6 = (bf16[1024,512]{1,0:T(8,128)(2,1)S(1)}, bf16[1024,512]{1,0:T(8,128)(2,1)S(1)}, u32[]{:S(2)}, u32[]{:S(2)}) collective-permute-start(bf16[1024,512]{1,0:T(8,128)(2,1)S(1)} %constant_dynamic-update-slice_fusion.refs_3_), channel_id=1, source_target_pairs={{0,1},{1,2},{2,3},{3,0},{4,5},{5,6},{6,7},{7,4},{8,9},{9,10},{10,1... | collective-permute-start | bytes 3145736 | tf_op jit(solution)/shard_map/ppermute | solution.py:39
  33.9 35.0 %collective-permute-start.7 = (bf16[1024,512]{1,0:T(8,128)(2,1)S(1)}, bf16[1024,512]{1,0:T(8,128)(2,1)S(1)}, u32[]{:S(2)}, u32[]{:S(2)}) collective-permute-start(bf16[1024,512]{1,0:T(8,128)(2,1)S(1)} %constant_dynamic-update-slice_fusion.refs_3_), channel_id=1, source_target_pairs={{0,3},{1,0},{2,1},{3,2},{4,7},{5,4},{6,5},{7,6},{8,11},{9,8},{10,9... | collective-permute-start | bytes 3145736 | tf_op jit(solution)/shard_map/ppermute | solution.py:39
  33.9 10.2 %collective-permute-start.8 = (bf16[512,512]{1,0:T(8,128)(2,1)S(1)}, bf16[512,512]{1,0:T(8,128)(2,1)S(1)}, u32[]{:S(2)}, u32[]{:S(2)}) collective-permute-start(bf16[512,512]{1,0:T(8,128)(2,1)S(1)} %collective-permute-done.4), channel_id=1, source_target_pairs={{0,0},{1,1},{2,32},{3,33},{4,4},{5,5},{6,36},{7,37},{8,8},{9,9},{1... | collective-permute-start | bytes 1572872 | tf_op jit(solution)/shard_map/ppermute | solution.py:39
  34.6 9.5 %collective-permute-start.10 = (f32[512,128]{0,1:T(8,128)S(1)}, f32[512,128]{0,1:T(8,128)S(1)}, u32[]{:S(2)}, u32[]{:S(2)}) collective-permute-start(f32[512,128]{0,1:T(8,128)S(1)} %add.335), channel_id=1, source_target_pairs={{0,4},{1,5},{2,6},{3,7},{4,0},{5,1},{6,2},{7,3},{8,12},{9,13},{10,... | collective-permute-start | bytes 786440 | tf_op jit(solution)/shard_map/ppermute | solution.py:39
  36.5 32.4 %collective-permute-start.9 = (bf16[512,512]{1,0:T(8,128)(2,1)S(1)}, bf16[512,512]{1,0:T(8,128)(2,1)S(1)}, u32[]{:S(2)}, u32[]{:S(2)}) collective-permute-start(bf16[512,512]{1,0:T(8,128)(2,1)S(1)} %collective-permute-done.4), channel_id=1, source_target_pairs={{0,32},{1,33},{2,0},{3,1},{4,36},{5,37},{6,4},{7,5},{8,40},{9,41},... | collective-permute-start | bytes 1572872 | tf_op jit(solution)/shard_map/ppermute | solution.py:39
  66.4 36.1 %copy-start.1 = (bf16[1024,512]{1,0:T(8,128)(2,1)}, bf16[1024,512]{1,0:T(8,128)(2,1)S(1)}, u32[]{:S(2)}) copy-start(bf16[1024,512]{1,0:T(8,128)(2,1)S(1)} %collective-permute-done.6.refs_4_) | copy-start | bytes 3145732
  68.9 28.4 %copy-start.10 = (bf16[1024,512]{1,0:T(8,128)(2,1)}, bf16[1024,512]{1,0:T(8,128)(2,1)S(1)}, u32[]{:S(2)}) copy-start(bf16[1024,512]{1,0:T(8,128)(2,1)S(1)} %collective-permute-done.7.refs_5_) | copy-start | bytes 3145732
  68.9 33.8 %collective-permute-start.11 = (bf16[1536,512]{1,0:T(8,128)(2,1)S(1)}, bf16[1536,512]{1,0:T(8,128)(2,1)S(1)}, u32[]{:S(2)}, u32[]{:S(2)}) collective-permute-start(bf16[1536,512]{1,0:T(8,128)(2,1)S(1)} %pad_maximum_fusion.1), channel_id=1, source_target_pairs={{0,1},{1,2},{2,3},{3,0},{4,5},{5,6},{6,7},{7,4},{8,9},{9,10},{10,1... | collective-permute-start | bytes 4718600 | tf_op jit(solution)/shard_map/ppermute | solution.py:39
  72.5 24.8 %copy-start.4 = (bf16[1024,512]{1,0:T(8,128)(2,1)}, bf16[1024,512]{1,0:T(8,128)(2,1)S(1)}, u32[]{:S(2)}) copy-start(bf16[1024,512]{1,0:T(8,128)(2,1)S(1)} %constant_dynamic-update-slice_fusion.2.refs_8_.refs_10_.refs_11_) | copy-start | bytes 3145732
  72.5 24.7 %collective-permute-start.13 = (bf16[1024,512]{1,0:T(8,128)(2,1)S(1)}, bf16[1024,512]{1,0:T(8,128)(2,1)S(1)}, u32[]{:S(2)}, u32[]{:S(2)}) collective-permute-start(bf16[1024,512]{1,0:T(8,128)(2,1)S(1)} %constant_dynamic-update-slice_fusion.2.refs_8_.refs_10_.refs_11_), channel_id=1, source_target_pairs={{0,64},{1,65},{2,66},{3,67},{4,68},{5,69},{6,70},{7,71},{8,72},{9,... | collective-permute-start | bytes 3145736 | tf_op jit(solution)/shard_map/ppermute | solution.py:39
  76.0 24.8 %collective-permute-start.14 = (bf16[1024,512]{1,0:T(8,128)(2,1)S(1)}, bf16[1024,512]{1,0:T(8,128)(2,1)S(1)}, u32[]{:S(2)}, u32[]{:S(2)}) collective-permute-start(bf16[1024,512]{1,0:T(8,128)(2,1)S(1)} %constant_dynamic-update-slice_fusion.2.refs_8_.refs_10_.refs_11_), channel_id=1, source_target_pairs={{0,192},{1,193},{2,194},{3,195},{4,196},{5,197},{6,198},{7,199},{8... | collective-permute-start | bytes 3145736 | tf_op jit(solution)/shard_map/ppermute | solution.py:39
  76.0 19.5 %collective-permute-start.15 = (f32[512,128]{0,1:T(8,128)S(1)}, f32[512,128]{0,1:T(8,128)S(1)}, u32[]{:S(2)}, u32[]{:S(2)}) collective-permute-start(f32[512,128]{0,1:T(8,128)S(1)} %add.336), channel_id=1, source_target_pairs={{0,3},{1,2},{2,1},{3,0},{4,7},{5,6},{6,5},{7,4},{8,11},{9,10},{10,... | collective-permute-start | bytes 786440 | tf_op jit(solution)/shard_map/ppermute | solution.py:39
  76.4 26.3 %collective-permute-start.12 = (bf16[512,512]{1,0:T(8,128)(2,1)S(1)}, bf16[512,512]{1,0:T(8,128)(2,1)S(1)}, u32[]{:S(2)}, u32[]{:S(2)}) collective-permute-start(bf16[512,512]{1,0:T(8,128)(2,1)S(1)} %copy-done.7), channel_id=1, source_target_pairs={{0,8},{1,9},{2,10},{3,11},{4,12},{5,13},{6,14},{7,15},{8,0},{9,1},... | collective-permute-start | bytes 1572872 | tf_op jit(solution)/shard_map/ppermute | solution.py:39
  95.5 13.3 %copy-start.15 = (f32[512,128]{0,1:T(8,128)}, f32[512,128]{0,1:T(8,128)S(1)}, u32[]{:S(2)}) copy-start(f32[512,128]{0,1:T(8,128)S(1)} %add.337) | copy-start | bytes 786436
  97.3 5.7 %copy-start.2 = (bf16[1024,512]{1,0:T(8,128)(2,1)}, bf16[1024,512]{1,0:T(8,128)(2,1)S(1)}, u32[]{:S(2)}) copy-start(bf16[1024,512]{1,0:T(8,128)(2,1)S(1)} %collective-permute-done.13.refs_9_.refs_11_.refs_12_) | copy-start | bytes 3145732
  100.8 2.0 %copy-start.3 = (bf16[1024,512]{1,0:T(8,128)(2,1)}, bf16[1024,512]{1,0:T(8,128)(2,1)S(1)}, u32[]{:S(2)}) copy-start(bf16[1024,512]{1,0:T(8,128)(2,1)S(1)} %collective-permute-done.14.refs_10_.refs_12_.refs_13_) | copy-start | bytes 3145732
  102.7 8.0 %copy-start.12 = (bf16[512,512]{1,0:T(8,128)(2,1)}, bf16[512,512]{1,0:T(8,128)(2,1)S(1)}, u32[]{:S(2)}) copy-start(bf16[512,512]{1,0:T(8,128)(2,1)S(1)} %collective-permute-done.12.refs_7_) | copy-start | bytes 1572868
  102.7 3.6 %copy-start.6 = (bf16[1536,512]{1,0:T(8,128)(2,1)}, bf16[1536,512]{1,0:T(8,128)(2,1)S(1)}, u32[]{:S(2)}) copy-start(bf16[1536,512]{1,0:T(8,128)(2,1)S(1)} %collective-permute-done.11.refs_6_) | copy-start | bytes 4718596
  102.7 19.0 %collective-permute-start.19 = (bf16[3072,512]{1,0:T(8,128)(2,1)}, bf16[3072,512]{1,0:T(8,128)(2,1)}, u32[]{:S(2)}, u32[]{:S(2)}) collective-permute-start(bf16[3072,512]{1,0:T(8,128)(2,1)} %pad_maximum_fusion), channel_id=1, source_target_pairs={{0,16},{1,17},{2,18},{3,19},{4,20},{5,21},{6,22},{7,23},{8,24},{9,... | collective-permute-start | bytes 9437192 | tf_op jit(solution)/shard_map/ppermute | solution.py:39
  103.0 18.7 %collective-permute-start.18 = (bf16[1024,512]{1,0:T(8,128)(2,1)S(1)}, bf16[1024,512]{1,0:T(8,128)(2,1)}, u32[]{:S(2)}, u32[]{:S(2)}) collective-permute-start(bf16[1024,512]{1,0:T(8,128)(2,1)S(1)} %collective-permute-done.13.refs_9_.refs_11_.refs_12_), channel_id=1, source_target_pairs={{0,64},{1,65},{2,66},{3,67},{4,68},{5,69},{6,70},{7,71},{8,72},{9,... | collective-permute-start | bytes 3145736 | tf_op jit(solution)/shard_map/ppermute | solution.py:39
  106.4 15.3 %collective-permute-start.16 = (bf16[512,512]{1,0:T(8,128)(2,1)S(1)}, bf16[512,512]{1,0:T(8,128)(2,1)S(1)}, u32[]{:S(2)}, u32[]{:S(2)}) collective-permute-start(bf16[512,512]{1,0:T(8,128)(2,1)S(1)} %collective-permute-done.12.refs_7_), channel_id=1, source_target_pairs={{0,1},{1,2},{2,3},{3,0},{4,5},{5,6},{6,7},{7,4},{8,9},{9,10},{10,1... | collective-permute-start | bytes 1572872 | tf_op jit(solution)/shard_map/ppermute | solution.py:39
  107.5 14.2 %collective-permute-start.17 = (bf16[512,512]{1,0:T(8,128)(2,1)S(1)}, bf16[512,512]{1,0:T(8,128)(2,1)}, u32[]{:S(2)}, u32[]{:S(2)}) collective-permute-start(bf16[512,512]{1,0:T(8,128)(2,1)S(1)} %collective-permute-done.12.refs_7_), channel_id=1, source_target_pairs={{0,3},{1,0},{2,1},{3,2},{4,7},{5,4},{6,5},{7,6},{8,11},{9,8},{10,9... | collective-permute-start | bytes 1572872 | tf_op jit(solution)/shard_map/ppermute | solution.py:39
  108.8 14.9 %copy-start.8 = (bf16[512,512]{1,0:T(8,128)(2,1)S(1)}, bf16[512,512]{1,0:T(8,128)(2,1)}, u32[]{:S(2)}) copy-start(bf16[512,512]{1,0:T(8,128)(2,1)} %refs_0_.5) | copy-start | bytes 1572868
  108.8 18.4 %copy-start.18 = (bf16[1,64,512]{2,1,0:T(8,128)(2,1)S(1)}, bf16[1,64,512]{2,1,0:T(8,128)(2,1)}, u32[]{:S(2)}) copy-start(bf16[1,64,512]{2,1,0:T(8,128)(2,1)} %param.9) | copy-start | bytes 196612
  108.8 12.8 %collective-permute-start.20 = (f32[512,128]{0,1:T(8,128)S(1)}, f32[512,128]{0,1:T(8,128)S(1)}, u32[]{:S(2)}, u32[]{:S(2)}) collective-permute-start(f32[512,128]{0,1:T(8,128)S(1)} %add.337), channel_id=1, source_target_pairs={{0,8},{1,9},{2,10},{3,11},{4,12},{5,13},{6,14},{7,15},{8,0},{9,1},... | collective-permute-start | bytes 786440 | tf_op jit(solution)/shard_map/ppermute | solution.py:39
  110.7 10.9 %copy-start.16 = (f32[512,128]{0,1:T(8,128)S(1)}, f32[512,128]{0,1:T(8,128)}, u32[]{:S(2)}) copy-start(f32[512,128]{0,1:T(8,128)} %copy-done.15) | copy-start | bytes 786436
  121.6 7.2 %copy-start.13 = (bf16[512,512]{1,0:T(8,128)(2,1)}, bf16[512,512]{1,0:T(8,128)(2,1)S(1)}, u32[]{:S(2)}) copy-start(bf16[512,512]{1,0:T(8,128)(2,1)S(1)} %collective-permute-done.16.refs_8_) | copy-start | bytes 1572868
  121.7 14.7 %collective-permute-start.22 = (bf16[1024,512]{1,0:T(8,128)(2,1)}, bf16[1024,512]{1,0:T(8,128)(2,1)S(1)}, u32[]{:S(2)}, u32[]{:S(2)}) collective-permute-start(bf16[1024,512]{1,0:T(8,128)(2,1)} %collective-permute-done.18.refs_14_.refs_15_), channel_id=1, source_target_pairs={{0,16},{1,17},{2,18},{3,19},{4,20},{5,21},{6,22},{7,23},{8,24},{9,... | collective-permute-start | bytes 3145736 | tf_op jit(solution)/shard_map/ppermute | solution.py:39
  124.8 11.6 %collective-permute-start.21 = (bf16[512,512]{1,0:T(8,128)(2,1)S(1)}, bf16[512,512]{1,0:T(8,128)(2,1)S(1)}, u32[]{:S(2)}, u32[]{:S(2)}) collective-permute-start(bf16[512,512]{1,0:T(8,128)(2,1)S(1)} %collective-permute-done.16.refs_8_), channel_id=1, source_target_pairs={{0,1},{1,2},{2,3},{3,0},{4,5},{5,6},{6,7},{7,4},{8,9},{9,10},{10,1... | collective-permute-start | bytes 1572872 | tf_op jit(solution)/shard_map/ppermute | solution.py:39
  136.4 0.8 copy-start.17
  137.2 1.0 copy-start.14

commit v5 on v4

--- a/solution.py
+++ b/solution.py
@@ -13,6 +13,8 @@
 SIZES = (4, 2, 2, 4, 4)
 DIM = 512
 VMEM = 56 * 1024 * 1024
+NEXT_VMEM = 46 * 1024 * 1024
+LAST_VMEM = 16 * 1024 * 1024
 ORDER = (
     ("a", "A0", "B0", "Z1", "Z3", "Ry1:A0"),
     ("b0", "b1", "+Z", "A13", "B13", "Rz1"),
@@ -22,7 +24,7 @@
 )
 HELD = {"G": 0, "A0": 1, "B0": 1, "+Z": 1, "A13": 2, "B13": 2, "F013": 3, "Z2": 3, "A2": 4, "B2": 4, "F2": 5}
 WEIGHTS = {"+X": 2, "XA": 3, "XB": 3, "S1": 4, "XF": 4, "SF": 5}
-STAGES = (3, 4, 5)
+STAGES = (3, 4)
 
 
 def moves(target):
@@ -51,24 +53,39 @@
     return lax.dot_general(g, w, (((1,), (1,)), ((), ())), preferred_element_type=jnp.float32)
 
 
-def product_kernel(pairs, n_g, n_w, first, final, which_ref, *refs):
+def product_kernel(pairs, aside, n_g, n_w, first, which_ref, *refs):
     g_refs, w_refs, rest = refs[:n_g], refs[n_g : n_g + n_w], refs[n_g + n_w :]
     if not first:
         sum_ref, rest = rest[0], rest[1:]
-    if final:
-        kept_ref, add_ref, rest = rest[0], rest[1], rest[2:]
-    out_ref, gs, ws, acc, g_sems, w_sems = rest
+    out_ref, rest = rest[0], rest[1:]
+    if aside:
+        g_out, w_out, rest = rest[0], rest[1], rest[2:]
+    gs, ws, acc, g_sems, w_sems, aside_sems = rest
+
+    def block(ref, place):
+        return ref.at[pl.ds(place * DIM, DIM)]
+
     for k, (i, w_array, w_place, choices) in enumerate(pairs):
         for n, g_array, g_place in choices:
 
             @pl.when(which_ref[i] == n)
             def _():
-                pltpu.make_async_copy(
-                    g_refs[g_array].at[pl.ds(g_place * DIM, DIM)], gs.at[k], g_sems.at[k]
-                ).start()
-                pltpu.make_async_copy(
-                    w_refs[w_array].at[pl.ds(w_place * DIM, DIM)], ws.at[k], w_sems.at[k]
-                ).start()
+                pltpu.make_async_copy(block(g_refs[g_array], g_place), gs.at[k], g_sems.at[k]).start()
+                pltpu.make_async_copy(block(w_refs[w_array], w_place), ws.at[k], w_sems.at[k]).start()
+
+    if aside:
+        for u in range(2):
+            for n, g_array, g_place in aside:
+
+                @pl.when(which_ref[14 + u] == n)
+                def _():
+                    pltpu.make_async_copy(block(g_refs[g_array], g_place), g_out.at[u], aside_sems.at[u]).start()
+
+        for i, w_array, w_place, _ in pairs:
+
+            @pl.when(which_ref[i] == 15)
+            def _():
+                pltpu.make_async_copy(block(w_refs[w_array], w_place), w_out, aside_sems.at[2]).start()
 
     acc[...] = jnp.zeros_like(acc) if first else sum_ref[...]
     for k, (i, _, _, choices) in enumerate(pairs):
@@ -82,15 +99,53 @@
             pltpu.make_async_copy(ws.at[k], ws.at[k], w_sems.at[k]).wait()
             acc[...] += times(gs[k], ws[k])
 
-    if final:
-        out_ref[...] = (acc[...] * kept_ref[...] + add_ref[...]).astype(out_ref.dtype)
-    else:
-        out_ref[...] = acc[...]
-
-
-def partial_sum(stage, which, value, g_places, w_places, total, *ends):
-    place = STAGES.index(stage)
-    ahead = STAGES[place - 1] if place else -1
+    out_ref[...] = acc[...]
+    if aside:
+        for u in range(2):
+
+            @pl.when(which_ref[14 + u] != 15)
+            def _():
+                pltpu.make_async_copy(g_out.at[u], g_out.at[u], aside_sems.at[u]).wait()
+
+        @pl.when(jnp.logical_and(which_ref[14] != 15, which_ref[15] != 15))
+        def _():
+            pltpu.make_async_copy(w_out, w_out, aside_sems.at[2]).wait()
+
+
+def last_kernel(which_ref, g_ref, w_ref, g_aside, w_aside, sum_ref, kept_ref, add_ref, out_ref, acc):
+    acc[...] = sum_ref[...]
+    for u in range(2):
+        rows = slice(u * DIM, (u + 1) * DIM)
+
+        @pl.when(which_ref[14 + u] == 15)
+        def _():
+            acc[...] += times(g_ref[...], w_ref[rows])
+
+        @pl.when(which_ref[14 + u] != 15)
+        def _():
+            acc[...] += times(g_aside[u], w_ref[rows])
+
+    @pl.when(jnp.logical_and(which_ref[14] != 15, which_ref[15] != 15))
+    def _():
+        acc[...] += times(g_ref[...], w_aside[...])
+
+    out_ref[...] = (acc[...] * kept_ref[...] + add_ref[...]).astype(out_ref.dtype)
+
+
+def costs(rows, count, vmem):
+    return {
+        "compiler_params": pltpu.CompilerParams(vmem_limit_bytes=vmem),
+        "cost_estimate": pl.CostEstimate(
+            flops=2 * rows * DIM * DIM * count,
+            bytes_accessed=count * 1024 * 1024,
+            transcendentals=0,
+        ),
+    }
+
+
+def partial_sum(stage, which, value, g_places, w_places, total):
+    first, aside = total is None, []
+    ahead = -1 if first else STAGES[0]
     g_names = [n for n in HELD if HELD[n] <= stage]
     w_names = [n for n in WEIGHTS if WEIGHTS[n] <= stage]
     pairs = []
@@ -98,44 +153,50 @@
         if w_name not in w_names:
             continue
         choices = [
-            (n, g_name, g_place)
+            (n, g_names.index(g_name), g_place)
             for n, (g_name, g_place) in enumerate(g_places)
             if g_name in g_names and max(HELD[g_name], WEIGHTS[w_name]) > ahead
         ]
-        if choices:
-            pairs.append((i, w_name, w_place, choices))
-    g_names = [n for n in g_names if any(g == n for p in pairs for _, g, _ in p[3])]
-    w_names = [n for n in w_names if any(p[1] == n for p in pairs)]
-    pairs = [
-        (i, w_names.index(w), w_place, [(n, g_names.index(g), g_place) for n, g, g_place in choices])
-        for i, w, w_place, choices in pairs
-    ]
+        pairs.append((i, w_names.index(w_name), w_place, choices))
+    if not first:
+        aside = [(n, g_names.index(g), g_place) for n, (g, g_place) in enumerate(g_places) if g in g_names]
     rows = value["G"].shape[0]
     anywhere = pl.BlockSpec(memory_space=pl.ANY)
     in_vmem = pl.BlockSpec(memory_space=pltpu.VMEM)
-    more = [v for v in (total, *ends) if v is not None]
-    count = 16 if stage == STAGES[0] else 8
+    shapes = [jax.ShapeDtypeStruct((rows, DIM), jnp.float32)]
+    if aside:
+        shapes.append(jax.ShapeDtypeStruct((2, rows, DIM), jnp.bfloat16))
+        shapes.append(jax.ShapeDtypeStruct((DIM, DIM), jnp.bfloat16))
     return pl.pallas_call(
-        functools.partial(product_kernel, pairs, len(g_names), len(w_names), total is None, bool(ends)),
-        out_shape=jax.ShapeDtypeStruct((rows, DIM), jnp.bfloat16 if ends else jnp.float32),
+        functools.partial(product_kernel, pairs, aside, len(g_names), len(w_names), first),
+        out_shape=shapes,
         in_specs=[pl.BlockSpec(memory_space=pltpu.SMEM)]
         + [anywhere] * (len(g_names) + len(w_names))
-        + [in_vmem] * len(more),
-        out_specs=in_vmem,
+        + ([] if first else [in_vmem]),
+        out_specs=[in_vmem] * len(shapes),
         scratch_shapes=[
             pltpu.VMEM((len(pairs), rows, DIM), jnp.bfloat16),
             pltpu.VMEM((len(pairs), DIM, DIM), jnp.bfloat16),
             pltpu.VMEM((rows, DIM), jnp.float32),
             pltpu.SemaphoreType.DMA((len(pairs),)),
             pltpu.SemaphoreType.DMA((len(pairs),)),
+            pltpu.SemaphoreType.DMA((3,)),
         ],
-        compiler_params=pltpu.CompilerParams(vmem_limit_bytes=VMEM),
-        cost_estimate=pl.CostEstimate(
-            flops=2 * rows * DIM * DIM * count,
-            bytes_accessed=count * 1024 * 1024,
-            transcendentals=0,
-        ),
-    )(which, *[value[n] for n in g_names], *[value[n] for n in w_names], *more)
+        **costs(rows, 16 if first else 8, VMEM if first else NEXT_VMEM),
+    )(which, *[value[n] for n in g_names], *[value[n] for n in w_names], *([] if first else [total]))
+
+
+def last_sum(which, *arrays):
+    in_vmem = pl.BlockSpec(memory_space=pltpu.VMEM)
+    rows = arrays[0].shape[0]
+    return pl.pallas_call(
+        last_kernel,
+        out_shape=jax.ShapeDtypeStruct((rows, DIM), jnp.bfloat16),
+        in_specs=[pl.BlockSpec(memory_space=pltpu.SMEM)] + [in_vmem] * len(arrays),
+        out_specs=in_vmem,
+        scratch_shapes=[pltpu.VMEM((rows, DIM), jnp.float32)],
+        **costs(rows, 3, LAST_VMEM),
+    )(which, *arrays)
 
 
 def shards(projection_input, output_gradient, frozen_weight, down_adapters, up_adapters, lengths):
@@ -258,12 +319,13 @@
             value[name] = act(*given)
         before, beside = [value[n] for n in names] + beside, []
         if number == 3:
-            total = partial_sum(number, which, value, g_places, w_places, None)
+            (total,) = partial_sum(number, which, value, g_places, w_places, None)
             beside = [total]
         if number == 4:
-            total = partial_sum(number, which, value, g_places, w_places, total)
+            total, g_aside, w_aside = partial_sum(number, which, value, g_places, w_places, total)
     adapter_part, down_gradient, up_gradient = ends(value["Rz2"])
-    grad_input = partial_sum(5, which, value, g_places, w_places, total, kept.astype(jnp.float32)[:, None], adapter_part)
+    kept_column = kept.astype(jnp.float32)[:, None]
+    grad_input = last_sum(which, value["F2"], value["SF"], g_aside, w_aside, total, kept_column, adapter_part)
     return (grad_input, down_gradient, up_gradient)
 
 

time: 144 us -> 139 us (0.965)
  Pallas kernels: 18.7 us -> 16.1 us
  starting transfers between devices: 43.8 us -> 42 us
    pallas_call x3, Pallas kernels: 18.7 us -> 16.1 us  [the longest x2 12.8 us: partial_sum(): pl.pallas_call(functools.partial(product_kernel, pairs, aside, len(g_name...]
    ppermute x23, starting transfers between devices: 43.8 us -> 42 us  [send(): return lax.ppermute(value, AXES, moves(target))]
  transfers between devices with their start and end apart: 23 -> 23, of which waited for: 8 -> 9; matrix products, arithmetic and copies ran while one was open for 7% -> 7% of each run, Pallas kernels for 9% -> 9%
where the time goes in v5:
time: 139 us
  waiting for transfers between devices  68.4 us (49%)
  starting transfers between devices  42 us (30%)
  Pallas kernels  16.1 us (12%)
  matrix products  5.3 us (4%)
  other arithmetic  4.25 us (3%)
  between operations  1.74 us (1%)
    ppermute x23, waiting for transfers between devices, send(): return lax.ppermute(value, AXES, moves(target))  68.4 us
    ppermute x23, starting transfers between devices, send(): return lax.ppermute(value, AXES, moves(target))  42 us
    pallas_call x2, Pallas kernels, partial_sum(): pl.pallas_call(functools.partial(product_kernel, pairs, aside, len(g_name...  12.8 us
    concatenate x2, other arithmetic, join(): return jnp.concatenate(parts, axis=0)  3.28 us
    pallas_call x1, Pallas kernels, last_sum(): pl.pallas_call(last_kernel, out_shape=jax.ShapeDtypeStruct((rows, DIM), j...  3.25 us
  transfers between devices with their start and end apart: 23, of which 9 were waited for; matrix products, arithmetic and copies ran while one was open for 7% of the time, Pallas kernels for 9%

profile of v5, /device:TPU:1, one launch (start us, length us, event | category | flops | bytes accessed | tf_op | source)
XLA Modules:
  0.0 139.0 jit_solution(18184279105880519020)
XLA Ops:
  0.6 0.0 copy-start
  0.6 3.6 %collective-permute-start.1 = (bf16[512,512]{1,0:T(8,128)(2,1)}, bf16[512,512]{1,0:T(8,128)(2,1)S(1)}, u32[]{:S(2)}, u32[]{:S(2)}) collective-permute-start(bf16[512,512]{1,0:T(8,128)(2,1)} %refs_0_.3), channel_id=1, source_target_pairs={{0,1},{1,2},{2,3},{3,0},{4,5},{5,6},{6,7},{7,4},{8,9},{9,10},{10,1... | collective-permute-start | bytes 1572872 | tf_op jit(solution)/shard_map/ppermute | solution.py:41
  4.3 0.0 collective-permute-start.2
  4.3 1.6 %collective-permute-start.3 = (bf16[512,512]{1,0:T(8,128)(2,1)}, bf16[512,512]{1,0:T(8,128)(2,1)S(1)}, u32[]{:S(2)}, u32[]{:S(2)}) collective-permute-start(bf16[512,512]{1,0:T(8,128)(2,1)} %refs_0_.3), channel_id=1, source_target_pairs={{0,4},{1,5},{2,6},{3,7},{4,8},{5,9},{6,10},{7,11},{8,12},{9,13},{1... | collective-permute-start | bytes 1572872 | tf_op jit(solution)/shard_map/ppermute | solution.py:41
  5.9 2.7 %collective-permute-start.4 = (bf16[512,512]{1,0:T(8,128)(2,1)}, bf16[512,512]{1,0:T(8,128)(2,1)S(1)}, u32[]{:S(2)}, u32[]{:S(2)}) collective-permute-start(bf16[512,512]{1,0:T(8,128)(2,1)} %refs_0_.3), channel_id=1, source_target_pairs={{0,12},{1,13},{2,14},{3,15},{4,0},{5,1},{6,2},{7,3},{8,4},{9,5},{1... | collective-permute-start | bytes 1572872 | tf_op jit(solution)/shard_map/ppermute | solution.py:41
  8.6 3.3 %collective-permute-start = (bf16[512,512]{1,0:T(8,128)(2,1)}, bf16[512,512]{1,0:T(8,128)(2,1)S(1)}, u32[]{:S(2)}, u32[]{:S(2)}) collective-permute-start(bf16[512,512]{1,0:T(8,128)(2,1)} %param.8), channel_id=1, source_target_pairs={{0,0},{1,16},{2,2},{3,18},{4,196},{5,84},{6,198},{7,86},{8,136},{9... | collective-permute-start | bytes 1572872 | tf_op jit(solution)/shard_map/ppermute | solution.py:41
  12.6 1.4 %fusion.3 = f32[512,64]{0,1:T(8,128)S(1)} fusion(bf16[512,512]{1,0:T(8,128)(2,1)} %refs_0_.3, bf16[512]{0:T(512)(128)(2,1)S(1)} %fusion.16, bf16[1,64,512]{2,1,0:T(8,128)(2,1)} %param.10), kind=kOutput, calls=%fused_computation.7 | convolution fusion | flops 33816576 | bytes 721920 | tf_op jit(solution)/shard_map/dot_general | solution.py:215
  14.0 1.1 fusion.12
  15.2 0.0 collective-permute-done.1.refs_1_
  15.2 0.0 copy-start.7
  15.2 0.1 collective-permute-start.5
  15.3 3.9 %collective-permute-done.3 = bf16[512,512]{1,0:T(8,128)(2,1)S(1)} collective-permute-done((bf16[512,512]{1,0:T(8,128)(2,1)}, bf16[512,512]{1,0:T(8,128)(2,1)S(1)}, u32[]{:S(2)}, u32[]{:S(2)}) %collective-permute-start.3) | collective-permute-done | bytes 524320 | tf_op jit(solution)/shard_map/ppermute | solution.py:41
  19.2 11.0 %collective-permute-done.4 = bf16[512,512]{1,0:T(8,128)(2,1)S(1)} collective-permute-done((bf16[512,512]{1,0:T(8,128)(2,1)}, bf16[512,512]{1,0:T(8,128)(2,1)S(1)}, u32[]{:S(2)}, u32[]{:S(2)}) %collective-permute-start.4) | collective-permute-done | bytes 524320 | tf_op jit(solution)/shard_map/ppermute | solution.py:41
  30.3 0.0 collective-permute-done.5
  30.4 0.0 copy-start.5
  30.4 0.0 collective-permute-done.2.refs_2_
  30.4 0.8 copy-done.9
  31.2 0.0 collective-permute-done
  31.2 3.4 %collective-permute-start.8 = (bf16[1024,512]{1,0:T(8,128)(2,1)S(1)}, bf16[1024,512]{1,0:T(8,128)(2,1)S(1)}, u32[]{:S(2)}, u32[]{:S(2)}) collective-permute-start(bf16[1024,512]{1,0:T(8,128)(2,1)S(1)} %constant_dynamic-update-slice_fusion.refs_3_), channel_id=1, source_target_pairs={{0,1},{1,2},{2,3},{3,0},{4,5},{5,6},{6,7},{7,4},{8,9},{9,10},{10,1... | collective-permute-start | bytes 3145736 | tf_op jit(solution)/shard_map/ppermute | solution.py:41
  34.6 0.0 collective-permute-start.9
  34.6 0.7 collective-permute-start.6
  35.3 1.9 %collective-permute-start.10 = (f32[512,128]{0,1:T(8,128)S(1)}, f32[512,128]{0,1:T(8,128)S(1)}, u32[]{:S(2)}, u32[]{:S(2)}) collective-permute-start(f32[512,128]{0,1:T(8,128)S(1)} %add.335), channel_id=1, source_target_pairs={{0,4},{1,5},{2,6},{3,7},{4,0},{5,1},{6,2},{7,3},{8,12},{9,13},{10,... | collective-permute-start | bytes 786440 | tf_op jit(solution)/shard_map/ppermute | solution.py:41
  37.2 7.5 %collective-permute-start.7 = (bf16[512,512]{1,0:T(8,128)(2,1)S(1)}, bf16[512,512]{1,0:T(8,128)(2,1)S(1)}, u32[]{:S(2)}, u32[]{:S(2)}) collective-permute-start(bf16[512,512]{1,0:T(8,128)(2,1)S(1)} %collective-permute-done), channel_id=1, source_target_pairs={{0,32},{1,33},{2,0},{3,1},{4,36},{5,37},{6,4},{7,5},{8,40},{9,41},... | collective-permute-start | bytes 1572872 | tf_op jit(solution)/shard_map/ppermute | solution.py:41
  44.7 0.0 collective-permute-done.10
  44.7 0.0 collective-permute-done.6
  44.8 22.4 %collective-permute-done.8.refs_4_ = bf16[1024,512]{1,0:T(8,128)(2,1)S(1)} collective-permute-done((bf16[1024,512]{1,0:T(8,128)(2,1)S(1)}, bf16[1024,512]{1,0:T(8,128)(2,1)S(1)}, u32[]{:S(2)}, u32[]{:S(2)}) %collective-permute-start.8) | collective-permute-done | bytes 1048608 | tf_op jit(solution)/shard_map/ppermute | solution.py:41
  67.2 0.1 pad_maximum_fusion.1
  67.3 2.2 %collective-permute-done.7 = bf16[512,512]{1,0:T(8,128)(2,1)S(1)} collective-permute-done((bf16[512,512]{1,0:T(8,128)(2,1)S(1)}, bf16[512,512]{1,0:T(8,128)(2,1)S(1)}, u32[]{:S(2)}, u32[]{:S(2)}) %collective-permute-start.7) | collective-permute-done | bytes 524320 | tf_op jit(solution)/shard_map/ppermute | solution.py:41
  69.4 1.4 %collective-permute-done.9.refs_5_ = bf16[1024,512]{1,0:T(8,128)(2,1)S(1)} collective-permute-done((bf16[1024,512]{1,0:T(8,128)(2,1)S(1)}, bf16[1024,512]{1,0:T(8,128)(2,1)S(1)}, u32[]{:S(2)}, u32[]{:S(2)}) %collective-permute-start.9) | collective-permute-done | bytes 1048608 | tf_op jit(solution)/shard_map/ppermute | solution.py:41
  70.8 2.4 %collective-permute-start.14 = (bf16[1536,512]{1,0:T(8,128)(2,1)S(1)}, bf16[1536,512]{1,0:T(8,128)(2,1)}, u32[]{:S(2)}, u32[]{:S(2)}) collective-permute-start(bf16[1536,512]{1,0:T(8,128)(2,1)S(1)} %pad_maximum_fusion.1), channel_id=1, source_target_pairs={{0,1},{1,2},{2,3},{3,0},{4,5},{5,6},{6,7},{7,4},{8,9},{9,10},{10,1... | collective-permute-start | bytes 4718600 | tf_op jit(solution)/shard_map/ppermute | solution.py:41
  73.2 3.4 %collective-permute-start.12 = (bf16[1024,512]{1,0:T(8,128)(2,1)S(1)}, bf16[1024,512]{1,0:T(8,128)(2,1)}, u32[]{:S(2)}, u32[]{:S(2)}) collective-permute-start(bf16[1024,512]{1,0:T(8,128)(2,1)S(1)} %constant_dynamic-update-slice_fusion.2.refs_8_.refs_10_), channel_id=1, source_target_pairs={{0,64},{1,65},{2,66},{3,67},{4,68},{5,69},{6,70},{7,71},{8,72},{9,... | collective-permute-start | bytes 3145736 | tf_op jit(solution)/shard_map/ppermute | solution.py:41
  76.7 0.0 collective-permute-start.13
  76.7 0.4 collective-permute-start.15
  77.1 1.7 %collective-permute-start.11 = (bf16[512,512]{1,0:T(8,128)(2,1)S(1)}, bf16[512,512]{1,0:T(8,128)(2,1)}, u32[]{:S(2)}, u32[]{:S(2)}) collective-permute-start(bf16[512,512]{1,0:T(8,128)(2,1)S(1)} %copy-done.5), channel_id=1, source_target_pairs={{0,8},{1,9},{2,10},{3,11},{4,12},{5,13},{6,14},{7,15},{8,0},{9,1},... | collective-permute-start | bytes 1572872 | tf_op jit(solution)/shard_map/ppermute | solution.py:41
  78.9 17.3 %collective-permute-done.15 = f32[512,128]{0,1:T(8,128)S(1)} collective-permute-done((f32[512,128]{0,1:T(8,128)S(1)}, f32[512,128]{0,1:T(8,128)S(1)}, u32[]{:S(2)}, u32[]{:S(2)}) %collective-permute-start.15) | collective-permute-done | bytes 262176 | tf_op jit(solution)/shard_map/ppermute | solution.py:41
  96.2 1.8 %collective-permute-done.12.refs_9_.refs_11_ = bf16[1024,512]{1,0:T(8,128)(2,1)} collective-permute-done((bf16[1024,512]{1,0:T(8,128)(2,1)S(1)}, bf16[1024,512]{1,0:T(8,128)(2,1)}, u32[]{:S(2)}, u32[]{:S(2)}) %collective-permute-start.12) | collective-permute-done | bytes 1048608 | tf_op jit(solution)/shard_map/ppermute | solution.py:41
  98.0 3.6 %collective-permute-done.13.refs_10_.refs_12_ = bf16[1024,512]{1,0:T(8,128)(2,1)S(1)} collective-permute-done((bf16[1024,512]{1,0:T(8,128)(2,1)S(1)}, bf16[1024,512]{1,0:T(8,128)(2,1)S(1)}, u32[]{:S(2)}, u32[]{:S(2)}) %collective-permute-start.13) | collective-permute-done | bytes 1048608 | tf_op jit(solution)/shard_map/ppermute | solution.py:41
  101.6 3.2 %pad_maximum_fusion = bf16[3072,512]{1,0:T(8,128)(2,1)} fusion(bf16[1024,512]{1,0:T(8,128)(2,1)S(1)} %collective-permute-done.13.refs_10_.refs_12_, bf16[1024,512]{1,0:T(8,128)(2,1)} %collective-permute-done.12.refs_9_.refs_11_, bf16[512,512]{1,0:T(8,128)(2,1)S(1)} %collective-permute-done.7, bf16[512,512]{1,0:T(8,128)(2,1)S(1)} %collective-permute-done.6), kind=kLoop, calls=%fused_computation | loop fusion | flops 12582912 | bytes 6291456 | tf_op jit(solution)/shard_map/concatenate | solution.py:222
  104.7 0.0 collective-permute-done.11.refs_7_
  104.7 0.0 collective-permute-done.14.refs_6_
  104.8 0.1 collective-permute-start.19
  104.9 3.4 %collective-permute-start.17 = (bf16[1024,512]{1,0:T(8,128)(2,1)}, bf16[1024,512]{1,0:T(8,128)(2,1)}, u32[]{:S(2)}, u32[]{:S(2)}) collective-permute-start(bf16[1024,512]{1,0:T(8,128)(2,1)} %collective-permute-done.12.refs_9_.refs_11_), channel_id=1, source_target_pairs={{0,64},{1,65},{2,66},{3,67},{4,68},{5,69},{6,70},{7,71},{8,72},{9,... | collective-permute-start | bytes 3145736 | tf_op jit(solution)/shard_map/ppermute | solution.py:41
  108.2 0.0 collective-permute-start.16
  108.2 1.5 %collective-permute-start.18 = (bf16[512,512]{1,0:T(8,128)(2,1)}, bf16[512,512]{1,0:T(8,128)(2,1)}, u32[]{:S(2)}, u32[]{:S(2)}) collective-permute-start(bf16[512,512]{1,0:T(8,128)(2,1)} %collective-permute-done.11.refs_7_), channel_id=1, source_target_pairs={{0,3},{1,0},{2,1},{3,2},{4,7},{5,4},{6,5},{7,6},{8,11},{9,8},{10,9... | collective-permute-start | bytes 1572872 | tf_op jit(solution)/shard_map/ppermute | solution.py:41
  109.7 0.1 stack.118
  109.8 0.1 stack.135
  109.9 0.8 select_reduce_fusion.which_ref
  110.7 1.9 %collective-permute-start.20 = (f32[512,128]{0,1:T(8,128)S(1)}, f32[512,128]{0,1:T(8,128)S(1)}, u32[]{:S(2)}, u32[]{:S(2)}) collective-permute-start(f32[512,128]{0,1:T(8,128)S(1)} %add.337), channel_id=1, source_target_pairs={{0,8},{1,9},{2,10},{3,11},{4,12},{5,13},{6,14},{7,15},{8,0},{9,1},... | collective-permute-start | bytes 786440 | tf_op jit(solution)/shard_map/ppermute | solution.py:41
  112.6 6.0 %shard_map.85.refs_15_ = f32[512,512]{1,0:T(8,128)} custom-call(s32[16]{0:T(128)} %select_reduce_fusion.which_ref, bf16[512,512]{1,0:T(8,128)(2,1)} %refs_0_.3, bf16[512,512]{1,0:T(8,128)(2,1)} %copy-done.7, bf16[512,512]{1,0:T(8,128)(2,1)} %copy-done.9, bf16[1024,512]{1,0:T(8,128)(2,1)} %copy-done.3, bf16[1024,512]{1,0:T(8,128)(2,1)} %copy-done.1, ...), custom_call_target="tpu_custom_call" | custom-call | flops 4294967296 | bytes 16777216 | tf_op jit(solution)/shard_map/pallas_call | solution.py:170
  118.7 4.9 %collective-permute-done.20 = f32[512,128]{0,1:T(8,128)S(1)} collective-permute-done((f32[512,128]{0,1:T(8,128)S(1)}, f32[512,128]{0,1:T(8,128)S(1)}, u32[]{:S(2)}, u32[]{:S(2)}) %collective-permute-start.20) | collective-permute-done | bytes 262176 | tf_op jit(solution)/shard_map/ppermute | solution.py:41
  123.6 0.0 collective-permute-done.16.refs_8_
  123.6 0.0 collective-permute-done.18.refs_9_
  123.7 0.0 collective-permute-done.17.refs_14_
  123.7 0.0 collective-permute-done.19.refs_13_
  123.7 1.1 collective-permute-start.22
  124.8 0.0 copy-start.8
  124.9 1.1 fusion
  126.0 1.2 collective-permute-start.21
  127.2 1.0 fusion.1
  128.2 0.6 fusion.9.add_ref
  128.9 6.8 %shard_map.86 = (f32[512,512]{1,0:T(8,128)S(1)}, bf16[2,512,512]{2,1,0:T(8,128)(2,1)S(1)}, bf16[512,512]{1,0:T(8,128)(2,1)S(1)}) custom-call(s32[16]{0:T(128)S(1)} %copy-done.11, bf16[512,512]{1,0:T(8,128)(2,1)S(1)} %copy-done.6, bf16[512,512]{1,0:T(8,128)(2,1)S(1)} %copy-done.8, bf16[512,512]{1,0:T(8,128)(2,1)S(1)} %copy-done.10, ...), custom_call_target="tpu_custom_call" | custom-call | flops 2147483648 | bytes 8388608 | tf_op jit(solution)/shard_map/pallas_call | solution.py:170
  135.7 0.0 collective-permute-done.21.g_ref
  135.7 0.0 collective-permute-done.22.w_ref
  135.7 3.3 %shard_map.87 = bf16[512,512]{1,0:T(8,128)(2,1)} custom-call(s32[16]{0:T(128)S(1)} %copy-done.11, bf16[512,512]{1,0:T(8,128)(2,1)S(1)} %collective-permute-done.21.g_ref, bf16[1024,512]{1,0:T(8,128)(2,1)} %collective-permute-done.22.w_ref, bf16[2,512,512]{2,1,0:T(8,128)(2,1)S(1)} %get-tuple-element.34.g_aside, ...), custom_call_target="tpu_custom_call" | custom-call | flops 805306368 | bytes 3145728 | tf_op jit(solution)/shard_map/pallas_call | solution.py:192
  (42 shorter events, 0.4 us)
Async XLA Ops:
  0.6 13.4 %copy-start = (bf16[512,512]{1,0:T(8,128)(2,1)S(1)}, bf16[512,512]{1,0:T(8,128)(2,1)}, u32[]{:S(2)}) copy-start(bf16[512,512]{1,0:T(8,128)(2,1)} %param.6) | copy-start | bytes 1572868
  0.6 14.5 %collective-permute-start.1 = (bf16[512,512]{1,0:T(8,128)(2,1)}, bf16[512,512]{1,0:T(8,128)(2,1)S(1)}, u32[]{:S(2)}, u32[]{:S(2)}) collective-permute-start(bf16[512,512]{1,0:T(8,128)(2,1)} %refs_0_.3), channel_id=1, source_target_pairs={{0,1},{1,2},{2,3},{3,0},{4,5},{5,6},{6,7},{7,4},{8,9},{9,10},{10,1... | collective-permute-start | bytes 1572872 | tf_op jit(solution)/shard_map/ppermute | solution.py:41
  4.3 26.1 %collective-permute-start.2 = (bf16[512,512]{1,0:T(8,128)(2,1)}, bf16[512,512]{1,0:T(8,128)(2,1)S(1)}, u32[]{:S(2)}, u32[]{:S(2)}) collective-permute-start(bf16[512,512]{1,0:T(8,128)(2,1)} %refs_0_.3), channel_id=1, source_target_pairs={{0,3},{1,0},{2,1},{3,2},{4,7},{5,4},{6,5},{7,6},{8,11},{9,8},{10,9... | collective-permute-start | bytes 1572872 | tf_op jit(solution)/shard_map/ppermute | solution.py:41
  4.3 14.9 %collective-permute-start.3 = (bf16[512,512]{1,0:T(8,128)(2,1)}, bf16[512,512]{1,0:T(8,128)(2,1)S(1)}, u32[]{:S(2)}, u32[]{:S(2)}) collective-permute-start(bf16[512,512]{1,0:T(8,128)(2,1)} %refs_0_.3), channel_id=1, source_target_pairs={{0,4},{1,5},{2,6},{3,7},{4,8},{5,9},{6,10},{7,11},{8,12},{9,13},{1... | collective-permute-start | bytes 1572872 | tf_op jit(solution)/shard_map/ppermute | solution.py:41
  5.9 24.3 %collective-permute-start.4 = (bf16[512,512]{1,0:T(8,128)(2,1)}, bf16[512,512]{1,0:T(8,128)(2,1)S(1)}, u32[]{:S(2)}, u32[]{:S(2)}) collective-permute-start(bf16[512,512]{1,0:T(8,128)(2,1)} %refs_0_.3), channel_id=1, source_target_pairs={{0,12},{1,13},{2,14},{3,15},{4,0},{5,1},{6,2},{7,3},{8,4},{9,5},{1... | collective-permute-start | bytes 1572872 | tf_op jit(solution)/shard_map/ppermute | solution.py:41
  8.6 22.5 %collective-permute-start = (bf16[512,512]{1,0:T(8,128)(2,1)}, bf16[512,512]{1,0:T(8,128)(2,1)S(1)}, u32[]{:S(2)}, u32[]{:S(2)}) collective-permute-start(bf16[512,512]{1,0:T(8,128)(2,1)} %param.8), channel_id=1, source_target_pairs={{0,0},{1,16},{2,2},{3,18},{4,196},{5,84},{6,198},{7,86},{8,136},{9... | collective-permute-start | bytes 1572872 | tf_op jit(solution)/shard_map/ppermute | solution.py:41
  15.2 52.1 %copy-start.7 = (bf16[512,512]{1,0:T(8,128)(2,1)}, bf16[512,512]{1,0:T(8,128)(2,1)S(1)}, u32[]{:S(2)}) copy-start(bf16[512,512]{1,0:T(8,128)(2,1)S(1)} %collective-permute-done.1.refs_1_) | copy-start | bytes 1572868
  15.2 15.1 %collective-permute-start.5 = (f32[512,128]{0,1:T(8,128)S(1)}, f32[512,128]{0,1:T(8,128)S(1)}, u32[]{:S(2)}, u32[]{:S(2)}) collective-permute-start(f32[512,128]{0,1:T(8,128)S(1)} %pad_maximum_fusion.2), channel_id=1, source_target_pairs={{0,1},{1,0},{2,3},{3,2},{4,5},{5,4},{6,7},{7,6},{8,9},{9,8},{10,11... | collective-permute-start | bytes 786440 | tf_op jit(solution)/shard_map/ppermute | solution.py:41
  30.3 42.9 %copy-start.3 = (bf16[1024,512]{1,0:T(8,128)(2,1)}, bf16[1024,512]{1,0:T(8,128)(2,1)S(1)}, u32[]{:S(2)}) copy-start(bf16[1024,512]{1,0:T(8,128)(2,1)S(1)} %constant_dynamic-update-slice_fusion.refs_3_) | copy-start | bytes 3145732
  30.4 46.8 %copy-start.5 = (bf16[512,512]{1,0:T(8,128)(2,1)S(1)}, bf16[512,512]{1,0:T(8,128)(2,1)}, u32[]{:S(2)}) copy-start(bf16[512,512]{1,0:T(8,128)(2,1)} %refs_0_.3) | copy-start | bytes 1572868
  30.4 0.8 copy-start.9
  31.2 36.0 %collective-permute-start.8 = (bf16[1024,512]{1,0:T(8,128)(2,1)S(1)}, bf16[1024,512]{1,0:T(8,128)(2,1)S(1)}, u32[]{:S(2)}, u32[]{:S(2)}) collective-permute-start(bf16[1024,512]{1,0:T(8,128)(2,1)S(1)} %constant_dynamic-update-slice_fusion.refs_3_), channel_id=1, source_target_pairs={{0,1},{1,2},{2,3},{3,0},{4,5},{5,6},{6,7},{7,4},{8,9},{9,10},{10,1... | collective-permute-start | bytes 3145736 | tf_op jit(solution)/shard_map/ppermute | solution.py:41
  34.6 36.2 %collective-permute-start.9 = (bf16[1024,512]{1,0:T(8,128)(2,1)S(1)}, bf16[1024,512]{1,0:T(8,128)(2,1)S(1)}, u32[]{:S(2)}, u32[]{:S(2)}) collective-permute-start(bf16[1024,512]{1,0:T(8,128)(2,1)S(1)} %constant_dynamic-update-slice_fusion.refs_3_), channel_id=1, source_target_pairs={{0,3},{1,0},{2,1},{3,2},{4,7},{5,4},{6,5},{7,6},{8,11},{9,8},{10,9... | collective-permute-start | bytes 3145736 | tf_op jit(solution)/shard_map/ppermute | solution.py:41
  34.6 10.1 %collective-permute-start.6 = (bf16[512,512]{1,0:T(8,128)(2,1)S(1)}, bf16[512,512]{1,0:T(8,128)(2,1)S(1)}, u32[]{:S(2)}, u32[]{:S(2)}) collective-permute-start(bf16[512,512]{1,0:T(8,128)(2,1)S(1)} %collective-permute-done), channel_id=1, source_target_pairs={{0,0},{1,1},{2,32},{3,33},{4,4},{5,5},{6,36},{7,37},{8,8},{9,9},{1... | collective-permute-start | bytes 1572872 | tf_op jit(solution)/shard_map/ppermute | solution.py:41
  35.3 9.4 %collective-permute-start.10 = (f32[512,128]{0,1:T(8,128)S(1)}, f32[512,128]{0,1:T(8,128)S(1)}, u32[]{:S(2)}, u32[]{:S(2)}) collective-permute-start(f32[512,128]{0,1:T(8,128)S(1)} %add.335), channel_id=1, source_target_pairs={{0,4},{1,5},{2,6},{3,7},{4,0},{5,1},{6,2},{7,3},{8,12},{9,13},{10,... | collective-permute-start | bytes 786440 | tf_op jit(solution)/shard_map/ppermute | solution.py:41
  37.2 32.2 %collective-permute-start.7 = (bf16[512,512]{1,0:T(8,128)(2,1)S(1)}, bf16[512,512]{1,0:T(8,128)(2,1)S(1)}, u32[]{:S(2)}, u32[]{:S(2)}) collective-permute-start(bf16[512,512]{1,0:T(8,128)(2,1)S(1)} %collective-permute-done), channel_id=1, source_target_pairs={{0,32},{1,33},{2,0},{3,1},{4,36},{5,37},{6,4},{7,5},{8,40},{9,41},... | collective-permute-start | bytes 1572872 | tf_op jit(solution)/shard_map/ppermute | solution.py:41
  67.2 37.6 %copy-start.1 = (bf16[1024,512]{1,0:T(8,128)(2,1)}, bf16[1024,512]{1,0:T(8,128)(2,1)S(1)}, u32[]{:S(2)}) copy-start(bf16[1024,512]{1,0:T(8,128)(2,1)S(1)} %collective-permute-done.8.refs_4_) | copy-start | bytes 3145732
  70.8 27.2 %copy-start.14 = (bf16[1024,512]{1,0:T(8,128)(2,1)}, bf16[1024,512]{1,0:T(8,128)(2,1)S(1)}, u32[]{:S(2)}) copy-start(bf16[1024,512]{1,0:T(8,128)(2,1)S(1)} %collective-permute-done.9.refs_5_) | copy-start | bytes 3145732
  70.8 33.9 %collective-permute-start.14 = (bf16[1536,512]{1,0:T(8,128)(2,1)S(1)}, bf16[1536,512]{1,0:T(8,128)(2,1)}, u32[]{:S(2)}, u32[]{:S(2)}) collective-permute-start(bf16[1536,512]{1,0:T(8,128)(2,1)S(1)} %pad_maximum_fusion.1), channel_id=1, source_target_pairs={{0,1},{1,2},{2,3},{3,0},{4,5},{5,6},{6,7},{7,4},{8,9},{9,10},{10,1... | collective-permute-start | bytes 4718600 | tf_op jit(solution)/shard_map/ppermute | solution.py:41
  73.2 23.0 %copy-start.13 = (bf16[1024,512]{1,0:T(8,128)(2,1)}, bf16[1024,512]{1,0:T(8,128)(2,1)S(1)}, u32[]{:S(2)}) copy-start(bf16[1024,512]{1,0:T(8,128)(2,1)S(1)} %constant_dynamic-update-slice_fusion.2.refs_8_.refs_10_) | copy-start | bytes 3145732
  73.2 24.7 %collective-permute-start.12 = (bf16[1024,512]{1,0:T(8,128)(2,1)S(1)}, bf16[1024,512]{1,0:T(8,128)(2,1)}, u32[]{:S(2)}, u32[]{:S(2)}) collective-permute-start(bf16[1024,512]{1,0:T(8,128)(2,1)S(1)} %constant_dynamic-update-slice_fusion.2.refs_8_.refs_10_), channel_id=1, source_target_pairs={{0,64},{1,65},{2,66},{3,67},{4,68},{5,69},{6,70},{7,71},{8,72},{9,... | collective-permute-start | bytes 3145736 | tf_op jit(solution)/shard_map/ppermute | solution.py:41
  76.7 24.9 %collective-permute-start.13 = (bf16[1024,512]{1,0:T(8,128)(2,1)S(1)}, bf16[1024,512]{1,0:T(8,128)(2,1)S(1)}, u32[]{:S(2)}, u32[]{:S(2)}) collective-permute-start(bf16[1024,512]{1,0:T(8,128)(2,1)S(1)} %constant_dynamic-update-slice_fusion.2.refs_8_.refs_10_), channel_id=1, source_target_pairs={{0,192},{1,193},{2,194},{3,195},{4,196},{5,197},{6,198},{7,199},{8... | collective-permute-start | bytes 3145736 | tf_op jit(solution)/shard_map/ppermute | solution.py:41
  76.7 19.5 %collective-permute-start.15 = (f32[512,128]{0,1:T(8,128)S(1)}, f32[512,128]{0,1:T(8,128)S(1)}, u32[]{:S(2)}, u32[]{:S(2)}) collective-permute-start(f32[512,128]{0,1:T(8,128)S(1)} %add.336), channel_id=1, source_target_pairs={{0,3},{1,2},{2,1},{3,0},{4,7},{5,6},{6,5},{7,4},{8,11},{9,10},{10,... | collective-permute-start | bytes 786440 | tf_op jit(solution)/shard_map/ppermute | solution.py:41
  77.1 27.6 %collective-permute-start.11 = (bf16[512,512]{1,0:T(8,128)(2,1)S(1)}, bf16[512,512]{1,0:T(8,128)(2,1)}, u32[]{:S(2)}, u32[]{:S(2)}) collective-permute-start(bf16[512,512]{1,0:T(8,128)(2,1)S(1)} %copy-done.5), channel_id=1, source_target_pairs={{0,8},{1,9},{2,10},{3,11},{4,12},{5,13},{6,14},{7,15},{8,0},{9,1},... | collective-permute-start | bytes 1572872 | tf_op jit(solution)/shard_map/ppermute | solution.py:41
  96.2 14.4 %copy-start.15 = (f32[512,128]{0,1:T(8,128)}, f32[512,128]{0,1:T(8,128)S(1)}, u32[]{:S(2)}) copy-start(f32[512,128]{0,1:T(8,128)S(1)} %add.337) | copy-start | bytes 786436
  101.6 3.2 %copy-start.12 = (bf16[1024,512]{1,0:T(8,128)(2,1)}, bf16[1024,512]{1,0:T(8,128)(2,1)S(1)}, u32[]{:S(2)}) copy-start(bf16[1024,512]{1,0:T(8,128)(2,1)S(1)} %collective-permute-done.13.refs_10_.refs_12_) | copy-start | bytes 3145732
  104.8 18.9 %collective-permute-start.19 = (bf16[3072,512]{1,0:T(8,128)(2,1)}, bf16[3072,512]{1,0:T(8,128)(2,1)}, u32[]{:S(2)}, u32[]{:S(2)}) collective-permute-start(bf16[3072,512]{1,0:T(8,128)(2,1)} %pad_maximum_fusion), channel_id=1, source_target_pairs={{0,16},{1,17},{2,18},{3,19},{4,20},{5,21},{6,22},{7,23},{8,24},{9,... | collective-permute-start | bytes 9437192 | tf_op jit(solution)/shard_map/ppermute | solution.py:41
  104.9 18.8 %collective-permute-start.17 = (bf16[1024,512]{1,0:T(8,128)(2,1)}, bf16[1024,512]{1,0:T(8,128)(2,1)}, u32[]{:S(2)}, u32[]{:S(2)}) collective-permute-start(bf16[1024,512]{1,0:T(8,128)(2,1)} %collective-permute-done.12.refs_9_.refs_11_), channel_id=1, source_target_pairs={{0,64},{1,65},{2,66},{3,67},{4,68},{5,69},{6,70},{7,71},{8,72},{9,... | collective-permute-start | bytes 3145736 | tf_op jit(solution)/shard_map/ppermute | solution.py:41
  108.2 15.4 %collective-permute-start.16 = (bf16[512,512]{1,0:T(8,128)(2,1)}, bf16[512,512]{1,0:T(8,128)(2,1)}, u32[]{:S(2)}, u32[]{:S(2)}) collective-permute-start(bf16[512,512]{1,0:T(8,128)(2,1)} %collective-permute-done.11.refs_7_), channel_id=1, source_target_pairs={{0,1},{1,2},{2,3},{3,0},{4,5},{5,6},{6,7},{7,4},{8,9},{9,10},{10,1... | collective-permute-start | bytes 1572872 | tf_op jit(solution)/shard_map/ppermute | solution.py:41
  108.2 15.4 %collective-permute-start.18 = (bf16[512,512]{1,0:T(8,128)(2,1)}, bf16[512,512]{1,0:T(8,128)(2,1)}, u32[]{:S(2)}, u32[]{:S(2)}) collective-permute-start(bf16[512,512]{1,0:T(8,128)(2,1)} %collective-permute-done.11.refs_7_), channel_id=1, source_target_pairs={{0,3},{1,0},{2,1},{3,2},{4,7},{5,4},{6,5},{7,6},{8,11},{9,8},{10,9... | collective-permute-start | bytes 1572872 | tf_op jit(solution)/shard_map/ppermute | solution.py:41
  110.7 14.2 %copy-start.6 = (bf16[512,512]{1,0:T(8,128)(2,1)S(1)}, bf16[512,512]{1,0:T(8,128)(2,1)}, u32[]{:S(2)}) copy-start(bf16[512,512]{1,0:T(8,128)(2,1)} %refs_0_.3) | copy-start | bytes 1572868
  110.7 17.6 %copy-start.17 = (bf16[1,64,512]{2,1,0:T(8,128)(2,1)S(1)}, bf16[1,64,512]{2,1,0:T(8,128)(2,1)}, u32[]{:S(2)}) copy-start(bf16[1,64,512]{2,1,0:T(8,128)(2,1)} %param.9) | copy-start | bytes 196612
  110.7 12.9 %collective-permute-start.20 = (f32[512,128]{0,1:T(8,128)S(1)}, f32[512,128]{0,1:T(8,128)S(1)}, u32[]{:S(2)}, u32[]{:S(2)}) collective-permute-start(f32[512,128]{0,1:T(8,128)S(1)} %add.337), channel_id=1, source_target_pairs={{0,8},{1,9},{2,10},{3,11},{4,12},{5,13},{6,14},{7,15},{8,0},{9,1},... | collective-permute-start | bytes 786440 | tf_op jit(solution)/shard_map/ppermute | solution.py:41
  112.6 11.0 %copy-start.16 = (f32[512,128]{0,1:T(8,128)S(1)}, f32[512,128]{0,1:T(8,128)}, u32[]{:S(2)}) copy-start(f32[512,128]{0,1:T(8,128)} %copy-done.15) | copy-start | bytes 786436
  118.7 10.2 %copy-start.2 = (bf16[1024,512]{1,0:T(8,128)(2,1)S(1)}, bf16[1024,512]{1,0:T(8,128)(2,1)}, u32[]{:S(2)}) copy-start(bf16[1024,512]{1,0:T(8,128)(2,1)} %copy-done.1) | copy-start | bytes 3145732
  118.7 10.2 %copy-start.4 = (bf16[1024,512]{1,0:T(8,128)(2,1)S(1)}, bf16[1024,512]{1,0:T(8,128)(2,1)}, u32[]{:S(2)}) copy-start(bf16[1024,512]{1,0:T(8,128)(2,1)} %copy-done.3) | copy-start | bytes 3145732
  118.7 10.2 %copy-start.11 = (s32[16]{0:T(128)S(1)}, s32[16]{0:T(128)}, u32[]{:S(2)}) copy-start(s32[16]{0:T(128)} %select_reduce_fusion.which_ref) | copy-start | bytes 196
  123.7 12.0 %collective-permute-start.22 = (bf16[1024,512]{1,0:T(8,128)(2,1)}, bf16[1024,512]{1,0:T(8,128)(2,1)}, u32[]{:S(2)}, u32[]{:S(2)}) collective-permute-start(bf16[1024,512]{1,0:T(8,128)(2,1)} %collective-permute-done.17.refs_14_), channel_id=1, source_target_pairs={{0,16},{1,17},{2,18},{3,19},{4,20},{5,21},{6,22},{7,23},{8,24},{9,... | collective-permute-start | bytes 3145736 | tf_op jit(solution)/shard_map/ppermute | solution.py:41
  124.8 4.1 %copy-start.8 = (bf16[512,512]{1,0:T(8,128)(2,1)S(1)}, bf16[512,512]{1,0:T(8,128)(2,1)}, u32[]{:S(2)}) copy-start(bf16[512,512]{1,0:T(8,128)(2,1)} %copy-done.7) | copy-start | bytes 1572868
  124.8 4.1 %copy-start.10 = (bf16[512,512]{1,0:T(8,128)(2,1)S(1)}, bf16[512,512]{1,0:T(8,128)(2,1)}, u32[]{:S(2)}) copy-start(bf16[512,512]{1,0:T(8,128)(2,1)} %copy-done.9) | copy-start | bytes 1572868
  126.0 9.7 %collective-permute-start.21 = (bf16[512,512]{1,0:T(8,128)(2,1)}, bf16[512,512]{1,0:T(8,128)(2,1)S(1)}, u32[]{:S(2)}, u32[]{:S(2)}) collective-permute-start(bf16[512,512]{1,0:T(8,128)(2,1)} %collective-permute-done.16.refs_8_), channel_id=1, source_target_pairs={{0,1},{1,2},{2,3},{3,0},{4,5},{5,6},{6,7},{7,4},{8,9},{9,10},{10,1... | collective-permute-start | bytes 1572872 | tf_op jit(solution)/shard_map/ppermute | solution.py:41

commit v6 on v5

--- a/solution.py
+++ b/solution.py
@@ -20,7 +20,7 @@
     ("b0", "b1", "+Z", "A13", "B13", "Rz1"),
     ("+X", "XA", "XB", "Z2", "+F", "F013", "Ry3"),
     ("XF", "A2", "B2", "+S", "S1", "Rz2"),
-    ("F2", "SF"),
+    ("F2", "SF", "Ry4"),
 )
 HELD = {"G": 0, "A0": 1, "B0": 1, "+Z": 1, "A13": 2, "B13": 2, "F013": 3, "Z2": 3, "A2": 4, "B2": 4, "F2": 5}
 WEIGHTS = {"+X": 2, "XA": 3, "XB": 3, "S1": 4, "XF": 4, "SF": 5}
@@ -227,6 +227,17 @@
     def add_from(dz, dy):
         return lambda v: v + swap(dz, dy)(v)
 
+    half = (y & 1) ^ (y >> 1)
+
+    def halved(v):
+        n = v.shape[0] // 2
+        rest = swap(0, 1)(lax.dynamic_slice_in_dim(v, (1 - half) * n, n))
+        return lax.dynamic_slice_in_dim(v, half * n, n) + rest
+
+    def doubled(v):
+        there = swap(0, 1)(v)
+        return jnp.where(half == 0, join(v, there), join(there, v))
+
     def on(v):
         return send(v, lambda x, zh, c, zl, y: (x, zh, c, zl, y + way(c)))
 
@@ -260,10 +271,11 @@
         "A2": (("Z2",), on),
         "B2": (("Z2",), back),
         "F2": (("A2",), on),
-        "Ry1": (("R",), add_from(0, 1)),
+        "Ry1": (("R",), halved),
         "Rz1": (("Ry1",), add_from(1, 0)),
         "Ry3": (("Rz1",), add_from(0, 3)),
         "Rz2": (("Ry3",), add_from(2, 0)),
+        "Ry4": (("Rz2",), doubled),
     }
     value = {"W": frozen_weight, "G": output_gradient, "R": rank_both}
     g_places, g_slots = [], []
@@ -323,7 +335,7 @@
             beside = [total]
         if number == 4:
             total, g_aside, w_aside = partial_sum(number, which, value, g_places, w_places, total)
-    adapter_part, down_gradient, up_gradient = ends(value["Rz2"])
+    adapter_part, down_gradient, up_gradient = ends(value["Ry4"])
     kept_column = kept.astype(jnp.float32)[:, None]
     grad_input = last_sum(which, value["F2"], value["SF"], g_aside, w_aside, total, kept_column, adapter_part)
     return (grad_input, down_gradient, up_gradient)

time: 139 us -> 137 us (0.986)
  waiting for transfers between devices: 68.4 us -> 62.3 us
  local copies, waits for them, and re-layouts: 1.2 us -> 4.14 us
    ppermute x23 -> x24, waiting for transfers between devices: 68.4 us -> 62.3 us  [send(): return lax.ppermute(value, AXES, moves(target))]
    unnamed x38 -> x36, local copies, waits for them, and re-layouts: 0.94 us -> 3.87 us
    ppermute x23 -> x24, starting transfers between devices: 42 us -> 42.7 us  [send(): return lax.ppermute(value, AXES, moves(target))]
  transfers between devices with their start and end apart: 23 -> 24, of which waited for: 9 -> 9; matrix products, arithmetic and copies ran while one was open for 7% -> 7% of each run, Pallas kernels for 9% -> 9%
where the time goes in v6:
time: 137 us; the launch traced here: 136 us
  waiting for transfers between devices  62.3 us (45%)
  starting transfers between devices  42.7 us (31%)
  Pallas kernels  15.9 us (12%)
  matrix products  5.29 us (4%)
  other arithmetic  4.17 us (3%)
  local copies, waits for them, and re-layouts  4.14 us (3%)
  between operations  1.68 us (1%)
    ppermute x24, waiting for transfers between devices, send(): return lax.ppermute(value, AXES, moves(target))  62.3 us
    ppermute x24, starting transfers between devices, send(): return lax.ppermute(value, AXES, moves(target))  42.7 us
    pallas_call x2, Pallas kernels, partial_sum(): pl.pallas_call(functools.partial(product_kernel, pairs, aside, len(g_name...  12.7 us
    unnamed x36, local copies, waits for them, and re-layouts  3.87 us
    concatenate x2, other arithmetic, join(): return jnp.concatenate(parts, axis=0)  3.31 us
    pallas_call x1, Pallas kernels, last_sum(): pl.pallas_call(last_kernel, out_shape=jax.ShapeDtypeStruct((rows, DIM), j...  3.21 us
  transfers between devices with their start and end apart: 24, of which 9 were waited for; matrix products, arithmetic and copies ran while one was open for 7% of the time, Pallas kernels for 9%

profile of v6, /device:TPU:1, one launch (start us, length us, event | category | flops | bytes accessed | tf_op | source)
XLA Modules:
  0.0 136.1 jit_solution(15821266434649631651)
XLA Ops:
  0.6 0.0 copy-start
  0.6 5.3 %collective-permute-start.4 = (bf16[512,512]{1,0:T(8,128)(2,1)}, bf16[512,512]{1,0:T(8,128)(2,1)S(1)}, u32[]{:S(2)}, u32[]{:S(2)}) collective-permute-start(bf16[512,512]{1,0:T(8,128)(2,1)} %refs_0_.3), channel_id=1, source_target_pairs={{0,12},{1,13},{2,14},{3,15},{4,0},{5,1},{6,2},{7,3},{8,4},{9,5},{1... | collective-permute-start | bytes 1572872 | tf_op jit(solution)/shard_map/ppermute | solution.py:41
  5.9 0.0 collective-permute-start.3
  5.9 1.3 collective-permute-start.2
  7.2 1.4 %collective-permute-start.1 = (bf16[512,512]{1,0:T(8,128)(2,1)}, bf16[512,512]{1,0:T(8,128)(2,1)S(1)}, u32[]{:S(2)}, u32[]{:S(2)}) collective-permute-start(bf16[512,512]{1,0:T(8,128)(2,1)} %refs_0_.3), channel_id=1, source_target_pairs={{0,1},{1,2},{2,3},{3,0},{4,5},{5,6},{6,7},{7,4},{8,9},{9,10},{10,1... | collective-permute-start | bytes 1572872 | tf_op jit(solution)/shard_map/ppermute | solution.py:41
  8.6 3.3 %collective-permute-start = (bf16[512,512]{1,0:T(8,128)(2,1)}, bf16[512,512]{1,0:T(8,128)(2,1)S(1)}, u32[]{:S(2)}, u32[]{:S(2)}) collective-permute-start(bf16[512,512]{1,0:T(8,128)(2,1)} %param.8), channel_id=1, source_target_pairs={{0,0},{1,16},{2,2},{3,18},{4,196},{5,84},{6,198},{7,86},{8,136},{9... | collective-permute-start | bytes 1572872 | tf_op jit(solution)/shard_map/ppermute | solution.py:41
  12.6 1.4 %fusion.3 = f32[512,64]{0,1:T(8,128)S(1)} fusion(bf16[512,512]{1,0:T(8,128)(2,1)} %refs_0_.3, bf16[512]{0:T(512)(128)(2,1)S(1)} %fusion.16, bf16[1,64,512]{2,1,0:T(8,128)(2,1)} %param.10), kind=kOutput, calls=%fused_computation.7 | convolution fusion | flops 33816576 | bytes 721920 | tf_op jit(solution)/shard_map/dot_general | solution.py:215
  14.0 1.1 fusion.12
  15.2 6.0 %collective-permute-done.1.refs_1_ = bf16[512,512]{1,0:T(8,128)(2,1)S(1)} collective-permute-done((bf16[512,512]{1,0:T(8,128)(2,1)}, bf16[512,512]{1,0:T(8,128)(2,1)S(1)}, u32[]{:S(2)}, u32[]{:S(2)}) %collective-permute-start.1) | collective-permute-done | bytes 524320 | tf_op jit(solution)/shard_map/ppermute | solution.py:41
  21.2 1.4 %collective-permute-start.5 = (f32[256,128]{0,1:T(8,128)S(1)}, f32[256,128]{0,1:T(8,128)S(1)}, u32[]{:S(2)}, u32[]{:S(2)}) collective-permute-start(f32[256,128]{0,1:T(8,128)S(1)} %constant_dynamic-slice_fusion), channel_id=1, source_target_pairs={{0,1},{1,0},{2,3},{3,2},{4,5},{5,4},{6,7},{7,6},{8,9},{9,8},{10,11... | collective-permute-start | bytes 393224 | tf_op jit(solution)/shard_map/ppermute | solution.py:41
  22.6 6.2 %collective-permute-done.3 = bf16[512,512]{1,0:T(8,128)(2,1)S(1)} collective-permute-done((bf16[512,512]{1,0:T(8,128)(2,1)}, bf16[512,512]{1,0:T(8,128)(2,1)S(1)}, u32[]{:S(2)}, u32[]{:S(2)}) %collective-permute-start.3) | collective-permute-done | bytes 524320 | tf_op jit(solution)/shard_map/ppermute | solution.py:41
  28.9 0.0 collective-permute-done.4
  29.0 0.0 copy-start.5
  29.0 0.0 collective-permute-done.5
  29.0 0.0 collective-permute-done
  29.0 0.0 collective-permute-done.2.refs_2_
  29.1 2.8 %collective-permute-start.8 = (bf16[1024,512]{1,0:T(8,128)(2,1)S(1)}, bf16[1024,512]{1,0:T(8,128)(2,1)S(1)}, u32[]{:S(2)}, u32[]{:S(2)}) collective-permute-start(bf16[1024,512]{1,0:T(8,128)(2,1)S(1)} %constant_dynamic-update-slice_fusion.refs_3_), channel_id=1, source_target_pairs={{0,1},{1,2},{2,3},{3,0},{4,5},{5,6},{6,7},{7,4},{8,9},{9,10},{10,1... | collective-permute-start | bytes 3145736 | tf_op jit(solution)/shard_map/ppermute | solution.py:41
  31.9 0.7 collective-permute-start.6
  32.6 1.4 %collective-permute-start.10 = (f32[256,128]{0,1:T(8,128)S(1)}, f32[256,128]{0,1:T(8,128)S(1)}, u32[]{:S(2)}, u32[]{:S(2)}) collective-permute-start(f32[256,128]{0,1:T(8,128)S(1)} %dynamic-slice_add_fusion), channel_id=1, source_target_pairs={{0,4},{1,5},{2,6},{3,7},{4,0},{5,1},{6,2},{7,3},{8,12},{9,13},{10,... | collective-permute-start | bytes 393224 | tf_op jit(solution)/shard_map/ppermute | solution.py:41
  34.0 7.9 %collective-permute-start.7 = (bf16[512,512]{1,0:T(8,128)(2,1)S(1)}, bf16[512,512]{1,0:T(8,128)(2,1)S(1)}, u32[]{:S(2)}, u32[]{:S(2)}) collective-permute-start(bf16[512,512]{1,0:T(8,128)(2,1)S(1)} %collective-permute-done), channel_id=1, source_target_pairs={{0,32},{1,33},{2,0},{3,1},{4,36},{5,37},{6,4},{7,5},{8,40},{9,41},... | collective-permute-start | bytes 1572872 | tf_op jit(solution)/shard_map/ppermute | solution.py:41
  41.9 0.0 collective-permute-done.10
  42.0 0.0 collective-permute-done.6
  42.0 22.0 %collective-permute-done.8.refs_4_ = bf16[1024,512]{1,0:T(8,128)(2,1)S(1)} collective-permute-done((bf16[1024,512]{1,0:T(8,128)(2,1)S(1)}, bf16[1024,512]{1,0:T(8,128)(2,1)S(1)}, u32[]{:S(2)}, u32[]{:S(2)}) %collective-permute-start.8) | collective-permute-done | bytes 1048608 | tf_op jit(solution)/shard_map/ppermute | solution.py:41
  64.0 0.1 pad_maximum_fusion.1
  64.1 3.0 %collective-permute-done.7 = bf16[512,512]{1,0:T(8,128)(2,1)S(1)} collective-permute-done((bf16[512,512]{1,0:T(8,128)(2,1)S(1)}, bf16[512,512]{1,0:T(8,128)(2,1)S(1)}, u32[]{:S(2)}, u32[]{:S(2)}) %collective-permute-start.7) | collective-permute-done | bytes 524320 | tf_op jit(solution)/shard_map/ppermute | solution.py:41
  67.1 0.0 collective-permute-done.9.refs_5_
  67.1 0.5 collective-permute-start.14
  67.6 0.5 copy-done.15
  68.2 3.6 %collective-permute-start.13 = (bf16[1024,512]{1,0:T(8,128)(2,1)S(1)}, bf16[1024,512]{1,0:T(8,128)(2,1)S(1)}, u32[]{:S(2)}, u32[]{:S(2)}) collective-permute-start(bf16[1024,512]{1,0:T(8,128)(2,1)S(1)} %constant_dynamic-update-slice_fusion.2.refs_8_.refs_10_), channel_id=1, source_target_pairs={{0,192},{1,193},{2,194},{3,195},{4,196},{5,197},{6,198},{7,199},{8... | collective-permute-start | bytes 3145736 | tf_op jit(solution)/shard_map/ppermute | solution.py:41
  71.8 3.4 %collective-permute-start.12 = (bf16[1024,512]{1,0:T(8,128)(2,1)S(1)}, bf16[1024,512]{1,0:T(8,128)(2,1)}, u32[]{:S(2)}, u32[]{:S(2)}) collective-permute-start(bf16[1024,512]{1,0:T(8,128)(2,1)S(1)} %constant_dynamic-update-slice_fusion.2.refs_8_.refs_10_), channel_id=1, source_target_pairs={{0,64},{1,65},{2,66},{3,67},{4,68},{5,69},{6,70},{7,71},{8,72},{9,... | collective-permute-start | bytes 3145736 | tf_op jit(solution)/shard_map/ppermute | solution.py:41
  75.2 0.0 collective-permute-start.15
  75.2 1.6 %collective-permute-start.11 = (bf16[512,512]{1,0:T(8,128)(2,1)S(1)}, bf16[512,512]{1,0:T(8,128)(2,1)}, u32[]{:S(2)}, u32[]{:S(2)}) collective-permute-start(bf16[512,512]{1,0:T(8,128)(2,1)S(1)} %copy-done.5), channel_id=1, source_target_pairs={{0,8},{1,9},{2,10},{3,11},{4,12},{5,13},{6,14},{7,15},{8,0},{9,1},... | collective-permute-start | bytes 1572872 | tf_op jit(solution)/shard_map/ppermute | solution.py:41
  76.9 11.0 %collective-permute-done.15 = f32[256,128]{0,1:T(8,128)S(1)} collective-permute-done((f32[256,128]{0,1:T(8,128)S(1)}, f32[256,128]{0,1:T(8,128)S(1)}, u32[]{:S(2)}, u32[]{:S(2)}) %collective-permute-start.15) | collective-permute-done | bytes 131104 | tf_op jit(solution)/shard_map/ppermute | solution.py:41
  87.8 10.8 %collective-permute-done.13.refs_10_.refs_12_ = bf16[1024,512]{1,0:T(8,128)(2,1)S(1)} collective-permute-done((bf16[1024,512]{1,0:T(8,128)(2,1)S(1)}, bf16[1024,512]{1,0:T(8,128)(2,1)S(1)}, u32[]{:S(2)}, u32[]{:S(2)}) %collective-permute-start.13) | collective-permute-done | bytes 1048608 | tf_op jit(solution)/shard_map/ppermute | solution.py:41
  98.7 0.0 collective-permute-done.12.refs_9_.refs_11_
  98.7 3.2 %pad_maximum_fusion = bf16[3072,512]{1,0:T(8,128)(2,1)} fusion(bf16[1024,512]{1,0:T(8,128)(2,1)S(1)} %collective-permute-done.13.refs_10_.refs_12_, bf16[1024,512]{1,0:T(8,128)(2,1)} %collective-permute-done.12.refs_9_.refs_11_, bf16[512,512]{1,0:T(8,128)(2,1)S(1)} %collective-permute-done.7, bf16[512,512]{1,0:T(8,128)(2,1)S(1)} %collective-permute-done.6), kind=kLoop, calls=%fused_computation | loop fusion | flops 12582912 | bytes 6291456 | tf_op jit(solution)/shard_map/concatenate | solution.py:222
  101.9 0.0 collective-permute-done.11.refs_7_
  101.9 1.2 copy-done.14
  103.1 0.3 collective-permute-start.19
  103.4 0.6 collective-permute-start.17
  104.0 0.9 collective-permute-start.18
  104.8 1.8 %collective-permute-start.16 = (bf16[512,512]{1,0:T(8,128)(2,1)}, bf16[512,512]{1,0:T(8,128)(2,1)}, u32[]{:S(2)}, u32[]{:S(2)}) collective-permute-start(bf16[512,512]{1,0:T(8,128)(2,1)} %collective-permute-done.11.refs_7_), channel_id=1, source_target_pairs={{0,1},{1,2},{2,3},{3,0},{4,5},{5,6},{6,7},{7,4},{8,9},{9,10},{10,1... | collective-permute-start | bytes 1572872 | tf_op jit(solution)/shard_map/ppermute | solution.py:41
  106.7 0.1 stack.118
  106.7 0.1 stack.135
  106.8 0.7 select_reduce_fusion.which_ref
  107.6 1.7 %collective-permute-start.20 = (f32[256,128]{0,1:T(8,128)S(1)}, f32[256,128]{0,1:T(8,128)S(1)}, u32[]{:S(2)}, u32[]{:S(2)}) collective-permute-start(f32[256,128]{0,1:T(8,128)S(1)} %add.345), channel_id=1, source_target_pairs={{0,8},{1,9},{2,10},{3,11},{4,12},{5,13},{6,14},{7,15},{8,0},{9,1},... | collective-permute-start | bytes 393224 | tf_op jit(solution)/shard_map/ppermute | solution.py:41
  109.3 5.9 %shard_map.85.refs_15_ = f32[512,512]{1,0:T(8,128)} custom-call(s32[16]{0:T(128)} %select_reduce_fusion.which_ref, bf16[512,512]{1,0:T(8,128)(2,1)} %refs_0_.3, bf16[512,512]{1,0:T(8,128)(2,1)} %copy-done.7, bf16[512,512]{1,0:T(8,128)(2,1)} %copy-done.9, bf16[1024,512]{1,0:T(8,128)(2,1)} %copy-done.3, bf16[1024,512]{1,0:T(8,128)(2,1)} %copy-done.1, ...), custom_call_target="tpu_custom_call" | custom-call | flops 4294967296 | bytes 16777216 | tf_op jit(solution)/shard_map/pallas_call | solution.py:170
  115.2 0.9 collective-permute-done.20
  116.2 1.9 %collective-permute-done.18.refs_9_ = bf16[512,512]{1,0:T(8,128)(2,1)} collective-permute-done((bf16[512,512]{1,0:T(8,128)(2,1)}, bf16[512,512]{1,0:T(8,128)(2,1)}, u32[]{:S(2)}, u32[]{:S(2)}) %collective-permute-start.18) | collective-permute-done | bytes 524320 | tf_op jit(solution)/shard_map/ppermute | solution.py:41
  118.0 0.4 collective-permute-done.16.refs_8_
  118.5 1.4 %collective-permute-start.22 = (bf16[1024,512]{1,0:T(8,128)(2,1)}, bf16[1024,512]{1,0:T(8,128)(2,1)}, u32[]{:S(2)}, u32[]{:S(2)}) collective-permute-start(bf16[1024,512]{1,0:T(8,128)(2,1)} %collective-permute-done.17.refs_14_), channel_id=1, source_target_pairs={{0,16},{1,17},{2,18},{3,19},{4,20},{5,21},{6,22},{7,23},{8,24},{9,... | collective-permute-start | bytes 3145736 | tf_op jit(solution)/shard_map/ppermute | solution.py:41
  120.0 0.0 copy-start.16
  120.0 0.3 collective-permute-start.23
  120.3 0.9 collective-permute-start.21
  121.2 0.0 copy-start.8
  121.2 1.0 copy-done.8
  122.3 1.0 copy-done.10
  123.3 6.7 %shard_map.86 = (f32[512,512]{1,0:T(8,128)S(1)}, bf16[2,512,512]{2,1,0:T(8,128)(2,1)S(1)}, bf16[512,512]{1,0:T(8,128)(2,1)S(1)}) custom-call(s32[16]{0:T(128)S(1)} %copy-done.11, bf16[512,512]{1,0:T(8,128)(2,1)S(1)} %copy-done.6, bf16[512,512]{1,0:T(8,128)(2,1)S(1)} %copy-done.8, bf16[512,512]{1,0:T(8,128)(2,1)S(1)} %copy-done.10, ...), custom_call_target="tpu_custom_call" | custom-call | flops 2147483648 | bytes 8388608 | tf_op jit(solution)/shard_map/pallas_call | solution.py:170
  130.1 0.0 collective-permute-done.23
  130.1 1.0 fusion.1
  131.1 1.1 fusion
  132.3 0.6 fusion.9.add_ref
  132.9 0.0 collective-permute-done.21.g_ref
  132.9 3.2 %shard_map.87 = bf16[512,512]{1,0:T(8,128)(2,1)} custom-call(s32[16]{0:T(128)S(1)} %copy-done.11, bf16[512,512]{1,0:T(8,128)(2,1)S(1)} %collective-permute-done.21.g_ref, bf16[1024,512]{1,0:T(8,128)(2,1)} %collective-permute-done.22.w_ref, bf16[2,512,512]{2,1,0:T(8,128)(2,1)S(1)} %get-tuple-element.35.g_aside, ...), custom_call_target="tpu_custom_call" | custom-call | flops 805306368 | bytes 3145728 | tf_op jit(solution)/shard_map/pallas_call | solution.py:192
  (44 shorter events, 0.4 us)
Async XLA Ops:
  0.6 13.4 %copy-start = (bf16[512,512]{1,0:T(8,128)(2,1)S(1)}, bf16[512,512]{1,0:T(8,128)(2,1)}, u32[]{:S(2)}) copy-start(bf16[512,512]{1,0:T(8,128)(2,1)} %param.6) | copy-start | bytes 1572868
  0.6 28.3 %collective-permute-start.4 = (bf16[512,512]{1,0:T(8,128)(2,1)}, bf16[512,512]{1,0:T(8,128)(2,1)S(1)}, u32[]{:S(2)}, u32[]{:S(2)}) collective-permute-start(bf16[512,512]{1,0:T(8,128)(2,1)} %refs_0_.3), channel_id=1, source_target_pairs={{0,12},{1,13},{2,14},{3,15},{4,0},{5,1},{6,2},{7,3},{8,4},{9,5},{1... | collective-permute-start | bytes 1572872 | tf_op jit(solution)/shard_map/ppermute | solution.py:41
  5.9 23.0 %collective-permute-start.3 = (bf16[512,512]{1,0:T(8,128)(2,1)}, bf16[512,512]{1,0:T(8,128)(2,1)S(1)}, u32[]{:S(2)}, u32[]{:S(2)}) collective-permute-start(bf16[512,512]{1,0:T(8,128)(2,1)} %refs_0_.3), channel_id=1, source_target_pairs={{0,4},{1,5},{2,6},{3,7},{4,8},{5,9},{6,10},{7,11},{8,12},{9,13},{1... | collective-permute-start | bytes 1572872 | tf_op jit(solution)/shard_map/ppermute | solution.py:41
  5.9 23.1 %collective-permute-start.2 = (bf16[512,512]{1,0:T(8,128)(2,1)}, bf16[512,512]{1,0:T(8,128)(2,1)S(1)}, u32[]{:S(2)}, u32[]{:S(2)}) collective-permute-start(bf16[512,512]{1,0:T(8,128)(2,1)} %refs_0_.3), channel_id=1, source_target_pairs={{0,3},{1,0},{2,1},{3,2},{4,7},{5,4},{6,5},{7,6},{8,11},{9,8},{10,9... | collective-permute-start | bytes 1572872 | tf_op jit(solution)/shard_map/ppermute | solution.py:41
  7.2 14.0 %collective-permute-start.1 = (bf16[512,512]{1,0:T(8,128)(2,1)}, bf16[512,512]{1,0:T(8,128)(2,1)S(1)}, u32[]{:S(2)}, u32[]{:S(2)}) collective-permute-start(bf16[512,512]{1,0:T(8,128)(2,1)} %refs_0_.3), channel_id=1, source_target_pairs={{0,1},{1,2},{2,3},{3,0},{4,5},{5,6},{6,7},{7,4},{8,9},{9,10},{10,1... | collective-permute-start | bytes 1572872 | tf_op jit(solution)/shard_map/ppermute | solution.py:41
  8.6 20.4 %collective-permute-start = (bf16[512,512]{1,0:T(8,128)(2,1)}, bf16[512,512]{1,0:T(8,128)(2,1)S(1)}, u32[]{:S(2)}, u32[]{:S(2)}) collective-permute-start(bf16[512,512]{1,0:T(8,128)(2,1)} %param.8), channel_id=1, source_target_pairs={{0,0},{1,16},{2,2},{3,18},{4,196},{5,84},{6,198},{7,86},{8,136},{9... | collective-permute-start | bytes 1572872 | tf_op jit(solution)/shard_map/ppermute | solution.py:41
  21.2 42.9 %copy-start.7 = (bf16[512,512]{1,0:T(8,128)(2,1)}, bf16[512,512]{1,0:T(8,128)(2,1)S(1)}, u32[]{:S(2)}) copy-start(bf16[512,512]{1,0:T(8,128)(2,1)S(1)} %collective-permute-done.1.refs_1_) | copy-start | bytes 1572868
  21.2 7.8 %collective-permute-start.5 = (f32[256,128]{0,1:T(8,128)S(1)}, f32[256,128]{0,1:T(8,128)S(1)}, u32[]{:S(2)}, u32[]{:S(2)}) collective-permute-start(f32[256,128]{0,1:T(8,128)S(1)} %constant_dynamic-slice_fusion), channel_id=1, source_target_pairs={{0,1},{1,0},{2,3},{3,2},{4,5},{5,4},{6,7},{7,6},{8,9},{9,8},{10,11... | collective-permute-start | bytes 393224 | tf_op jit(solution)/shard_map/ppermute | solution.py:41
  29.0 58.9 %copy-start.3 = (bf16[1024,512]{1,0:T(8,128)(2,1)}, bf16[1024,512]{1,0:T(8,128)(2,1)S(1)}, u32[]{:S(2)}) copy-start(bf16[1024,512]{1,0:T(8,128)(2,1)S(1)} %constant_dynamic-update-slice_fusion.refs_3_) | copy-start | bytes 3145732
  29.0 46.2 %copy-start.5 = (bf16[512,512]{1,0:T(8,128)(2,1)S(1)}, bf16[512,512]{1,0:T(8,128)(2,1)}, u32[]{:S(2)}) copy-start(bf16[512,512]{1,0:T(8,128)(2,1)} %refs_0_.3) | copy-start | bytes 1572868
  29.1 72.8 %copy-start.9 = (bf16[512,512]{1,0:T(8,128)(2,1)}, bf16[512,512]{1,0:T(8,128)(2,1)S(1)}, u32[]{:S(2)}) copy-start(bf16[512,512]{1,0:T(8,128)(2,1)S(1)} %collective-permute-done.2.refs_2_) | copy-start | bytes 1572868
  29.1 34.9 %collective-permute-start.8 = (bf16[1024,512]{1,0:T(8,128)(2,1)S(1)}, bf16[1024,512]{1,0:T(8,128)(2,1)S(1)}, u32[]{:S(2)}, u32[]{:S(2)}) collective-permute-start(bf16[1024,512]{1,0:T(8,128)(2,1)S(1)} %constant_dynamic-update-slice_fusion.refs_3_), channel_id=1, source_target_pairs={{0,1},{1,2},{2,3},{3,0},{4,5},{5,6},{6,7},{7,4},{8,9},{9,10},{10,1... | collective-permute-start | bytes 3145736 | tf_op jit(solution)/shard_map/ppermute | solution.py:41
  31.9 35.3 %collective-permute-start.9 = (bf16[1024,512]{1,0:T(8,128)(2,1)S(1)}, bf16[1024,512]{1,0:T(8,128)(2,1)S(1)}, u32[]{:S(2)}, u32[]{:S(2)}) collective-permute-start(bf16[1024,512]{1,0:T(8,128)(2,1)S(1)} %constant_dynamic-update-slice_fusion.refs_3_), channel_id=1, source_target_pairs={{0,3},{1,0},{2,1},{3,2},{4,7},{5,4},{6,5},{7,6},{8,11},{9,8},{10,9... | collective-permute-start | bytes 3145736 | tf_op jit(solution)/shard_map/ppermute | solution.py:41
  31.9 10.1 %collective-permute-start.6 = (bf16[512,512]{1,0:T(8,128)(2,1)S(1)}, bf16[512,512]{1,0:T(8,128)(2,1)S(1)}, u32[]{:S(2)}, u32[]{:S(2)}) collective-permute-start(bf16[512,512]{1,0:T(8,128)(2,1)S(1)} %collective-permute-done), channel_id=1, source_target_pairs={{0,0},{1,1},{2,32},{3,33},{4,4},{5,5},{6,36},{7,37},{8,8},{9,9},{1... | collective-permute-start | bytes 1572872 | tf_op jit(solution)/shard_map/ppermute | solution.py:41
  32.6 9.4 %collective-permute-start.10 = (f32[256,128]{0,1:T(8,128)S(1)}, f32[256,128]{0,1:T(8,128)S(1)}, u32[]{:S(2)}, u32[]{:S(2)}) collective-permute-start(f32[256,128]{0,1:T(8,128)S(1)} %dynamic-slice_add_fusion), channel_id=1, source_target_pairs={{0,4},{1,5},{2,6},{3,7},{4,0},{5,1},{6,2},{7,3},{8,12},{9,13},{10,... | collective-permute-start | bytes 393224 | tf_op jit(solution)/shard_map/ppermute | solution.py:41
  34.0 33.1 %collective-permute-start.7 = (bf16[512,512]{1,0:T(8,128)(2,1)S(1)}, bf16[512,512]{1,0:T(8,128)(2,1)S(1)}, u32[]{:S(2)}, u32[]{:S(2)}) collective-permute-start(bf16[512,512]{1,0:T(8,128)(2,1)S(1)} %collective-permute-done), channel_id=1, source_target_pairs={{0,32},{1,33},{2,0},{3,1},{4,36},{5,37},{6,4},{7,5},{8,40},{9,41},... | collective-permute-start | bytes 1572872 | tf_op jit(solution)/shard_map/ppermute | solution.py:41
  64.0 37.9 %copy-start.1 = (bf16[1024,512]{1,0:T(8,128)(2,1)}, bf16[1024,512]{1,0:T(8,128)(2,1)S(1)}, u32[]{:S(2)}) copy-start(bf16[1024,512]{1,0:T(8,128)(2,1)S(1)} %collective-permute-done.8.refs_4_) | copy-start | bytes 3145732
  67.1 1.0 copy-start.15
  67.1 34.8 %collective-permute-start.14 = (bf16[1536,512]{1,0:T(8,128)(2,1)S(1)}, bf16[1536,512]{1,0:T(8,128)(2,1)S(1)}, u32[]{:S(2)}, u32[]{:S(2)}) collective-permute-start(bf16[1536,512]{1,0:T(8,128)(2,1)S(1)} %pad_maximum_fusion.1), channel_id=1, source_target_pairs={{0,1},{1,2},{2,3},{3,0},{4,5},{5,6},{6,7},{7,4},{8,9},{9,10},{10,1... | collective-permute-start | bytes 4718600 | tf_op jit(solution)/shard_map/ppermute | solution.py:41
  68.2 30.5 %copy-start.13 = (bf16[1024,512]{1,0:T(8,128)(2,1)}, bf16[1024,512]{1,0:T(8,128)(2,1)S(1)}, u32[]{:S(2)}) copy-start(bf16[1024,512]{1,0:T(8,128)(2,1)S(1)} %constant_dynamic-update-slice_fusion.2.refs_8_.refs_10_) | copy-start | bytes 3145732
  68.2 30.5 %collective-permute-start.13 = (bf16[1024,512]{1,0:T(8,128)(2,1)S(1)}, bf16[1024,512]{1,0:T(8,128)(2,1)S(1)}, u32[]{:S(2)}, u32[]{:S(2)}) collective-permute-start(bf16[1024,512]{1,0:T(8,128)(2,1)S(1)} %constant_dynamic-update-slice_fusion.2.refs_8_.refs_10_), channel_id=1, source_target_pairs={{0,192},{1,193},{2,194},{3,195},{4,196},{5,197},{6,198},{7,199},{8... | collective-permute-start | bytes 3145736 | tf_op jit(solution)/shard_map/ppermute | solution.py:41
  71.8 26.8 %collective-permute-start.12 = (bf16[1024,512]{1,0:T(8,128)(2,1)S(1)}, bf16[1024,512]{1,0:T(8,128)(2,1)}, u32[]{:S(2)}, u32[]{:S(2)}) collective-permute-start(bf16[1024,512]{1,0:T(8,128)(2,1)S(1)} %constant_dynamic-update-slice_fusion.2.refs_8_.refs_10_), channel_id=1, source_target_pairs={{0,64},{1,65},{2,66},{3,67},{4,68},{5,69},{6,70},{7,71},{8,72},{9,... | collective-permute-start | bytes 3145736 | tf_op jit(solution)/shard_map/ppermute | solution.py:41
  75.2 12.6 %collective-permute-start.15 = (f32[256,128]{0,1:T(8,128)S(1)}, f32[256,128]{0,1:T(8,128)S(1)}, u32[]{:S(2)}, u32[]{:S(2)}) collective-permute-start(f32[256,128]{0,1:T(8,128)S(1)} %add.344), channel_id=1, source_target_pairs={{0,3},{1,2},{2,1},{3,0},{4,7},{5,6},{6,5},{7,4},{8,11},{9,10},{10,... | collective-permute-start | bytes 393224 | tf_op jit(solution)/shard_map/ppermute | solution.py:41
  75.2 26.7 %collective-permute-start.11 = (bf16[512,512]{1,0:T(8,128)(2,1)S(1)}, bf16[512,512]{1,0:T(8,128)(2,1)}, u32[]{:S(2)}, u32[]{:S(2)}) collective-permute-start(bf16[512,512]{1,0:T(8,128)(2,1)S(1)} %copy-done.5), channel_id=1, source_target_pairs={{0,8},{1,9},{2,10},{3,11},{4,12},{5,13},{6,14},{7,15},{8,0},{9,1},... | collective-permute-start | bytes 1572872 | tf_op jit(solution)/shard_map/ppermute | solution.py:41
  98.6 3.2 %copy-start.12 = (bf16[1024,512]{1,0:T(8,128)(2,1)}, bf16[1024,512]{1,0:T(8,128)(2,1)S(1)}, u32[]{:S(2)}) copy-start(bf16[1024,512]{1,0:T(8,128)(2,1)S(1)} %collective-permute-done.13.refs_10_.refs_12_) | copy-start | bytes 3145732
  101.9 1.2 copy-start.14
  103.1 15.4 %collective-permute-start.19 = (bf16[3072,512]{1,0:T(8,128)(2,1)}, bf16[3072,512]{1,0:T(8,128)(2,1)}, u32[]{:S(2)}, u32[]{:S(2)}) collective-permute-start(bf16[3072,512]{1,0:T(8,128)(2,1)} %pad_maximum_fusion), channel_id=1, source_target_pairs={{0,16},{1,17},{2,18},{3,19},{4,20},{5,21},{6,22},{7,23},{8,24},{9,... | collective-permute-start | bytes 9437192 | tf_op jit(solution)/shard_map/ppermute | solution.py:41
  103.4 15.1 %collective-permute-start.17 = (bf16[1024,512]{1,0:T(8,128)(2,1)}, bf16[1024,512]{1,0:T(8,128)(2,1)}, u32[]{:S(2)}, u32[]{:S(2)}) collective-permute-start(bf16[1024,512]{1,0:T(8,128)(2,1)} %collective-permute-done.12.refs_9_.refs_11_), channel_id=1, source_target_pairs={{0,64},{1,65},{2,66},{3,67},{4,68},{5,69},{6,70},{7,71},{8,72},{9,... | collective-permute-start | bytes 3145736 | tf_op jit(solution)/shard_map/ppermute | solution.py:41
  104.0 14.1 %collective-permute-start.18 = (bf16[512,512]{1,0:T(8,128)(2,1)}, bf16[512,512]{1,0:T(8,128)(2,1)}, u32[]{:S(2)}, u32[]{:S(2)}) collective-permute-start(bf16[512,512]{1,0:T(8,128)(2,1)} %collective-permute-done.11.refs_7_), channel_id=1, source_target_pairs={{0,3},{1,0},{2,1},{3,2},{4,7},{5,4},{6,5},{7,6},{8,11},{9,8},{10,9... | collective-permute-start | bytes 1572872 | tf_op jit(solution)/shard_map/ppermute | solution.py:41
  104.8 13.6 %collective-permute-start.16 = (bf16[512,512]{1,0:T(8,128)(2,1)}, bf16[512,512]{1,0:T(8,128)(2,1)}, u32[]{:S(2)}, u32[]{:S(2)}) collective-permute-start(bf16[512,512]{1,0:T(8,128)(2,1)} %collective-permute-done.11.refs_7_), channel_id=1, source_target_pairs={{0,1},{1,2},{2,3},{3,0},{4,5},{5,6},{6,7},{7,4},{8,9},{9,10},{10,1... | collective-permute-start | bytes 1572872 | tf_op jit(solution)/shard_map/ppermute | solution.py:41
  107.5 13.7 %copy-start.2 = (bf16[1024,512]{1,0:T(8,128)(2,1)S(1)}, bf16[1024,512]{1,0:T(8,128)(2,1)}, u32[]{:S(2)}) copy-start(bf16[1024,512]{1,0:T(8,128)(2,1)} %copy-done.1) | copy-start | bytes 3145732
  107.6 13.7 %copy-start.4 = (bf16[1024,512]{1,0:T(8,128)(2,1)S(1)}, bf16[1024,512]{1,0:T(8,128)(2,1)}, u32[]{:S(2)}) copy-start(bf16[1024,512]{1,0:T(8,128)(2,1)} %copy-done.3) | copy-start | bytes 3145732
  107.6 13.7 %copy-start.6 = (bf16[512,512]{1,0:T(8,128)(2,1)S(1)}, bf16[512,512]{1,0:T(8,128)(2,1)}, u32[]{:S(2)}) copy-start(bf16[512,512]{1,0:T(8,128)(2,1)} %refs_0_.3) | copy-start | bytes 1572868
  107.6 13.7 %copy-start.11 = (s32[16]{0:T(128)S(1)}, s32[16]{0:T(128)}, u32[]{:S(2)}) copy-start(s32[16]{0:T(128)} %select_reduce_fusion.which_ref) | copy-start | bytes 196
  107.6 8.6 %collective-permute-start.20 = (f32[256,128]{0,1:T(8,128)S(1)}, f32[256,128]{0,1:T(8,128)S(1)}, u32[]{:S(2)}, u32[]{:S(2)}) collective-permute-start(f32[256,128]{0,1:T(8,128)S(1)} %add.345), channel_id=1, source_target_pairs={{0,8},{1,9},{2,10},{3,11},{4,12},{5,13},{6,14},{7,15},{8,0},{9,1},... | collective-permute-start | bytes 393224 | tf_op jit(solution)/shard_map/ppermute | solution.py:41
  118.5 14.4 %collective-permute-start.22 = (bf16[1024,512]{1,0:T(8,128)(2,1)}, bf16[1024,512]{1,0:T(8,128)(2,1)}, u32[]{:S(2)}, u32[]{:S(2)}) collective-permute-start(bf16[1024,512]{1,0:T(8,128)(2,1)} %collective-permute-done.17.refs_14_), channel_id=1, source_target_pairs={{0,16},{1,17},{2,18},{3,19},{4,20},{5,21},{6,22},{7,23},{8,24},{9,... | collective-permute-start | bytes 3145736 | tf_op jit(solution)/shard_map/ppermute | solution.py:41
  120.0 12.3 %copy-start.16 = (bf16[1,64,512]{2,1,0:T(8,128)(2,1)S(1)}, bf16[1,64,512]{2,1,0:T(8,128)(2,1)}, u32[]{:S(2)}) copy-start(bf16[1,64,512]{2,1,0:T(8,128)(2,1)} %param.9) | copy-start | bytes 196612
  120.0 10.1 %collective-permute-start.23 = (f32[256,128]{0,1:T(8,128)S(1)}, f32[256,128]{0,1:T(8,128)S(1)}, u32[]{:S(2)}, u32[]{:S(2)}) collective-permute-start(f32[256,128]{0,1:T(8,128)S(1)} %add.346), channel_id=1, source_target_pairs={{0,1},{1,0},{2,3},{3,2},{4,5},{5,4},{6,7},{7,6},{8,9},{9,8},{10,11... | collective-permute-start | bytes 393224 | tf_op jit(solution)/shard_map/ppermute | solution.py:41
  120.3 12.6 %collective-permute-start.21 = (bf16[512,512]{1,0:T(8,128)(2,1)}, bf16[512,512]{1,0:T(8,128)(2,1)S(1)}, u32[]{:S(2)}, u32[]{:S(2)}) collective-permute-start(bf16[512,512]{1,0:T(8,128)(2,1)} %collective-permute-done.16.refs_8_), channel_id=1, source_target_pairs={{0,1},{1,2},{2,3},{3,0},{4,5},{5,6},{6,7},{7,4},{8,9},{9,10},{10,1... | collective-permute-start | bytes 1572872 | tf_op jit(solution)/shard_map/ppermute | solution.py:41
  121.2 1.0 copy-start.8
  122.3 1.0 copy-start.10

commit v7 on v6

--- a/solution.py
+++ b/solution.py
@@ -221,6 +221,12 @@
     def join(*parts):
         return jnp.concatenate(parts, axis=0)
 
+    def in_turn(*parts):
+        whole = jnp.zeros((sum(p.shape[0] for p in parts), parts[0].shape[1]), parts[0].dtype)
+        for i, part in enumerate(parts):
+            whole = lax.dynamic_update_slice(whole, part, (i * part.shape[0], 0))
+        return whole
+
     def swap(dz, dy):
         return lambda v: send(v, lambda x, zh, c, zl, y: (x, zh, c, zl ^ dz, y ^ dy))
 
@@ -255,7 +261,7 @@
         "XA": (("+X",), lambda v: send(v, lambda x, zh, c, zl, y: (x + way(c), zh, c, zl, y))),
         "XB": (("+X",), lambda v: send(v, lambda x, zh, c, zl, y: (x - way(c), zh, c, zl, y))),
         "XF": (("XA",), lambda v: send(v, lambda x, zh, c, zl, y: (x + way(c), zh, c, zl, y))),
-        "+S": (("+X", "XA", "XB"), join),
+        "+S": (("+X", "XA", "XB"), in_turn),
         "S1": (("+S",), sibling),
         "SF": (("XF",), sibling),
         "Z1": (("G",), lambda v: send(v, lambda x, zh, c, zl, y: (x, zh, c, zl + 1, y))),

time: 137 us -> 138 us (level)
  local copies, waits for them, and re-layouts: 4.14 us -> 10.2 us
  starting transfers between devices: 42.7 us -> 37.5 us
  waiting for transfers between devices: 62.3 us -> 65.7 us
  other arithmetic: 4.17 us -> 0.95 us
    dynamic_update_slice x0 -> x3, local copies, waits for them, and re-layouts: none -> 5.36 us  [in_turn(): whole = lax.dynamic_update_slice(whole, part, (i * part.shape[0], 0))]
    ppermute x24, starting transfers between devices: 42.7 us -> 37.5 us  [send(): return lax.ppermute(value, AXES, moves(target))]
    ppermute x24, waiting for transfers between devices: 62.3 us -> 65.7 us  [send(): return lax.ppermute(value, AXES, moves(target))]
    concatenate x2 -> x1, other arithmetic: 3.31 us -> 0.1 us  [join(): return jnp.concatenate(parts, axis=0)]
  transfers between devices with their start and end apart: 24 -> 24, of which waited for: 9 -> 9; matrix products, arithmetic and copies ran while one was open for 7% -> 9% of each run, Pallas kernels for 9% -> 9%
where the time goes in v7:
time: 138 us; the launch traced here: 137 us
  waiting for transfers between devices  65.7 us (48%)
  starting transfers between devices  37.5 us (27%)
  Pallas kernels  16 us (12%)
  local copies, waits for them, and re-layouts  10.2 us (7%)
  matrix products  5.29 us (4%)
  between operations  1.65 us (1%)
    ppermute x24, waiting for transfers between devices, send(): return lax.ppermute(value, AXES, moves(target))  65.7 us
    ppermute x24, starting transfers between devices, send(): return lax.ppermute(value, AXES, moves(target))  37.5 us
    pallas_call x2, Pallas kernels, partial_sum(): pl.pallas_call(functools.partial(product_kernel, pairs, aside, len(g_name...  12.8 us
    dynamic_update_slice x3, local copies, waits for them, and re-layouts, in_turn(): whole = lax.dynamic_update_slice(whole, part, (i * part.shape[0], 0))  5.36 us
    unnamed x36, local copies, waits for them, and re-layouts  4.54 us
    pallas_call x1, Pallas kernels, last_sum(): pl.pallas_call(last_kernel, out_shape=jax.ShapeDtypeStruct((rows, DIM), j...  3.21 us
  transfers between devices with their start and end apart: 24, of which 9 were waited for; matrix products, arithmetic and copies ran while one was open for 9% of the time, Pallas kernels for 9%

profile of v7, /device:TPU:1, one launch (start us, length us, event | category | flops | bytes accessed | tf_op | source)
XLA Modules:
  0.0 137.3 jit_solution(1712437095205203140)
XLA Ops:
  0.6 0.0 copy-start
  0.6 5.3 %collective-permute-start.4 = (bf16[512,512]{1,0:T(8,128)(2,1)}, bf16[512,512]{1,0:T(8,128)(2,1)S(1)}, u32[]{:S(2)}, u32[]{:S(2)}) collective-permute-start(bf16[512,512]{1,0:T(8,128)(2,1)} %refs_0_.3), channel_id=1, source_target_pairs={{0,12},{1,13},{2,14},{3,15},{4,0},{5,1},{6,2},{7,3},{8,4},{9,5},{1... | collective-permute-start | bytes 1572872 | tf_op jit(solution)/shard_map/ppermute | solution.py:41
  5.9 0.0 collective-permute-start.3
  5.9 1.3 collective-permute-start.2
  7.2 1.4 %collective-permute-start.1 = (bf16[512,512]{1,0:T(8,128)(2,1)}, bf16[512,512]{1,0:T(8,128)(2,1)S(1)}, u32[]{:S(2)}, u32[]{:S(2)}) collective-permute-start(bf16[512,512]{1,0:T(8,128)(2,1)} %refs_0_.3), channel_id=1, source_target_pairs={{0,1},{1,2},{2,3},{3,0},{4,5},{5,6},{6,7},{7,4},{8,9},{9,10},{10,1... | collective-permute-start | bytes 1572872 | tf_op jit(solution)/shard_map/ppermute | solution.py:41
  8.6 3.3 %collective-permute-start = (bf16[512,512]{1,0:T(8,128)(2,1)}, bf16[512,512]{1,0:T(8,128)(2,1)S(1)}, u32[]{:S(2)}, u32[]{:S(2)}) collective-permute-start(bf16[512,512]{1,0:T(8,128)(2,1)} %param.8), channel_id=1, source_target_pairs={{0,0},{1,16},{2,2},{3,18},{4,196},{5,84},{6,198},{7,86},{8,136},{9... | collective-permute-start | bytes 1572872 | tf_op jit(solution)/shard_map/ppermute | solution.py:41
  12.6 1.4 %fusion.3 = f32[512,64]{0,1:T(8,128)S(1)} fusion(bf16[512,512]{1,0:T(8,128)(2,1)} %refs_0_.3, bf16[512]{0:T(512)(128)(2,1)S(1)} %fusion.16, bf16[1,64,512]{2,1,0:T(8,128)(2,1)} %param.10), kind=kOutput, calls=%fused_computation.6 | convolution fusion | flops 33816576 | bytes 721920 | tf_op jit(solution)/shard_map/dot_general | solution.py:215
  14.0 1.1 fusion.12
  15.2 6.0 %collective-permute-done.1.refs_1_ = bf16[512,512]{1,0:T(8,128)(2,1)S(1)} collective-permute-done((bf16[512,512]{1,0:T(8,128)(2,1)}, bf16[512,512]{1,0:T(8,128)(2,1)S(1)}, u32[]{:S(2)}, u32[]{:S(2)}) %collective-permute-start.1) | collective-permute-done | bytes 524320 | tf_op jit(solution)/shard_map/ppermute | solution.py:41
  21.2 1.4 %collective-permute-start.5 = (f32[256,128]{0,1:T(8,128)S(1)}, f32[256,128]{0,1:T(8,128)S(1)}, u32[]{:S(2)}, u32[]{:S(2)}) collective-permute-start(f32[256,128]{0,1:T(8,128)S(1)} %constant_dynamic-slice_fusion), channel_id=1, source_target_pairs={{0,1},{1,0},{2,3},{3,2},{4,5},{5,4},{6,7},{7,6},{8,9},{9,8},{10,11... | collective-permute-start | bytes 393224 | tf_op jit(solution)/shard_map/ppermute | solution.py:41
  22.6 6.2 %collective-permute-done.3 = bf16[512,512]{1,0:T(8,128)(2,1)S(1)} collective-permute-done((bf16[512,512]{1,0:T(8,128)(2,1)}, bf16[512,512]{1,0:T(8,128)(2,1)S(1)}, u32[]{:S(2)}, u32[]{:S(2)}) %collective-permute-start.3) | collective-permute-done | bytes 524320 | tf_op jit(solution)/shard_map/ppermute | solution.py:41
  28.9 0.0 collective-permute-done.4
  29.0 0.0 copy-start.5
  29.0 0.0 collective-permute-done.5
  29.1 2.8 %collective-permute-start.8 = (bf16[1024,512]{1,0:T(8,128)(2,1)S(1)}, bf16[1024,512]{1,0:T(8,128)(2,1)S(1)}, u32[]{:S(2)}, u32[]{:S(2)}) collective-permute-start(bf16[1024,512]{1,0:T(8,128)(2,1)S(1)} %constant_dynamic-update-slice_fusion.refs_3_), channel_id=1, source_target_pairs={{0,1},{1,2},{2,3},{3,0},{4,5},{5,6},{6,7},{7,4},{8,9},{9,10},{10,1... | collective-permute-start | bytes 3145736 | tf_op jit(solution)/shard_map/ppermute | solution.py:41
  31.9 0.0 collective-permute-start.9
  31.9 4.7 %collective-permute-start.7 = (bf16[512,512]{1,0:T(8,128)(2,1)S(1)}, bf16[512,512]{1,0:T(8,128)(2,1)S(1)}, u32[]{:S(2)}, u32[]{:S(2)}) collective-permute-start(bf16[512,512]{1,0:T(8,128)(2,1)S(1)} %collective-permute-done), channel_id=1, source_target_pairs={{0,32},{1,33},{2,0},{3,1},{4,36},{5,37},{6,4},{7,5},{8,40},{9,41},... | collective-permute-start | bytes 1572872 | tf_op jit(solution)/shard_map/ppermute | solution.py:41
  36.6 0.7 collective-permute-start.6
  37.3 1.7 %collective-permute-start.10 = (f32[256,128]{0,1:T(8,128)S(1)}, f32[256,128]{0,1:T(8,128)S(1)}, u32[]{:S(2)}, u32[]{:S(2)}) collective-permute-start(f32[256,128]{0,1:T(8,128)S(1)} %dynamic-slice_add_fusion), channel_id=1, source_target_pairs={{0,4},{1,5},{2,6},{3,7},{4,0},{5,1},{6,2},{7,3},{8,12},{9,13},{10,... | collective-permute-start | bytes 393224 | tf_op jit(solution)/shard_map/ppermute | solution.py:41
  39.0 23.1 %collective-permute-done.10 = f32[256,128]{0,1:T(8,128)S(1)} collective-permute-done((f32[256,128]{0,1:T(8,128)S(1)}, f32[256,128]{0,1:T(8,128)S(1)}, u32[]{:S(2)}, u32[]{:S(2)}) %collective-permute-start.10) | collective-permute-done | bytes 131104 | tf_op jit(solution)/shard_map/ppermute | solution.py:41
  62.1 0.5 collective-permute-done.8.refs_4_
  62.7 0.1 pad_maximum_fusion
  62.8 4.3 %collective-permute-done.7 = bf16[512,512]{1,0:T(8,128)(2,1)S(1)} collective-permute-done((bf16[512,512]{1,0:T(8,128)(2,1)S(1)}, bf16[512,512]{1,0:T(8,128)(2,1)S(1)}, u32[]{:S(2)}, u32[]{:S(2)}) %collective-permute-start.7) | collective-permute-done | bytes 524320 | tf_op jit(solution)/shard_map/ppermute | solution.py:41
  67.1 0.0 collective-permute-done.6
  67.1 0.0 collective-permute-done.9.refs_5_
  67.1 1.0 copy-done.15
  68.1 4.4 %collective-permute-start.14 = (bf16[1536,512]{1,0:T(8,128)(2,1)S(1)}, bf16[1536,512]{1,0:T(8,128)(2,1)S(1)}, u32[]{:S(2)}, u32[]{:S(2)}) collective-permute-start(bf16[1536,512]{1,0:T(8,128)(2,1)S(1)} %pad_maximum_fusion), channel_id=1, source_target_pairs={{0,1},{1,2},{2,3},{3,0},{4,5},{5,6},{6,7},{7,4},{8,9},{9,10},{10,1... | collective-permute-start | bytes 4718600 | tf_op jit(solution)/shard_map/ppermute | solution.py:41
  72.6 1.0 collective-permute-start.12
  73.5 0.6 collective-permute-start.13
  74.1 0.5 collective-permute-start.11
  74.6 0.0 collective-permute-start.15
  74.6 1.9 %dynamic_update_slice.9 = bf16[3072,512]{1,0:T(8,128)(2,1)} pad(bf16[1024,512]{1,0:T(8,128)(2,1)S(1)} %constant_dynamic-update-slice_fusion.2.refs_8_.refs_10_, bf16[]{:T(256)} %constant.180.clone.1), padding=0_2048x0_0 | pad | bytes 4194306 | tf_op jit(solution)/shard_map/dynamic_update_slice | solution.py:227
  76.5 16.1 %collective-permute-done.15 = f32[256,128]{0,1:T(8,128)S(1)} collective-permute-done((f32[256,128]{0,1:T(8,128)S(1)}, f32[256,128]{0,1:T(8,128)S(1)}, u32[]{:S(2)}, u32[]{:S(2)}) %collective-permute-start.15) | collective-permute-done | bytes 131104 | tf_op jit(solution)/shard_map/ppermute | solution.py:41
  92.7 5.1 %collective-permute-done.12.refs_9_.refs_11_ = bf16[1024,512]{1,0:T(8,128)(2,1)} collective-permute-done((bf16[1024,512]{1,0:T(8,128)(2,1)S(1)}, bf16[1024,512]{1,0:T(8,128)(2,1)}, u32[]{:S(2)}, u32[]{:S(2)}) %collective-permute-start.12) | collective-permute-done | bytes 1048608 | tf_op jit(solution)/shard_map/ppermute | solution.py:41
  97.8 2.3 %constant_dynamic-update-slice_fusion.5 = bf16[3072,512]{1,0:T(8,128)(2,1)} fusion(bf16[3072,512]{1,0:T(8,128)(2,1)} %dynamic_update_slice.9, bf16[1024,512]{1,0:T(8,128)(2,1)} %collective-permute-done.12.refs_9_.refs_11_), kind=kLoop, calls=%fused_computation.32 | loop fusion | bytes 2097152 | tf_op jit(solution)/shard_map/dynamic_update_slice | solution.py:227
  100.1 0.0 collective-permute-done.13.refs_10_.refs_12_
  100.1 1.1 constant_dynamic-update-slice_fusion.4
  101.3 0.2 copy-done.13
  101.5 1.2 copy-done.14
  102.6 0.0 collective-permute-start.19
  102.6 1.9 %collective-permute-start.17 = (bf16[1024,512]{1,0:T(8,128)(2,1)}, bf16[1024,512]{1,0:T(8,128)(2,1)}, u32[]{:S(2)}, u32[]{:S(2)}) collective-permute-start(bf16[1024,512]{1,0:T(8,128)(2,1)} %collective-permute-done.12.refs_9_.refs_11_), channel_id=1, source_target_pairs={{0,64},{1,65},{2,66},{3,67},{4,68},{5,69},{6,70},{7,71},{8,72},{9,... | collective-permute-start | bytes 3145736 | tf_op jit(solution)/shard_map/ppermute | solution.py:41
  104.5 0.0 collective-permute-start.18
  104.5 2.7 %collective-permute-start.16 = (bf16[512,512]{1,0:T(8,128)(2,1)}, bf16[512,512]{1,0:T(8,128)(2,1)}, u32[]{:S(2)}, u32[]{:S(2)}) collective-permute-start(bf16[512,512]{1,0:T(8,128)(2,1)} %collective-permute-done.11.refs_7_), channel_id=1, source_target_pairs={{0,1},{1,2},{2,3},{3,0},{4,5},{5,6},{6,7},{7,4},{8,9},{9,10},{10,1... | collective-permute-start | bytes 1572872 | tf_op jit(solution)/shard_map/ppermute | solution.py:41
  107.2 0.1 stack.118
  107.3 0.1 stack.135
  107.4 0.7 select_reduce_fusion.which_ref
  108.1 0.1 collective-permute-start.20
  108.2 6.1 %shard_map.85.refs_15_ = f32[512,512]{1,0:T(8,128)} custom-call(s32[16]{0:T(128)} %select_reduce_fusion.which_ref, bf16[512,512]{1,0:T(8,128)(2,1)} %refs_0_.3, bf16[512,512]{1,0:T(8,128)(2,1)} %copy-done.7, bf16[512,512]{1,0:T(8,128)(2,1)} %copy-done.9, bf16[1024,512]{1,0:T(8,128)(2,1)} %copy-done.3, bf16[1024,512]{1,0:T(8,128)(2,1)} %copy-done.1, ...), custom_call_target="tpu_custom_call" | custom-call | flops 4294967296 | bytes 16777216 | tf_op jit(solution)/shard_map/pallas_call | solution.py:170
  114.2 2.1 %collective-permute-done.20 = f32[256,128]{0,1:T(8,128)S(1)} collective-permute-done((f32[256,128]{0,1:T(8,128)S(1)}, f32[256,128]{0,1:T(8,128)S(1)}, u32[]{:S(2)}, u32[]{:S(2)}) %collective-permute-start.20) | collective-permute-done | bytes 131104 | tf_op jit(solution)/shard_map/ppermute | solution.py:41
  116.4 2.0 %collective-permute-done.18.refs_9_ = bf16[512,512]{1,0:T(8,128)(2,1)} collective-permute-done((bf16[512,512]{1,0:T(8,128)(2,1)}, bf16[512,512]{1,0:T(8,128)(2,1)}, u32[]{:S(2)}, u32[]{:S(2)}) %collective-permute-start.18) | collective-permute-done | bytes 524320 | tf_op jit(solution)/shard_map/ppermute | solution.py:41
  118.4 2.0 %collective-permute-start.22 = (bf16[1024,512]{1,0:T(8,128)(2,1)}, bf16[1024,512]{1,0:T(8,128)(2,1)}, u32[]{:S(2)}, u32[]{:S(2)}) collective-permute-start(bf16[1024,512]{1,0:T(8,128)(2,1)} %collective-permute-done.17.refs_14_), channel_id=1, source_target_pairs={{0,16},{1,17},{2,18},{3,19},{4,20},{5,21},{6,22},{7,23},{8,24},{9,... | collective-permute-start | bytes 3145736 | tf_op jit(solution)/shard_map/ppermute | solution.py:41
  120.4 0.0 copy-start.16
  120.5 0.4 collective-permute-start.23
  120.9 1.6 %collective-permute-start.21 = (bf16[512,512]{1,0:T(8,128)(2,1)}, bf16[512,512]{1,0:T(8,128)(2,1)S(1)}, u32[]{:S(2)}, u32[]{:S(2)}) collective-permute-start(bf16[512,512]{1,0:T(8,128)(2,1)} %collective-permute-done.16.refs_8_), channel_id=1, source_target_pairs={{0,1},{1,2},{2,3},{3,0},{4,5},{5,6},{6,7},{7,4},{8,9},{9,10},{10,1... | collective-permute-start | bytes 1572872 | tf_op jit(solution)/shard_map/ppermute | solution.py:41
  122.4 0.0 copy-start.8
  122.4 1.0 copy-done.8
  123.5 1.0 copy-done.10
  124.5 6.7 %shard_map.86 = (f32[512,512]{1,0:T(8,128)S(1)}, bf16[2,512,512]{2,1,0:T(8,128)(2,1)S(1)}, bf16[512,512]{1,0:T(8,128)(2,1)S(1)}) custom-call(s32[16]{0:T(128)S(1)} %copy-done.11, bf16[512,512]{1,0:T(8,128)(2,1)S(1)} %copy-done.6, bf16[512,512]{1,0:T(8,128)(2,1)S(1)} %copy-done.8, bf16[512,512]{1,0:T(8,128)(2,1)S(1)} %copy-done.10, ...), custom_call_target="tpu_custom_call" | custom-call | flops 2147483648 | bytes 8388608 | tf_op jit(solution)/shard_map/pallas_call | solution.py:170
  131.3 0.0 collective-permute-done.23
  131.3 1.0 fusion.1
  132.3 1.1 fusion
  133.5 0.6 fusion.9.add_ref
  134.1 0.0 collective-permute-done.22.w_ref
  134.1 3.2 %shard_map.87 = bf16[512,512]{1,0:T(8,128)(2,1)} custom-call(s32[16]{0:T(128)S(1)} %copy-done.11, bf16[512,512]{1,0:T(8,128)(2,1)S(1)} %collective-permute-done.21.g_ref, bf16[1024,512]{1,0:T(8,128)(2,1)} %collective-permute-done.22.w_ref, bf16[2,512,512]{2,1,0:T(8,128)(2,1)S(1)} %get-tuple-element.35.g_aside, ...), custom_call_target="tpu_custom_call" | custom-call | flops 805306368 | bytes 3145728 | tf_op jit(solution)/shard_map/pallas_call | solution.py:192
  (46 shorter events, 0.4 us)
Async XLA Ops:
  0.6 13.4 %copy-start = (bf16[512,512]{1,0:T(8,128)(2,1)S(1)}, bf16[512,512]{1,0:T(8,128)(2,1)}, u32[]{:S(2)}) copy-start(bf16[512,512]{1,0:T(8,128)(2,1)} %param.6) | copy-start | bytes 1572868
  0.6 28.3 %collective-permute-start.4 = (bf16[512,512]{1,0:T(8,128)(2,1)}, bf16[512,512]{1,0:T(8,128)(2,1)S(1)}, u32[]{:S(2)}, u32[]{:S(2)}) collective-permute-start(bf16[512,512]{1,0:T(8,128)(2,1)} %refs_0_.3), channel_id=1, source_target_pairs={{0,12},{1,13},{2,14},{3,15},{4,0},{5,1},{6,2},{7,3},{8,4},{9,5},{1... | collective-permute-start | bytes 1572872 | tf_op jit(solution)/shard_map/ppermute | solution.py:41
  5.9 23.0 %collective-permute-start.3 = (bf16[512,512]{1,0:T(8,128)(2,1)}, bf16[512,512]{1,0:T(8,128)(2,1)S(1)}, u32[]{:S(2)}, u32[]{:S(2)}) collective-permute-start(bf16[512,512]{1,0:T(8,128)(2,1)} %refs_0_.3), channel_id=1, source_target_pairs={{0,4},{1,5},{2,6},{3,7},{4,8},{5,9},{6,10},{7,11},{8,12},{9,13},{1... | collective-permute-start | bytes 1572872 | tf_op jit(solution)/shard_map/ppermute | solution.py:41
  5.9 23.1 %collective-permute-start.2 = (bf16[512,512]{1,0:T(8,128)(2,1)}, bf16[512,512]{1,0:T(8,128)(2,1)S(1)}, u32[]{:S(2)}, u32[]{:S(2)}) collective-permute-start(bf16[512,512]{1,0:T(8,128)(2,1)} %refs_0_.3), channel_id=1, source_target_pairs={{0,3},{1,0},{2,1},{3,2},{4,7},{5,4},{6,5},{7,6},{8,11},{9,8},{10,9... | collective-permute-start | bytes 1572872 | tf_op jit(solution)/shard_map/ppermute | solution.py:41
  7.2 14.0 %collective-permute-start.1 = (bf16[512,512]{1,0:T(8,128)(2,1)}, bf16[512,512]{1,0:T(8,128)(2,1)S(1)}, u32[]{:S(2)}, u32[]{:S(2)}) collective-permute-start(bf16[512,512]{1,0:T(8,128)(2,1)} %refs_0_.3), channel_id=1, source_target_pairs={{0,1},{1,2},{2,3},{3,0},{4,5},{5,6},{6,7},{7,4},{8,9},{9,10},{10,1... | collective-permute-start | bytes 1572872 | tf_op jit(solution)/shard_map/ppermute | solution.py:41
  8.6 20.4 %collective-permute-start = (bf16[512,512]{1,0:T(8,128)(2,1)}, bf16[512,512]{1,0:T(8,128)(2,1)S(1)}, u32[]{:S(2)}, u32[]{:S(2)}) collective-permute-start(bf16[512,512]{1,0:T(8,128)(2,1)} %param.8), channel_id=1, source_target_pairs={{0,0},{1,16},{2,2},{3,18},{4,196},{5,84},{6,198},{7,86},{8,136},{9... | collective-permute-start | bytes 1572872 | tf_op jit(solution)/shard_map/ppermute | solution.py:41
  21.2 41.6 %copy-start.7 = (bf16[512,512]{1,0:T(8,128)(2,1)}, bf16[512,512]{1,0:T(8,128)(2,1)S(1)}, u32[]{:S(2)}) copy-start(bf16[512,512]{1,0:T(8,128)(2,1)S(1)} %collective-permute-done.1.refs_1_) | copy-start | bytes 1572868
  21.2 7.8 %collective-permute-start.5 = (f32[256,128]{0,1:T(8,128)S(1)}, f32[256,128]{0,1:T(8,128)S(1)}, u32[]{:S(2)}, u32[]{:S(2)}) collective-permute-start(f32[256,128]{0,1:T(8,128)S(1)} %constant_dynamic-slice_fusion), channel_id=1, source_target_pairs={{0,1},{1,0},{2,3},{3,2},{4,5},{5,4},{6,7},{7,6},{8,9},{9,8},{10,11... | collective-permute-start | bytes 393224 | tf_op jit(solution)/shard_map/ppermute | solution.py:41
  29.0 47.6 %copy-start.3 = (bf16[1024,512]{1,0:T(8,128)(2,1)}, bf16[1024,512]{1,0:T(8,128)(2,1)S(1)}, u32[]{:S(2)}) copy-start(bf16[1024,512]{1,0:T(8,128)(2,1)S(1)} %constant_dynamic-update-slice_fusion.refs_3_) | copy-start | bytes 3145732
  29.0 45.1 %copy-start.5 = (bf16[512,512]{1,0:T(8,128)(2,1)S(1)}, bf16[512,512]{1,0:T(8,128)(2,1)}, u32[]{:S(2)}) copy-start(bf16[512,512]{1,0:T(8,128)(2,1)} %refs_0_.3) | copy-start | bytes 1572868
  29.1 47.5 %copy-start.9 = (bf16[512,512]{1,0:T(8,128)(2,1)}, bf16[512,512]{1,0:T(8,128)(2,1)S(1)}, u32[]{:S(2)}) copy-start(bf16[512,512]{1,0:T(8,128)(2,1)S(1)} %collective-permute-done.2.refs_2_) | copy-start | bytes 1572868
  29.1 33.6 %collective-permute-start.8 = (bf16[1024,512]{1,0:T(8,128)(2,1)S(1)}, bf16[1024,512]{1,0:T(8,128)(2,1)S(1)}, u32[]{:S(2)}, u32[]{:S(2)}) collective-permute-start(bf16[1024,512]{1,0:T(8,128)(2,1)S(1)} %constant_dynamic-update-slice_fusion.refs_3_), channel_id=1, source_target_pairs={{0,1},{1,2},{2,3},{3,0},{4,5},{5,6},{6,7},{7,4},{8,9},{9,10},{10,1... | collective-permute-start | bytes 3145736 | tf_op jit(solution)/shard_map/ppermute | solution.py:41
  31.9 35.3 %collective-permute-start.9 = (bf16[1024,512]{1,0:T(8,128)(2,1)S(1)}, bf16[1024,512]{1,0:T(8,128)(2,1)S(1)}, u32[]{:S(2)}, u32[]{:S(2)}) collective-permute-start(bf16[1024,512]{1,0:T(8,128)(2,1)S(1)} %constant_dynamic-update-slice_fusion.refs_3_), channel_id=1, source_target_pairs={{0,3},{1,0},{2,1},{3,2},{4,7},{5,4},{6,5},{7,6},{8,11},{9,8},{10,9... | collective-permute-start | bytes 3145736 | tf_op jit(solution)/shard_map/ppermute | solution.py:41
  31.9 35.2 %collective-permute-start.7 = (bf16[512,512]{1,0:T(8,128)(2,1)S(1)}, bf16[512,512]{1,0:T(8,128)(2,1)S(1)}, u32[]{:S(2)}, u32[]{:S(2)}) collective-permute-start(bf16[512,512]{1,0:T(8,128)(2,1)S(1)} %collective-permute-done), channel_id=1, source_target_pairs={{0,32},{1,33},{2,0},{3,1},{4,36},{5,37},{6,4},{7,5},{8,40},{9,41},... | collective-permute-start | bytes 1572872 | tf_op jit(solution)/shard_map/ppermute | solution.py:41
  36.6 30.5 %collective-permute-start.6 = (bf16[512,512]{1,0:T(8,128)(2,1)S(1)}, bf16[512,512]{1,0:T(8,128)(2,1)S(1)}, u32[]{:S(2)}, u32[]{:S(2)}) collective-permute-start(bf16[512,512]{1,0:T(8,128)(2,1)S(1)} %collective-permute-done), channel_id=1, source_target_pairs={{0,0},{1,1},{2,32},{3,33},{4,4},{5,5},{6,36},{7,37},{8,8},{9,9},{1... | collective-permute-start | bytes 1572872 | tf_op jit(solution)/shard_map/ppermute | solution.py:41
  37.3 24.8 %collective-permute-start.10 = (f32[256,128]{0,1:T(8,128)S(1)}, f32[256,128]{0,1:T(8,128)S(1)}, u32[]{:S(2)}, u32[]{:S(2)}) collective-permute-start(f32[256,128]{0,1:T(8,128)S(1)} %dynamic-slice_add_fusion), channel_id=1, source_target_pairs={{0,4},{1,5},{2,6},{3,7},{4,0},{5,1},{6,2},{7,3},{8,12},{9,13},{10,... | collective-permute-start | bytes 393224 | tf_op jit(solution)/shard_map/ppermute | solution.py:41
  62.7 13.9 %copy-start.1 = (bf16[1024,512]{1,0:T(8,128)(2,1)}, bf16[1024,512]{1,0:T(8,128)(2,1)S(1)}, u32[]{:S(2)}) copy-start(bf16[1024,512]{1,0:T(8,128)(2,1)S(1)} %collective-permute-done.8.refs_4_) | copy-start | bytes 3145732
  67.1 1.0 copy-start.15
  68.1 33.3 %collective-permute-start.14 = (bf16[1536,512]{1,0:T(8,128)(2,1)S(1)}, bf16[1536,512]{1,0:T(8,128)(2,1)S(1)}, u32[]{:S(2)}, u32[]{:S(2)}) collective-permute-start(bf16[1536,512]{1,0:T(8,128)(2,1)S(1)} %pad_maximum_fusion), channel_id=1, source_target_pairs={{0,1},{1,2},{2,3},{3,0},{4,5},{5,6},{6,7},{7,4},{8,9},{9,10},{10,1... | collective-permute-start | bytes 4718600 | tf_op jit(solution)/shard_map/ppermute | solution.py:41
  72.6 27.5 %copy-start.12 = (bf16[1024,512]{1,0:T(8,128)(2,1)}, bf16[1024,512]{1,0:T(8,128)(2,1)S(1)}, u32[]{:S(2)}) copy-start(bf16[1024,512]{1,0:T(8,128)(2,1)S(1)} %constant_dynamic-update-slice_fusion.2.refs_8_.refs_10_) | copy-start | bytes 3145732
  72.6 25.2 %collective-permute-start.12 = (bf16[1024,512]{1,0:T(8,128)(2,1)S(1)}, bf16[1024,512]{1,0:T(8,128)(2,1)}, u32[]{:S(2)}, u32[]{:S(2)}) collective-permute-start(bf16[1024,512]{1,0:T(8,128)(2,1)S(1)} %constant_dynamic-update-slice_fusion.2.refs_8_.refs_10_), channel_id=1, source_target_pairs={{0,64},{1,65},{2,66},{3,67},{4,68},{5,69},{6,70},{7,71},{8,72},{9,... | collective-permute-start | bytes 3145736 | tf_op jit(solution)/shard_map/ppermute | solution.py:41
  73.5 26.6 %collective-permute-start.13 = (bf16[1024,512]{1,0:T(8,128)(2,1)S(1)}, bf16[1024,512]{1,0:T(8,128)(2,1)S(1)}, u32[]{:S(2)}, u32[]{:S(2)}) collective-permute-start(bf16[1024,512]{1,0:T(8,128)(2,1)S(1)} %constant_dynamic-update-slice_fusion.2.refs_8_.refs_10_), channel_id=1, source_target_pairs={{0,192},{1,193},{2,194},{3,195},{4,196},{5,197},{6,198},{7,199},{8... | collective-permute-start | bytes 3145736 | tf_op jit(solution)/shard_map/ppermute | solution.py:41
  74.1 27.1 %collective-permute-start.11 = (bf16[512,512]{1,0:T(8,128)(2,1)S(1)}, bf16[512,512]{1,0:T(8,128)(2,1)}, u32[]{:S(2)}, u32[]{:S(2)}) collective-permute-start(bf16[512,512]{1,0:T(8,128)(2,1)S(1)} %copy-done.5), channel_id=1, source_target_pairs={{0,8},{1,9},{2,10},{3,11},{4,12},{5,13},{6,14},{7,15},{8,0},{9,1},... | collective-permute-start | bytes 1572872 | tf_op jit(solution)/shard_map/ppermute | solution.py:41
  74.6 18.0 %collective-permute-start.15 = (f32[256,128]{0,1:T(8,128)S(1)}, f32[256,128]{0,1:T(8,128)S(1)}, u32[]{:S(2)}, u32[]{:S(2)}) collective-permute-start(f32[256,128]{0,1:T(8,128)S(1)} %add.346), channel_id=1, source_target_pairs={{0,3},{1,2},{2,1},{3,0},{4,7},{5,6},{6,5},{7,4},{8,11},{9,10},{10,... | collective-permute-start | bytes 393224 | tf_op jit(solution)/shard_map/ppermute | solution.py:41
  100.1 1.3 copy-start.13
  101.5 1.2 copy-start.14
  102.6 15.8 %collective-permute-start.19 = (bf16[3072,512]{1,0:T(8,128)(2,1)}, bf16[3072,512]{1,0:T(8,128)(2,1)}, u32[]{:S(2)}, u32[]{:S(2)}) collective-permute-start(bf16[3072,512]{1,0:T(8,128)(2,1)} %constant_dynamic-update-slice_fusion.4), channel_id=1, source_target_pairs={{0,16},{1,17},{2,18},{3,19},{4,20},{5,21},{6,22},{7,23},{8,24},{9,... | collective-permute-start | bytes 9437192 | tf_op jit(solution)/shard_map/ppermute | solution.py:41
  102.6 15.8 %collective-permute-start.17 = (bf16[1024,512]{1,0:T(8,128)(2,1)}, bf16[1024,512]{1,0:T(8,128)(2,1)}, u32[]{:S(2)}, u32[]{:S(2)}) collective-permute-start(bf16[1024,512]{1,0:T(8,128)(2,1)} %collective-permute-done.12.refs_9_.refs_11_), channel_id=1, source_target_pairs={{0,64},{1,65},{2,66},{3,67},{4,68},{5,69},{6,70},{7,71},{8,72},{9,... | collective-permute-start | bytes 3145736 | tf_op jit(solution)/shard_map/ppermute | solution.py:41
  104.5 13.9 %collective-permute-start.18 = (bf16[512,512]{1,0:T(8,128)(2,1)}, bf16[512,512]{1,0:T(8,128)(2,1)}, u32[]{:S(2)}, u32[]{:S(2)}) collective-permute-start(bf16[512,512]{1,0:T(8,128)(2,1)} %collective-permute-done.11.refs_7_), channel_id=1, source_target_pairs={{0,3},{1,0},{2,1},{3,2},{4,7},{5,4},{6,5},{7,6},{8,11},{9,8},{10,9... | collective-permute-start | bytes 1572872 | tf_op jit(solution)/shard_map/ppermute | solution.py:41
  104.5 13.9 %collective-permute-start.16 = (bf16[512,512]{1,0:T(8,128)(2,1)}, bf16[512,512]{1,0:T(8,128)(2,1)}, u32[]{:S(2)}, u32[]{:S(2)}) collective-permute-start(bf16[512,512]{1,0:T(8,128)(2,1)} %collective-permute-done.11.refs_7_), channel_id=1, source_target_pairs={{0,1},{1,2},{2,3},{3,0},{4,5},{5,6},{6,7},{7,4},{8,9},{9,10},{10,1... | collective-permute-start | bytes 1572872 | tf_op jit(solution)/shard_map/ppermute | solution.py:41
  108.1 14.3 %copy-start.2 = (bf16[1024,512]{1,0:T(8,128)(2,1)S(1)}, bf16[1024,512]{1,0:T(8,128)(2,1)}, u32[]{:S(2)}) copy-start(bf16[1024,512]{1,0:T(8,128)(2,1)} %copy-done.1) | copy-start | bytes 3145732
  108.1 14.3 %copy-start.4 = (bf16[1024,512]{1,0:T(8,128)(2,1)S(1)}, bf16[1024,512]{1,0:T(8,128)(2,1)}, u32[]{:S(2)}) copy-start(bf16[1024,512]{1,0:T(8,128)(2,1)} %copy-done.3) | copy-start | bytes 3145732
  108.1 14.3 %copy-start.6 = (bf16[512,512]{1,0:T(8,128)(2,1)S(1)}, bf16[512,512]{1,0:T(8,128)(2,1)}, u32[]{:S(2)}) copy-start(bf16[512,512]{1,0:T(8,128)(2,1)} %refs_0_.3) | copy-start | bytes 1572868
  108.1 14.3 %copy-start.11 = (s32[16]{0:T(128)S(1)}, s32[16]{0:T(128)}, u32[]{:S(2)}) copy-start(s32[16]{0:T(128)} %select_reduce_fusion.which_ref) | copy-start | bytes 196
  108.1 8.2 %collective-permute-start.20 = (f32[256,128]{0,1:T(8,128)S(1)}, f32[256,128]{0,1:T(8,128)S(1)}, u32[]{:S(2)}, u32[]{:S(2)}) collective-permute-start(f32[256,128]{0,1:T(8,128)S(1)} %add.347), channel_id=1, source_target_pairs={{0,8},{1,9},{2,10},{3,11},{4,12},{5,13},{6,14},{7,15},{8,0},{9,1},... | collective-permute-start | bytes 393224 | tf_op jit(solution)/shard_map/ppermute | solution.py:41
  118.4 15.7 %collective-permute-start.22 = (bf16[1024,512]{1,0:T(8,128)(2,1)}, bf16[1024,512]{1,0:T(8,128)(2,1)}, u32[]{:S(2)}, u32[]{:S(2)}) collective-permute-start(bf16[1024,512]{1,0:T(8,128)(2,1)} %collective-permute-done.17.refs_14_), channel_id=1, source_target_pairs={{0,16},{1,17},{2,18},{3,19},{4,20},{5,21},{6,22},{7,23},{8,24},{9,... | collective-permute-start | bytes 3145736 | tf_op jit(solution)/shard_map/ppermute | solution.py:41
  120.4 13.0 %copy-start.16 = (bf16[1,64,512]{2,1,0:T(8,128)(2,1)S(1)}, bf16[1,64,512]{2,1,0:T(8,128)(2,1)}, u32[]{:S(2)}) copy-start(bf16[1,64,512]{2,1,0:T(8,128)(2,1)} %param.9) | copy-start | bytes 196612
  120.5 10.8 %collective-permute-start.23 = (f32[256,128]{0,1:T(8,128)S(1)}, f32[256,128]{0,1:T(8,128)S(1)}, u32[]{:S(2)}, u32[]{:S(2)}) collective-permute-start(f32[256,128]{0,1:T(8,128)S(1)} %add.348), channel_id=1, source_target_pairs={{0,1},{1,0},{2,3},{3,2},{4,5},{5,4},{6,7},{7,6},{8,9},{9,8},{10,11... | collective-permute-start | bytes 393224 | tf_op jit(solution)/shard_map/ppermute | solution.py:41
  120.9 13.3 %collective-permute-start.21 = (bf16[512,512]{1,0:T(8,128)(2,1)}, bf16[512,512]{1,0:T(8,128)(2,1)S(1)}, u32[]{:S(2)}, u32[]{:S(2)}) collective-permute-start(bf16[512,512]{1,0:T(8,128)(2,1)} %collective-permute-done.16.refs_8_), channel_id=1, source_target_pairs={{0,1},{1,2},{2,3},{3,0},{4,5},{5,6},{6,7},{7,4},{8,9},{9,10},{10,1... | collective-permute-start | bytes 1572872 | tf_op jit(solution)/shard_map/ppermute | solution.py:41
  122.4 1.0 copy-start.8
  123.5 1.0 copy-start.10
